TPU v7x, 32 devices: a whole 2x2x4 slice. The times are simulated.
32 devices in a mesh: groups: 2 (over x), river: 8 (over z, y), hand: 2 (over core).
Axes of the slice: x: 2, y: 2, z: 4, core: 2. Of those that a mesh axis runs over, the one named last changes fastest.
Arguments:
- hand_rank: int32 [192, 1326], P(('groups', 'river'), 'hand'), parts along dimension 0, may hold values from -1 to 7461, as said below
- loads: int32 [16], P('groups'), parts along dimension 0, may hold values from 3 to 12, as said below
- turn_cards: int32 [8], P('groups'), parts along dimension 0, may hold values from 0 to 51, as said below
- turn_children: int32 [6, 16], replicated, may hold values from 0 to 1, as said below
- turn_parents: int32 [6, 16], replicated, may hold values from 0 to 1, as said below
- river_children: int32 [16, 64], replicated, may hold values from 0 to 1, as said below
- river_parents: int32 [16, 80], replicated, may hold values from 0 to 1, as said below
- showdown_pot: float32 [64, 64], replicated, may hold values from 0 to 0.0625
- river_fold: float32 [64, 64], replicated, may hold values from -0.75 to 0.75
- turn_fold: float32 [16, 16], replicated, may hold values from -1.5 to 1.5
- mover_turn: float32 [32, 1326], P('groups', 'hand'), parts along dimension 0, may hold values from 0 to 2
- mover_river: float32 [192, 64, 1326], P(('groups', 'river'), None, 'hand'), parts along dimension 0, may hold values from 0 to 120
- mover_turn_price: float32 [12, 1326], P('groups', 'hand'), parts along dimension 0, may hold values from -6 to 6
- mover_river_price: float32 [192, 16, 1326], P(('groups', 'river'), None, 'hand'), parts along dimension 0, may hold values from -120 to 120
- rival_turn: float32 [32, 1326], P('groups', 'hand'), parts along dimension 0, may hold values from 0 to 2
- rival_river: float32 [192, 64, 1326], P(('groups', 'river'), None, 'hand'), parts along dimension 0, may hold values from 0 to 120
- rival_turn_price: float32 [12, 1326], P('groups', 'hand'), parts along dimension 0, may hold values from -6 to 6
- rival_river_price: float32 [192, 16, 1326], P(('groups', 'river'), None, 'hand'), parts along dimension 0, may hold values from -120 to 120
Outputs:
- next_mover_turn: float32 [32, 1326], P('groups', 'hand'), parts along dimension 0
- next_mover_river: float32 [192, 64, 1326], P(('groups', 'river'), None, 'hand'), parts along dimension 0
- next_mover_turn_price: float32 [12, 1326], P('groups', 'hand'), parts along dimension 0
- next_mover_river_price: float32 [192, 16, 1326], P(('groups', 'river'), None, 'hand'), parts along dimension 0
- next_rival_turn: float32 [32, 1326], P('groups', 'hand'), parts along dimension 0
- next_rival_river: float32 [192, 64, 1326], P(('groups', 'river'), None, 'hand'), parts along dimension 0
- next_rival_turn_price: float32 [12, 1326], P('groups', 'hand'), parts along dimension 0
- next_rival_river_price: float32 [192, 16, 1326], P(('groups', 'river'), None, 'hand'), parts along dimension 0
There are 2 independent parts, one for each index of `groups`. A program takes and returns all parts, laid end to end along the dimension named above; an argument that names none is the same for every part. Nothing has to cross between parts.
Inputs may be any that keep to these rules, and one draw needn't show every extreme that they name: hand_rank is -1 exactly where a hand holds one of turn_cards or the slot's river card, and on every hand of an unused slot; the used slots of the river devices, taken in order, hold the 48 cards not in turn_cards, once each. The loads sum to 48; some river device holds 12. `turn_cards`: four different cards. `turn_children`: each turn sequence starts at exactly one decision point; each decision point starts one or more sequences, in a run of consecutive indices, the runs in order of the decision points. `turn_parents`: decision point 0 has no parent sequence; every other one has exactly one, a sequence starting at an earlier decision point. `river_children`: each river sequence starts at exactly one decision point; each decision point starts one or more sequences, in a run of consecutive indices, the runs in order of the decision points. `river_parents`: every river decision point has exactly one parent: a river sequence starting at an earlier decision point, or a turn sequence (the last 16 columns); decision point 0 has a turn sequence.
All inputs are finite; a program needn't handle non-finite values.
Results may differ from a plain program's by a relative error of at most 0.0003.
Values sent between devices are 32-bit elements; how exact they have to be, the bound alone decides.
No kernel may reach another device: no remote copies, remote signals or barrier semaphores. Data moves between devices by JAX's collectives and lax.ppermute only.
A program may use at most 192 MiB of HBM per device.

v0:
```python
import functools

import jax
import jax.numpy as jnp
import ml_dtypes
import numpy as np
from jax import lax
from jax.experimental import pallas as pl
from jax.experimental.pallas import tpu as pltpu
from jax.sharding import PartitionSpec as P

CARDS = 52
H = 1326
ITERS = 2
STEP_SCALE = 0.25
EPSILON = 1e-06
LANES = 128
TILE = 256
VMEM_BYTES = 20 * 2**20
F32 = jnp.float32
BF16 = jnp.bfloat16


def round_up(value, unit):
    return -(-value // unit) * unit


def halves(width, padded):
    pairs = np.stack(np.triu_indices(CARDS, 1)).astype(np.int32)
    deck = np.arange(CARDS)
    incidence = (pairs[0][:, None] == deck) | (pairs[1][:, None] == deck)
    parts = pairs.shape[1] // width
    cards = np.full((parts, 8, 2 * padded), -1, np.int32)
    gather = np.zeros((parts, 2 * padded, LANES), np.float32)
    spread = np.zeros((parts, LANES, 2 * padded), np.float32)
    for part in range(parts):
        spread[part, np.arange(CARDS + 1), width + np.arange(CARDS + 1)] = 1.0
        for place, half in enumerate((part, 1 - part)):
            far = slice(half * width, (half + 1) * width)
            rows = slice(place * padded, place * padded + width)
            cards[part, :2, rows] = pairs[:, far]
            gather[part, rows, :CARDS] = incidence[far]
            gather[part, rows, CARDS] = 1.0
            spread[part, :CARDS, rows] = -incidence[far].T.astype(np.float32)
            spread[part, CARDS, rows] = 1.0
    near = np.zeros((parts, LANES, padded), np.float32)
    first = width - (padded - LANES)
    near[:, first:first + CARDS + 1, :width] = spread[:, :CARDS + 1, :width]
    exact = ml_dtypes.bfloat16
    return (cards, gather.astype(exact), spread.astype(exact), near.astype(exact))


def split_two(value):
    high = value.astype(BF16)
    return high, (value - high.astype(F32)).astype(BF16)


def exact_right(value, matrix):
    rows = value.shape[0]
    first = value.astype(BF16)
    rest = value - first.astype(F32)
    second = rest.astype(BF16)
    third = (rest - second.astype(F32)).astype(BF16)
    total = jnp.dot(jnp.concatenate([first, second, third], axis=0), matrix, preferred_element_type=F32)
    return total[:rows] + total[rows:2 * rows] + total[2 * rows:]


def exact_left(matrix, value):
    first = value.astype(BF16)
    rest = value - first.astype(F32)
    second = rest.astype(BF16)
    third = (rest - second.astype(F32)).astype(BF16)
    matrix = matrix.astype(BF16)
    return jnp.dot(jnp.concatenate([matrix] * 3, axis=1), jnp.concatenate([first, second, third], axis=0),
                   preferred_element_type=F32)


def pair_dot(left, right):
    rows = left.shape[0]
    left_high, left_low = split_two(left)
    right_high, right_low = split_two(right)
    total = jnp.dot(
        jnp.concatenate([jnp.concatenate([left_high] * 2, axis=1), jnp.concatenate([left_low] * 2, axis=1)], axis=0),
        jnp.concatenate([right_high, right_low], axis=0), preferred_element_type=F32)
    return total[:rows] + total[rows:]


def alive_rows(card_rows, turn_cards):
    one, two = card_rows[0:1], card_rows[1:2]
    held = one < 0
    for place in range(4):
        card = turn_cards[place]
        held = held | (one == card) | (two == card)
    return jnp.where(held, 0.0, 1.0).astype(F32)


def row_sums(value):
    return jnp.sum(value, axis=0, keepdims=True)


def steps_from(own_norms, far_norms, count):
    totals = jnp.sum(own_norms + far_norms, axis=1, keepdims=True)
    weight = jnp.sqrt((totals[1:2] / count + EPSILON) / (totals[0:1] / count + EPSILON))
    return STEP_SCALE / weight, STEP_SCALE * weight


def river_steps(children_ref, parents_ref):
    sequences = children_ref.shape[1]
    step = (children_ref[...] - parents_ref[:, :sequences]).astype(F32)
    return step, parents_ref[:, sequences:].astype(F32)


def river_link(parents_ref, sequences):
    return parents_ref[:, sequences:].astype(F32)


def stats_kernel(slots, group, river_axis, loads_ref, cards_now_ref, card_ref, rank_ref, x_ref, v_ref, y_ref, u_ref,
                 xt_ref, vt_ref, yt_ref, ut_ref, children_ref, parents_ref,
                 sums_ref, pack_ref, live_scratch, plan_scratch):
    at = pl.program_id(0)
    padded = live_scratch.shape[2]
    prices = v_ref.shape[1]
    nx, ny = 3 * prices, 3 * prices + 1
    river_here = lax.axis_index(river_axis)

    @pl.when(at == 0)
    def _():
        turn = alive_rows(card_ref[0, :, :padded], cards_now_ref)
        slot = lax.broadcasted_iota(jnp.int32, (slots, padded), 0)
        rank = rank_ref[...]
        live = jnp.where((rank >= 0) & (slot < loads_ref[river_here]) & (turn > 0), 1.0, 0.0)
        for board in range(slots):
            live_scratch[board] = live[board:board + 1]
        sums_ref[...] = jnp.zeros_like(sums_ref)
        plan_scratch[...] = jnp.zeros_like(plan_scratch)
        pack_ref[...] = jnp.zeros_like(pack_ref)
        first = jnp.where(river_here == 0, 1.0, 0.0)
        base = 0
        for rows, row in ((xt_ref, nx), (yt_ref, ny), (vt_ref, nx), (ut_ref, ny)):
            value = jnp.where(turn > 0, rows[...], 0.0)
            pack_ref[base:base + value.shape[0]] = value
            base += round_up(value.shape[0], 8)
            sums_ref[row:row + 1] += first * row_sums(value * value)

    mover = jnp.zeros((1, padded), F32)
    rival = jnp.zeros((1, padded), F32)
    for inner in range(group):
        live = live_scratch[at * group + inner] > 0
        x = jnp.where(live, x_ref[inner], 0.0)
        v = jnp.where(live, v_ref[inner], 0.0)
        y = jnp.where(live, y_ref[inner], 0.0)
        u = jnp.where(live, u_ref[inner], 0.0)
        mover = mover + row_sums(x * x) + row_sums(v * v)
        rival = rival + row_sums(y * y) + row_sums(u * u)
        sums_ref[0:prices] += u
        sums_ref[prices:2 * prices] += v
        plan_scratch[...] += y
    sums_ref[nx:nx + 1] += mover
    sums_ref[ny:ny + 1] += rival

    @pl.when(at == pl.num_programs(0) - 1)
    def _():
        step, _ = river_steps(children_ref, parents_ref)
        sums_ref[2 * prices:3 * prices] = exact_left(step, plan_scratch[...])


def prepare_kernel(slots, group, river_axis, loads_ref, cards_now_ref, card_ref, gather_ref, spread_ref, own_ref, far_ref,
                   near_table_ref, pot_ref, fold_ref, children_ref, parents_ref,
                   live_ref, row_ref, col_ref, compat_ref, near_ref, main_ref, folds_ref, back_ref):
    padded = row_ref.shape[2]
    rank = jnp.concatenate([own_ref[...], far_ref[...]], axis=1)
    turn = alive_rows(card_ref[0], cards_now_ref)
    slot = lax.broadcasted_iota(jnp.int32, rank.shape, 0)
    live = jnp.where((rank >= 0) & (slot < loads_ref[lax.axis_index(river_axis)]) & (turn > 0), 1.0, 0.0)
    safe = jnp.where(live > 0, rank, 0)
    code = (128 + (safe & 127)).astype(F32)
    high = safe >> 7
    for bit in range(6):
        code = code * jnp.where((high >> bit) & 1 == 1, float(2.0 ** (1 << bit)), 1.0)
    lane = lax.broadcasted_iota(jnp.int32, rank.shape, 1)
    width = H // 2
    own_code = jnp.where(lane[:, :padded] < width, code[:, :padded], 0.0)
    for board in range(slots):
        live_ref[board] = live[board:board + 1]
        row_ref[board] = own_code[board:board + 1].astype(BF16)
    depth = round_up(slots, 8)
    if depth > slots:
        code = jnp.concatenate([code, jnp.zeros((depth - slots, code.shape[1]), F32)], axis=0)
    turned = code.T
    for place in range(slots // group):
        col_ref[place] = turned[:, place * group:(place + 1) * group]
    free = jnp.dot(gather_ref[0], spread_ref[0][:, :padded], preferred_element_type=F32)
    compat_ref[...] = jnp.maximum(free, 0.0).astype(BF16)
    near_ref[...] = near_table_ref[0]
    for place in range(2):
        set_operators(place == 1, pot_ref, fold_ref, children_ref, parents_ref, main_ref.at[place], folds_ref.at[place],
                      back_ref.at[place])


def set_operators(transposed, pot_ref, fold_ref, children_ref, parents_ref, main_scratch, fold_scratch, back_scratch):
    pot = pot_ref[...] / H
    fold = fold_ref[...] / H
    if transposed:
        pot, fold = -pot.T, fold.T
    step, _ = river_steps(children_ref, parents_ref)
    sequences = pot.shape[0]
    infosets = step.shape[0]
    pot_high, pot_low = split_two(pot)
    fold_high, fold_low = split_two(fold)
    main_scratch[:sequences] = jnp.concatenate([pot_high, pot_high, fold_high, fold_high], axis=1)
    main_scratch[sequences:2 * sequences] = jnp.concatenate([pot_low, pot_low, fold_low, fold_low], axis=1)
    exact = step.astype(BF16)
    main_scratch[2 * sequences:2 * sequences + infosets] = jnp.concatenate(
        [jnp.zeros((infosets, 2 * sequences), BF16), exact, exact], axis=1)
    fold_scratch[:sequences] = jnp.concatenate([fold_high, fold_high], axis=1)
    fold_scratch[sequences:] = jnp.concatenate([fold_low, fold_low], axis=1)
    turned = step.T
    if transposed:
        turned = -turned
    turned = turned.astype(BF16)
    back_scratch[...] = jnp.concatenate([turned, turned], axis=1)


def payoffs(own_plans, far_plans, prices, columns, strengths, compat_ref, near_ref, main, folds, back_step):
    sequences, padded = own_plans[0].shape
    tiles = padded // TILE
    width = H // 2
    depths = [min(TILE, round_up(width - at, 16)) for at in range(0, width, TILE)]
    boards = range(len(own_plans))
    owns = [split_two(plan) for plan in own_plans]
    fars = [split_two(plan) for plan in far_plans]
    price_parts = [split_two(price) for price in prices]
    mixes = []
    for inner in boards:
        left = (jnp.concatenate(owns[inner], axis=0), jnp.concatenate(fars[inner], axis=0))
        row = strengths[inner]
        sums = [None] * tiles
        for place in range(2 * tiles):
            depth = depths[place % tiles]
            rows = slice(place * TILE, place * TILE + depth)
            column = jnp.broadcast_to(columns(rows, inner), (depth, LANES)).astype(BF16)
            column = jnp.concatenate([column, column], axis=1)
            piece = left[place // tiles][:, (place % tiles) * TILE:(place % tiles) * TILE + depth]
            for across in range(tiles):
                lanes = slice(across * TILE, (across + 1) * TILE)
                bound = compat_ref[rows, lanes]
                signs = jnp.minimum(jnp.maximum(column - row[:, lanes], -bound), bound)
                part = jnp.dot(piece, signs, preferred_element_type=F32)
                sums[across] = part if sums[across] is None else sums[across] + part
        mixes.append(split_two(jnp.concatenate([item[:sequences] + item[sequences:] for item in sums], axis=1)))
    cards = []
    for inner in boards:
        tail = jnp.concatenate([item[:, padded - LANES:] for item in mixes[inner]], axis=0)
        folded = jnp.dot(folds, tail, preferred_element_type=F32)
        cards.extend(split_two(folded[:sequences] + folded[sequences:]))
    backs = [jnp.dot(back_step, jnp.concatenate(price_parts[inner], axis=0), preferred_element_type=F32) for inner in boards]
    products = [jnp.dot(main, jnp.concatenate(mixes[inner] + owns[inner], axis=0), preferred_element_type=F32)
                for inner in boards]
    nearby = jnp.dot(jnp.concatenate(cards, axis=0), near_ref[...], preferred_element_type=F32)
    done = []
    for inner in boards:
        base = 2 * inner * sequences
        close = nearby[base:base + sequences] + nearby[base + sequences:base + 2 * sequences]
        product = products[inner]
        done.append((product[:sequences] + product[sequences:2 * sequences] + backs[inner] + close, product[2 * sequences:]))
    return done


def pick(ref, base, at, inner, group):
    return ref[inner] if base is None else ref[base + at * group + inner]


def group_payoffs(group, start, side, at, plans, fars, prices, live_ref, row_ref, col_ref, compat_ref, near_ref,
                  main_ref, folds_ref, back_ref):
    strengths = [row_ref[start + at * group + inner] for inner in range(group)]

    def columns(rows, inner):
        return col_ref[start // group + at, rows, inner:inner + 1]

    return payoffs(plans, fars, prices, columns, strengths, compat_ref, near_ref, main_ref[side], folds_ref[side],
                   back_ref[side])


def mover_gradient_kernel(group, start, bases, turn_row, y_ref, far_ref, u_ref, live_ref, row_ref, col_ref, compat_ref,
                          near_ref, main_ref, folds_ref, back_ref, pack_ref, parents_ref, grad_ref, flow_ref):
    _, sequences, padded = grad_ref.shape
    link = river_link(parents_ref, sequences)
    turn_flow = exact_left(link, pack_ref[turn_row:turn_row + link.shape[1], :padded])
    own_plans, far_plans, prices, lives = [], [], [], []
    for inner in range(group):
        live = live_ref[start + inner]
        near_live = live[:, :padded]
        lives.append(near_live)
        own_plans.append(jnp.where(near_live > 0, pick(y_ref, bases[0], 0, inner, group), 0.0))
        far_plans.append(jnp.where(live[:, padded:] > 0, pick(far_ref, bases[1], 0, inner, group), 0.0))
        prices.append(jnp.where(near_live > 0, pick(u_ref, bases[2], 0, inner, group), 0.0))
    done = group_payoffs(group, start, 0, 0, own_plans, far_plans, prices, live_ref, row_ref, col_ref, compat_ref, near_ref,
                         main_ref, folds_ref, back_ref)
    for inner, (gradient, flow) in enumerate(done):
        grad_ref[inner] = gradient
        flow_ref[inner] = lives[inner] * (flow - turn_flow)


def mover_step_kernel(group, start, bases, count, norm_row, parts, last, own_norm_ref, far_norm_ref, x_ref, v_ref, live_ref,
                      *rest):
    grads, flows = rest[:parts], rest[parts:2 * parts]
    if last:
        new_x_ref, new_v_ref, bar_ref = rest[-3:]
    else:
        new_x_ref, new_v_ref, bar_ref, total_ref = rest[-4:]
        total_ref[...] = rest[2 * parts][...] if start else jnp.zeros_like(total_ref)
    padded = bar_ref.shape[2]
    primal, _ = steps_from(own_norm_ref[norm_row:norm_row + 8], far_norm_ref[norm_row:norm_row + 8], count)
    for board in range(parts * group):
        live = live_ref[start + board][:, :padded]
        x = jnp.where(live > 0, pick(x_ref, bases[0], 0, board, group), 0.0)
        v = jnp.where(live > 0, pick(v_ref, bases[1], 0, board, group), 0.0)
        new_x = live * jnp.maximum(x - primal * grads[board // group][board % group], 0.0)
        new_v = v + primal * flows[board // group][board % group]
        new_x_ref[board] = new_x
        new_v_ref[board] = new_v
        bar_ref[board] = 2.0 * new_x - x
        if not last:
            total_ref[0:1] += row_sums(new_x * new_x) + row_sums(new_v * new_v)


def rival_step_kernel(group, start, bases, count, norm_row, parts, last, own_norm_ref, far_norm_ref, bar_ref, far_ref, y_ref,
                      u_ref, new_v_ref, live_ref, row_ref, col_ref, compat_ref, near_ref, main_ref, folds_ref, back_ref,
                      bart_ref, children_ref, parents_ref, *rest):
    flows = rest[:parts]
    rest = rest[parts:]
    at = pl.program_id(0)
    if last:
        new_y_ref, new_u_ref, link_scratch, flow_scratch, step_scratch = rest[-5:]
    else:
        new_y_ref, new_u_ref, total_ref, link_scratch, flow_scratch, step_scratch, plan_scratch = rest[-7:]
    padded = live_ref.shape[2] // 2
    infosets = u_ref.shape[1]
    nx, ny = 2 * infosets, 2 * infosets + 1

    @pl.when(at == 0)
    def _():
        primal, dual = steps_from(own_norm_ref[norm_row:norm_row + 8], far_norm_ref[norm_row:norm_row + 8], count)
        step_scratch[0:1, :] = jnp.broadcast_to(primal, (1, LANES))
        step_scratch[1:2, :] = jnp.broadcast_to(dual, (1, LANES))
        link_scratch[...] = exact_left(river_link(parents_ref, bar_ref.shape[1]), bart_ref[:, :padded])
        if not last:
            plan_scratch[...] = jnp.zeros_like(plan_scratch)
            if start:
                total_ref[...] = rest[0][...]
            else:
                total_ref[...] = jnp.zeros_like(total_ref)
                total_ref[nx:ny + 1] = rest[0][0:2] + rest[1][0:2]

    for part in range(parts):
        @pl.when(at == part)
        def _():
            flow_scratch[...] = flows[part][...]

    primal = step_scratch[0:1, 0:1]
    dual = step_scratch[1:2, 0:1]
    own_plans, far_plans, prices = [], [], []
    for inner in range(group):
        own_plans.append(pick(bar_ref, bases[0], at, inner, group))
        far_plans.append(pick(far_ref, bases[1], at, inner, group))
        prices.append(pick(new_v_ref, bases[4], at, inner, group) + primal * flow_scratch[inner])
    done = group_payoffs(group, start, 1, at, own_plans, far_plans, prices, live_ref, row_ref, col_ref, compat_ref, near_ref,
                         main_ref, folds_ref, back_ref)
    for inner, (gradient, flow) in enumerate(done):
        live = live_ref[start + at * group + inner][:, :padded]
        y = jnp.where(live > 0, pick(y_ref, bases[2], at, inner, group), 0.0)
        u = jnp.where(live > 0, pick(u_ref, bases[3], at, inner, group), 0.0)
        flow = live * flow
        new_y = live * jnp.maximum(y + dual * gradient, 0.0)
        new_u = u + dual * (flow - live * link_scratch[...])
        place = inner if last else at * group + inner
        new_y_ref[place] = new_y
        new_u_ref[place] = new_u
        if not last:
            plan_scratch[...] += new_y
            total_ref[0:infosets] += flow
            total_ref[ny:ny + 1] += row_sums(new_y * new_y) + row_sums(new_u * new_u)

    if not last:
        @pl.when(at == pl.num_programs(0) - 1)
        def _():
            step, _ = river_steps(children_ref, parents_ref)
            total_ref[infosets:2 * infosets] += exact_left(step, plan_scratch[...])


def turn_step_kernel(count, first, names, hand_ref, cards_now_ref, card_ref, gather_ref, spread_ref, *rest):
    if first:
        own_ref, far_ref, sums_ref, sums_far_ref = rest[:4]
        rest = rest[4:]
    else:
        pack_ref, kept_ref, old_bar_ref, old_steps_ref, sums_ref, sums_far_ref = rest[:6]
        rest = rest[6:]
    turn_fold_ref, turn_children_ref, turn_parents_ref, children_ref, parents_ref = rest[:5]
    rest = rest[5:]
    turn = alive_rows(card_ref[0], cards_now_ref)
    _, link = river_steps(children_ref, parents_ref)
    link_turned = link.T
    parents = turn_parents_ref[...].astype(F32)
    turn_step = turn_children_ref[...].astype(F32) - parents
    turn_root = 1.0 - jnp.sum(parents, axis=1, keepdims=True)
    step_turned = turn_step.T
    fold = turn_fold_ref[...]
    meetings = (CARDS - 6) * turn
    sequences = fold.shape[0]
    points = turn_step.shape[0]
    slab = round_up(points, 8)
    starts = (0, 2 * sequences, sequences, 2 * sequences + slab)
    infosets = link.shape[0]
    norm_row = (3 if first else 2) * infosets
    primal, dual = steps_from(sums_ref[norm_row:norm_row + 8], sums_far_ref[norm_row:norm_row + 8], count)
    sums = jnp.concatenate([sums_ref[:norm_row], sums_far_ref[:norm_row]], axis=1)
    if first:
        pack = jnp.concatenate([own_ref[...], far_ref[...]], axis=1)
        price_sum = sums[:infosets]
        kept = sums[infosets:2 * infosets]
        plan_sum = sums[2 * infosets:]
    else:
        pack = pack_ref[...]
        old_dual = old_steps_ref[1:2, 0:1]
        price_sum = kept_ref[:infosets] + old_dual * (
            sums[:infosets] - meetings * exact_left(link, old_bar_ref[...]))
        kept = kept_ref[infosets:]
        plan_sum = sums[infosets:]
    x = pack[starts[0]:starts[0] + sequences]
    v = pack[starts[1]:starts[1] + points]
    y = pack[starts[2]:starts[2] + sequences]
    u = pack[starts[3]:starts[3] + points]

    def mix(plan):
        return turn * (exact_right(exact_right(plan, gather_ref[0]), spread_ref[0]) + plan)

    grad = pair_dot(fold, mix(y)) / H + turn * (exact_left(step_turned, u) - exact_left(link_turned, price_sum))
    new_x = turn * jnp.maximum(x - primal * grad, 0.0)
    new_v = v + primal * (turn * (exact_left(turn_step, y) - turn_root))
    bar = 2.0 * new_x - x
    price_bar = 2.0 * new_v - v
    drift = primal * (plan_sum - meetings * exact_left(link, y))
    rise = pair_dot(fold.T, mix(bar)) / H - turn * (
        exact_left(step_turned, price_bar) - exact_left(link_turned, kept + 2.0 * drift))
    new_y = turn * jnp.maximum(y + dual * rise, 0.0)
    new_u = u + dual * (turn * (exact_left(turn_step, bar) - turn_root))
    if first:
        out_pack_ref, out_kept_ref, bar_ref, out_norms_ref, steps_ref = rest
        steps_ref[0:1] = jnp.broadcast_to(primal, (1, LANES))
        steps_ref[1:2] = jnp.broadcast_to(dual, (1, LANES))
        out_pack_ref[...] = jnp.zeros_like(out_pack_ref)
        for start, value in zip(starts, (new_x, new_v, new_y, new_u)):
            out_pack_ref[start:start + value.shape[0]] = value
        out_kept_ref[:infosets] = price_sum
        out_kept_ref[infosets:] = kept + drift
        bar_ref[...] = bar
        river_name, hand_name = names
        flag = jnp.where((lax.axis_index(river_name) == 0) & (hand_ref[0] == 0), 1.0, 0.0)
        out_norms_ref[...] = jnp.zeros_like(out_norms_ref)
        mover = row_sums(new_x * new_x) + row_sums(new_v * new_v)
        rival = row_sums(new_y * new_y) + row_sums(new_u * new_u)
        half = mover.shape[1] // 2
        out_norms_ref[0:1] = flag * (mover[:, :half] + mover[:, half:])
        out_norms_ref[1:2] = flag * (rival[:, :half] + rival[:, half:])
    else:
        bar_ref = rest[0]
        bar_ref[...] = bar
        for out_ref, value in zip(rest[1:], (new_x, new_v, new_y, new_u)):
            out_ref[...] = value[:, :out_ref.shape[1]]


def whole(shape):
    return pl.BlockSpec(shape, lambda *at: (0,) * len(shape))


def smem():
    return pl.BlockSpec(memory_space=pltpu.SMEM)


def local(hand_rank, loads, turn_cards, turn_children, turn_parents, river_children, river_parents, showdown_pot, river_fold,
          turn_fold, mover_turn, mover_river, mover_turn_price, mover_river_price, rival_turn, rival_river,
          rival_turn_price, rival_river_price):
    slots, sequences, width = mover_river.shape
    infosets = mover_river_price.shape[1]
    turn_sequences = mover_turn.shape[0]
    points = mover_turn_price.shape[0]
    river_count = lax.axis_size("river")
    padded = round_up(width + CARDS + 1, TILE)
    both = 2 * padded
    count = float((turn_sequences + points) * H + river_count * slots * (sequences + infosets) * H)
    group = next(size for size in (3, 2, 1) if slots % size == 0)
    chunks = slots // group
    parts = 2 if chunks % 2 == 0 else 1
    span = parts * group
    cards, gather, spread, near = (jnp.asarray(table) for table in halves(width, padded))
    hand = lax.axis_index("hand").astype(jnp.int32).reshape(1)
    pack_rows = 2 * (turn_sequences + round_up(points, 8))
    stat_rows = 3 * infosets + 8
    total_rows = 2 * infosets + 8

    def shape(*dims, dtype=F32):
        return jax.ShapeDtypeStruct(dims, dtype)

    def swap(value):
        return lax.ppermute(value, "hand", [(0, 1), (1, 0)])

    def hop_total(value, hop, gate):
        came = lax.ppermute(value, "river", [(at, at ^ hop) for at in range(river_count)])
        if gate is not None:
            came, _ = lax.optimization_barrier((came, gate))
        return value + came

    def reduced(value, gates):
        gates = list(gates)
        if river_count & (river_count - 1):
            value = lax.psum(value, "river")
        else:
            hop = 1
            while hop < river_count:
                value = hop_total(value, hop, gates.pop(0) if gates else None)
                hop *= 2
        far = swap(value)
        if gates:
            far, _ = lax.optimization_barrier((far, gates[0]))
        return value, far

    def boards(rows, size=group, start=0):
        return pl.BlockSpec((size, rows, padded), lambda at, *_: (at + start, 0, 0))

    vmem = pl.BlockSpec(memory_space=pltpu.VMEM)

    def operand(item, first, size):
        if isinstance(item, list):
            length = slots // len(item)
            return item[first // length], vmem, first % length
        return item, boards(item.shape[1], size, first // size), None

    def call(kernel, name, scalars, steps, in_specs, out_specs, out_shape, scratch, args, micros, aliases=None, vmem=VMEM_BYTES):
        estimate = pl.CostEstimate(flops=int(micros * 1e9), bytes_accessed=0, transcendentals=0)
        return pl.pallas_call(
            kernel,
            grid_spec=pltpu.PrefetchScalarGridSpec(
                num_scalar_prefetch=scalars, grid=steps, in_specs=in_specs, out_specs=out_specs, scratch_shapes=scratch),
            out_shape=out_shape, compiler_params=pltpu.CompilerParams(vmem_limit_bytes=vmem),
            cost_estimate=estimate, input_output_aliases=aliases or {}, name=name,
        )(*args)

    card_block = pl.BlockSpec((1, 8, both), lambda at, ref: (ref[0], 0, 0))
    tree_blocks = [whole(river_children.shape), whole(river_parents.shape)]
    half_block = lambda rows, at_row=0: pl.BlockSpec((rows, padded), lambda at, *_: (at_row, 0))
    operator_sizes = ((2 * sequences + infosets, 4 * sequences), (2 * sequences, 2 * sequences), (sequences, 2 * infosets))
    link_scratch = pltpu.VMEM((infosets, padded), F32)
    flow_scratch = pltpu.VMEM((group, infosets, padded), F32)
    step_scratch = pltpu.VMEM((8, LANES), F32)
    plan_scratch = pltpu.VMEM((sequences, padded), F32)
    any_block = pl.BlockSpec(memory_space=pl.ANY)

    rank_far = swap(hand_rank)
    rival_far = swap(rival_river)

    def stats_kernel_here(hand_ref, *refs):
        stats_kernel(slots, group, "river", *refs)

    def prepare_kernel_here(hand_ref, *refs):
        prepare_kernel(slots, group, "river", *refs)

    sums, pack = call(
        stats_kernel_here, "stats", 1, (slots // group,),
        [smem(), smem(), card_block, half_block(slots), boards(sequences), boards(infosets),
         boards(sequences), boards(infosets), half_block(turn_sequences), half_block(points),
         half_block(turn_sequences), half_block(points)] + tree_blocks,
        [whole((stat_rows, padded)), whole((pack_rows, padded))],
        [shape(stat_rows, padded), shape(pack_rows, padded)],
        [pltpu.VMEM((slots, 1, padded), F32), plan_scratch],
        (hand, loads, turn_cards, cards, hand_rank, mover_river, mover_river_price, rival_river, rival_river_price,
         mover_turn, mover_turn_price, rival_turn, rival_turn_price, river_children, river_parents), 5,
        vmem=56 * 2**20)
    gather_block = pl.BlockSpec((1, both, LANES), lambda at, ref: (ref[0], 0, 0))
    spread_block = pl.BlockSpec((1, LANES, both), lambda at, ref: (ref[0], 0, 0))
    prepared = [shape(slots, 1, both), shape(slots, 1, padded, dtype=BF16), shape(slots // group, both, group),
                shape(both, padded, dtype=BF16), shape(LANES, padded, dtype=BF16)] + [shape(2, *size, dtype=BF16) for size in operator_sizes]
    near_block = pl.BlockSpec((1, LANES, padded), lambda at, ref: (ref[0], 0, 0))
    tables = call(
        prepare_kernel_here, "prepare", 1, (1,),
        [smem(), smem(), card_block, gather_block, spread_block, half_block(slots), half_block(slots), near_block,
         whole(showdown_pot.shape), whole(river_fold.shape)] + tree_blocks,
        [vmem] * len(prepared), prepared, [],
        (hand, loads, turn_cards, cards, gather, spread, hand_rank, rank_far, near, showdown_pot, river_fold,
         river_children, river_parents), 2)
    live = tables[0]

    def gradients(y, y_far, u, pack):
        out = []
        for first in range(0, slots, group):
            arrays, specs, bases = zip(*(operand(item, first, group) for item in (y, y_far, u)))
            args = (*arrays, *tables, pack, river_parents)
            out.append(call(
                functools.partial(mover_gradient_kernel, group, first, bases, turn_sequences), "mover_gradient", 0, (1,),
                [*specs] + [vmem] * (len(args) - 3), [vmem] * 2,
                [shape(group, sequences, padded), shape(group, infosets, padded)], [], args, group))
        return [item[0] for item in out], [item[1] for item in out]

    def mover_steps(last, norms, norm_row, x, v, grad, flow):
        outs = []
        for first in range(0, slots, span):
            arrays, specs, bases = zip(*(operand(item, first, span) for item in (x, v)))
            here = slice(first // group, first // group + parts)
            args = (*norms, *arrays, live, *grad[here], *flow[here])
            in_specs = [vmem] * 2 + [*specs] + [vmem] * (1 + 2 * parts)
            aliases = {}
            if last:
                out_specs = [boards(sequences, span, first // span), boards(infosets, span, first // span), vmem]
                out_shape = [shape(slots, sequences, width), shape(slots, infosets, width), shape(span, sequences, padded)]
                if first:
                    aliases = {len(args): 0, len(args) + 1: 1}
                    in_specs += [any_block] * 2
                    args += tuple(outs[-1][:2])
            else:
                out_specs = [vmem] * 4
                out_shape = [shape(span, sequences, padded), shape(span, infosets, padded),
                             shape(span, sequences, padded), shape(8, padded)]
                if first:
                    in_specs += [vmem]
                    args += (outs[-1][3],)
            outs.append(call(functools.partial(mover_step_kernel, group, first, bases, count, norm_row, parts, last),
                             "mover_step", 0, (1,), in_specs, out_specs, out_shape, [], args, parts, aliases))
        if last:
            return outs[-1][0], outs[-1][1], [item[2] for item in outs]
        return [item[0] for item in outs], [item[1] for item in outs], [item[2] for item in outs], outs[-1][3]

    def rival_steps(last, norms, norm_row, bar, bar_far, y, u, new_v, flow, bar_turn, parts_before):
        outs = []
        for first in range(0, slots, span):
            arrays, specs, bases = zip(*(operand(item, first, group) for item in (bar, bar_far, y, u, new_v)))
            here = slice(first // group, first // group + parts)
            args = (*norms, *arrays, *tables, bar_turn, river_children, river_parents, *flow[here])
            in_specs = [vmem] * 2 + [*specs] + [vmem] * (len(args) - 7)
            aliases = {}
            scratch = [link_scratch, flow_scratch, step_scratch]
            if last:
                out_specs = [boards(sequences, group, first // group), boards(infosets, group, first // group)]
                out_shape = [shape(slots, sequences, width), shape(slots, infosets, width)]
                if first:
                    aliases = {len(args): 0, len(args) + 1: 1}
                    in_specs += [any_block] * 2
                    args += tuple(outs[-1][:2])
            else:
                out_specs = [vmem] * 3
                out_shape = [shape(span, sequences, padded), shape(span, infosets, padded), shape(total_rows, padded)]
                scratch = scratch + [plan_scratch]
                before = (outs[-1][2],) if first else tuple(parts_before)
                in_specs += [vmem] * len(before)
                args += before
            outs.append(call(functools.partial(rival_step_kernel, group, first, bases, count, norm_row, parts, last),
                             "rival_step", 0, (parts,), in_specs, out_specs, out_shape, scratch, args, span, aliases))
        if last:
            return outs[-1]
        return [item[0] for item in outs], [item[1] for item in outs], outs[-1][2]

    turn_blocks = [smem(), card_block, gather_block, spread_block]
    turn_tables = (turn_cards, cards, gather, spread)
    turn_matrices = (turn_fold, turn_children, turn_parents, river_children, river_parents)

    def turn_call(first, data):
        if first:
            out_shape = [shape(pack_rows, both), shape(2 * infosets, both), shape(turn_sequences, both), shape(8, padded),
                         shape(8, LANES)]
        else:
            out_shape = [shape(turn_sequences, both), shape(turn_sequences, width), shape(points, width),
                         shape(turn_sequences, width), shape(points, width)]
        return call(
            functools.partial(turn_step_kernel, count, first, ("river", "hand")), "turn_step", 1, (1,),
            turn_blocks + [vmem] * len(data) + [whole(item.shape) for item in turn_matrices],
            [vmem] * 5 if first else [vmem] + [whole(item.shape) for item in out_shape[1:]],
            out_shape, [], (hand, *turn_tables, *data, *turn_matrices), 3)

    pack_far = swap(pack)
    grad, flow = gradients(rival_river, rival_far, rival_river_price, pack)
    norms = reduced(sums, [live] + flow[:3])
    x, v, bar, part = mover_steps(False, norms, 3 * infosets, mover_river, mover_river_price, grad, flow)
    bar_far = [swap(item) for item in bar]
    pack, kept, bar_turn, turn_norms, turn_steps = turn_call(True, (pack, pack_far, *norms))
    y, u, total = rival_steps(False, norms, 3 * infosets, bar, bar_far, rival_river, rival_river_price, v, flow, bar_turn,
                              (part, turn_norms))
    y_far = [swap(item) for item in y]
    grad, flow = gradients(y, y_far, u, pack)
    norms = reduced(total, flow)
    next_x, next_v, bar = mover_steps(True, norms, 2 * infosets, x, v, grad, flow)
    bar_far = [swap(item) for item in bar]
    bar_turn, next_xt, next_vt, next_yt, next_ut = turn_call(False, (pack, kept, bar_turn, turn_steps, *norms))
    next_y, next_u = rival_steps(True, norms, 2 * infosets, bar, bar_far, y, u, next_v, flow, bar_turn, None)
    return (next_xt, next_x, next_vt, next_v, next_yt, next_y, next_ut, next_u)


def solution(mesh):
    river = P(("groups", "river"), None, "hand")
    turn = P("groups", "hand")
    placed = (P(("groups", "river"), "hand"), P("groups"), P("groups"), P(), P(), P(), P(), P(), P(), P(),
              turn, river, turn, river, turn, river, turn, river)
    return jax.shard_map(local, mesh=mesh, in_specs=placed,
                         out_specs=(turn, river, turn, river, turn, river, turn, river), check_vma=False)
```

profile of v0, /device:TPU:0, one launch (start us, length us, event | category | flops | bytes accessed | tf_op | source)
XLA Modules:
  0.0 90.8 jit_solution(4671162535931685964)
XLA Ops:
  1.3 5.2 %stats.1 = (f32[56,768]{1,0:T(8,128)}, f32[48,768]{1,0:T(8,128)}) custom-call(s32[1]{0:T(128)} %bitcast.hand_ref, s32[8]{0:T(128)} %refs_0_.3, s32[4]{0:T(128)} %cards_now_ref.3, s32[2,8,1536]{2,1,0:T(8,128)} %constant.12.clone.refs_2_.card_ref, s32[12,663]{1,0:T(8,128)} %refs_5_.3, f32[12,64,663]{2,1,0:T(8,128)} %x_ref.3, f32[12,16,663]{2,1,0:T(8,128)} %v_ref.3, ...), custom_call_target="tpu_custom_call" | custom-call | flops 5000000000 | tf_op jit(solution)/shard_map/stats/pallas_call | solution.py:540
  6.6 3.0 %collective-permute-start.1 = (f32[56,768]{1,0:T(8,128)}, f32[56,768]{1,0:T(8,128)S(1)}, u32[]{:S(2)}, u32[]{:S(2)}) collective-permute-start(f32[56,768]{1,0:T(8,128)} %get-tuple-element.77), channel_id=1, source_target_pairs={{0,2},{2,0},{4,6},{6,4},{8,10},{10,8},{12,14},{14,12},{1,3},{3,1},... | collective-permute-start | bytes 516104 | tf_op jit(solution)/shard_map/ppermute | solution.py:508
  11.3 3.1 %collective-permute-done.1 = f32[56,768]{1,0:T(8,128)S(1)} collective-permute-done((f32[56,768]{1,0:T(8,128)}, f32[56,768]{1,0:T(8,128)S(1)}, u32[]{:S(2)}, u32[]{:S(2)}) %collective-permute-start.1) | collective-permute-done | bytes 172064 | tf_op jit(solution)/shard_map/ppermute | solution.py:508
  14.5 1.9 %collective-permute-start.3 = (f32[56,768]{1,0:T(8,128)S(1)}, f32[56,768]{1,0:T(8,128)S(1)}, u32[]{:S(2)}, u32[]{:S(2)}) collective-permute-start(f32[56,768]{1,0:T(8,128)S(1)} %add.18), channel_id=1, source_target_pairs={{0,4},{2,6},{4,0},{6,2},{8,12},{10,14},{12,8},{14,10},{1,5},{3,7},... | collective-permute-start | bytes 516104 | tf_op jit(solution)/shard_map/ppermute | solution.py:508
  16.3 2.4 %mover_gradient.8 = (f32[3,64,768]{2,1,0:T(8,128)S(1)}, f32[3,16,768]{2,1,0:T(8,128)S(1)}) custom-call(f32[12,64,663]{2,1,0:T(8,128)S(1)} %copy-done, f32[12,64,663]{2,1,0:T(8,128)S(1)} %collective-permute-done.4.far_ref, f32[12,16,663]{2,1,0:T(8,128)S(1)} %copy-done.1, f32[12,1,1536]{2,1,0:T(1,128)S(1)} %get-tuple-element.78.live_ref, ...), custom_call_target="tpu_custom_call" | custom-call | flops 3000000000 | tf_op jit(solution)/shard_map/mover_gradient/pallas_call | solution.py:540
  20.4 2.6 %collective-permute-start.5 = (f32[56,768]{1,0:T(8,128)S(1)}, f32[56,768]{1,0:T(8,128)S(1)}, u32[]{:S(2)}, u32[]{:S(2)}) collective-permute-start(f32[56,768]{1,0:T(8,128)S(1)} %add.19), channel_id=1, source_target_pairs={{0,8},{2,10},{4,12},{6,14},{8,0},{10,2},{12,4},{14,6},{1,9},{3,11}... | collective-permute-start | bytes 516104 | tf_op jit(solution)/shard_map/ppermute | solution.py:508
  22.9 2.3 %mover_gradient.9 = (f32[3,64,768]{2,1,0:T(8,128)S(1)}, f32[3,16,768]{2,1,0:T(8,128)S(1)}) custom-call(f32[12,64,663]{2,1,0:T(8,128)S(1)} %copy-done, f32[12,64,663]{2,1,0:T(8,128)S(1)} %collective-permute-done.4.far_ref, f32[12,16,663]{2,1,0:T(8,128)S(1)} %copy-done.1, f32[12,1,1536]{2,1,0:T(1,128)S(1)} %get-tuple-element.78.live_ref, ...), custom_call_target="tpu_custom_call" | custom-call | flops 3000000000 | tf_op jit(solution)/shard_map/mover_gradient/pallas_call | solution.py:540
  25.3 4.7 %collective-permute-done.5 = f32[56,768]{1,0:T(8,128)S(1)} collective-permute-done((f32[56,768]{1,0:T(8,128)S(1)}, f32[56,768]{1,0:T(8,128)S(1)}, u32[]{:S(2)}, u32[]{:S(2)}) %collective-permute-start.5) | collective-permute-done | bytes 172064 | tf_op jit(solution)/shard_map/ppermute | solution.py:508
  30.1 2.4 %mover_gradient.10 = (f32[3,64,768]{2,1,0:T(8,128)S(1)}, f32[3,16,768]{2,1,0:T(8,128)S(1)}) custom-call(f32[12,64,663]{2,1,0:T(8,128)S(1)} %copy-done, f32[12,64,663]{2,1,0:T(8,128)S(1)} %collective-permute-done.4.far_ref, f32[12,16,663]{2,1,0:T(8,128)S(1)} %copy-done.1, f32[12,1,1536]{2,1,0:T(1,128)S(1)} %get-tuple-element.78.live_ref, ...), custom_call_target="tpu_custom_call" | custom-call | flops 3000000000 | tf_op jit(solution)/shard_map/mover_gradient/pallas_call | solution.py:540
  33.8 2.4 %mover_gradient.11 = (f32[3,64,768]{2,1,0:T(8,128)S(1)}, f32[3,16,768]{2,1,0:T(8,128)S(1)}) custom-call(f32[12,64,663]{2,1,0:T(8,128)S(1)} %copy-done, f32[12,64,663]{2,1,0:T(8,128)S(1)} %collective-permute-done.4.far_ref, f32[12,16,663]{2,1,0:T(8,128)S(1)} %copy-done.1, f32[12,1,1536]{2,1,0:T(1,128)S(1)} %get-tuple-element.78.live_ref, ...), custom_call_target="tpu_custom_call" | custom-call | flops 3000000000 | tf_op jit(solution)/shard_map/mover_gradient/pallas_call | solution.py:540
  37.5 2.5 %collective-permute-done.rest_1_ = f32[48,768]{1,0:T(8,128)S(1)} collective-permute-done((f32[48,768]{1,0:T(8,128)S(1)}, f32[48,768]{1,0:T(8,128)S(1)}, u32[]{:S(2)}, u32[]{:S(2)}) %collective-permute-start) | collective-permute-done | bytes 147488 | tf_op jit(solution)/shard_map/ppermute | solution.py:505
  40.1 1.9 %turn_step.2 = (f32[48,1536]{1,0:T(8,128)S(1)}, f32[32,1536]{1,0:T(8,128)S(1)}, f32[16,1536]{1,0:T(8,128)S(1)}, f32[8,768]{1,0:T(8,128)S(1)}, f32[8,128]{1,0:T(8,128)S(1)}) custom-call(s32[1]{0:T(128)} %bitcast.hand_ref, s32[4]{0:T(128)S(1)} %copy-done.14, s32[2,8,1536]{2,1,0:T(8,128)S(1)} %copy-done.19, bf16[2,1536,128]{2,1,0:T(8,128)(2,1)S(1)} %copy-done.16, ...), custom_call_target="tpu_custom_call" | custom-call | flops 3000000000 | tf_op jit(solution)/shard_map/turn_step/pallas_call | solution.py:540
  42.1 5.2 %rival_step.4 = (f32[6,64,768]{2,1,0:T(8,128)S(1)}, f32[6,16,768]{2,1,0:T(8,128)S(1)}, f32[40,768]{1,0:T(8,128)S(1)}) custom-call(f32[56,768]{1,0:T(8,128)S(1)} %add.20.rest_2_.own_norm_ref, f32[56,768]{1,0:T(8,128)S(1)} %collective-permute-done.6.rest_3_.far_norm_ref, f32[6,64,768]{2,1,0:T(8,128)S(1)} %get-tuple-element.105.bar_ref, ...), custom_call_target="tpu_custom_call" | custom-call | flops 6000000000 | tf_op jit(solution)/shard_map/rival_step/pallas_call | solution.py:540
  47.4 5.1 %rival_step.5 = (f32[6,64,768]{2,1,0:T(8,128)S(1)}, f32[6,16,768]{2,1,0:T(8,128)S(1)}, f32[40,768]{1,0:T(8,128)S(1)}) custom-call(f32[56,768]{1,0:T(8,128)S(1)} %add.20.rest_2_.own_norm_ref, f32[56,768]{1,0:T(8,128)S(1)} %collective-permute-done.6.rest_3_.far_norm_ref, f32[6,64,768]{2,1,0:T(8,128)S(1)} %get-tuple-element.103.bar_ref, ...), custom_call_target="tpu_custom_call" | custom-call | flops 6000000000 | tf_op jit(solution)/shard_map/rival_step/pallas_call | solution.py:540
  54.0 2.3 %mover_gradient.12 = (f32[3,64,768]{2,1,0:T(8,128)S(1)}, f32[3,16,768]{2,1,0:T(8,128)S(1)}) custom-call(f32[6,64,768]{2,1,0:T(8,128)S(1)} %get-tuple-element.111.y_ref, f32[6,64,768]{2,1,0:T(8,128)S(1)} %collective-permute-done.10.far_ref, f32[6,16,768]{2,1,0:T(8,128)S(1)} %get-tuple-element.112.u_ref, f32[12,1,1536]{2,1,0:T(1,128)S(1)} %get-tuple-element.78.live_ref, ...), custom_call_target="tpu_custom_call" | custom-call | flops 3000000000 | tf_op jit(solution)/shard_map/mover_gradient/pallas_call | solution.py:540
  56.3 1.9 %collective-permute-done.9 = f32[40,768]{1,0:T(8,128)S(1)} collective-permute-done((f32[40,768]{1,0:T(8,128)S(1)}, f32[40,768]{1,0:T(8,128)S(1)}, u32[]{:S(2)}, u32[]{:S(2)}) %collective-permute-start.9) | collective-permute-done | bytes 122912 | tf_op jit(solution)/shard_map/ppermute | solution.py:508
  58.5 2.3 %mover_gradient.13 = (f32[3,64,768]{2,1,0:T(8,128)S(1)}, f32[3,16,768]{2,1,0:T(8,128)S(1)}) custom-call(f32[6,64,768]{2,1,0:T(8,128)S(1)} %get-tuple-element.111.y_ref, f32[6,64,768]{2,1,0:T(8,128)S(1)} %collective-permute-done.10.far_ref, f32[6,16,768]{2,1,0:T(8,128)S(1)} %get-tuple-element.112.u_ref, f32[12,1,1536]{2,1,0:T(1,128)S(1)} %get-tuple-element.78.live_ref, ...), custom_call_target="tpu_custom_call" | custom-call | flops 3000000000 | tf_op jit(solution)/shard_map/mover_gradient/pallas_call | solution.py:540
  60.9 2.3 %collective-permute-done.11 = f32[40,768]{1,0:T(8,128)S(1)} collective-permute-done((f32[40,768]{1,0:T(8,128)S(1)}, f32[40,768]{1,0:T(8,128)S(1)}, u32[]{:S(2)}, u32[]{:S(2)}) %collective-permute-start.11) | collective-permute-done | bytes 122912 | tf_op jit(solution)/shard_map/ppermute | solution.py:508
  64.9 2.4 %mover_gradient.14 = (f32[3,64,768]{2,1,0:T(8,128)S(1)}, f32[3,16,768]{2,1,0:T(8,128)S(1)}) custom-call(f32[6,64,768]{2,1,0:T(8,128)S(1)} %get-tuple-element.117.y_ref, f32[6,64,768]{2,1,0:T(8,128)S(1)} %collective-permute-done.13.far_ref, f32[6,16,768]{2,1,0:T(8,128)S(1)} %get-tuple-element.118.u_ref, f32[12,1,1536]{2,1,0:T(1,128)S(1)} %get-tuple-element.78.live_ref, ...), custom_call_target="tpu_custom_call" | custom-call | flops 3000000000 | tf_op jit(solution)/shard_map/mover_gradient/pallas_call | solution.py:540
  67.3 3.1 %collective-permute-done.12 = f32[40,768]{1,0:T(8,128)S(1)} collective-permute-done((f32[40,768]{1,0:T(8,128)S(1)}, f32[40,768]{1,0:T(8,128)S(1)}, u32[]{:S(2)}, u32[]{:S(2)}) %collective-permute-start.12) | collective-permute-done | bytes 122912 | tf_op jit(solution)/shard_map/ppermute | solution.py:508
  70.4 2.4 %mover_gradient.15 = (f32[3,64,768]{2,1,0:T(8,128)S(1)}, f32[3,16,768]{2,1,0:T(8,128)S(1)}) custom-call(f32[6,64,768]{2,1,0:T(8,128)S(1)} %get-tuple-element.117.y_ref, f32[6,64,768]{2,1,0:T(8,128)S(1)} %collective-permute-done.13.far_ref, f32[6,16,768]{2,1,0:T(8,128)S(1)} %get-tuple-element.118.u_ref, f32[12,1,1536]{2,1,0:T(1,128)S(1)} %get-tuple-element.78.live_ref, ...), custom_call_target="tpu_custom_call" | custom-call | flops 3000000000 | tf_op jit(solution)/shard_map/mover_gradient/pallas_call | solution.py:540
  76.7 2.3 %turn_step.3 = (f32[16,1536]{1,0:T(8,128)S(1)}, f32[16,663]{1,0:T(8,128)}, f32[6,663]{1,0:T(8,128)}, f32[16,663]{1,0:T(8,128)}, f32[6,663]{1,0:T(8,128)}) custom-call(s32[1]{0:T(128)} %bitcast.hand_ref, s32[4]{0:T(128)S(1)} %copy-done.14, s32[2,8,1536]{2,1,0:T(8,128)S(1)} %copy-done.19, bf16[2,1536,128]{2,1,0:T(8,128)(2,1)S(1)} %copy-done.16, ...), custom_call_target="tpu_custom_call" | custom-call | flops 3000000000 | tf_op jit(solution)/shard_map/turn_step/pallas_call | solution.py:540
  79.0 6.0 %rival_step.6 = (f32[12,64,663]{2,1,0:T(8,128)}, f32[12,16,663]{2,1,0:T(8,128)}) custom-call(f32[40,768]{1,0:T(8,128)S(1)} %add.23.rest_4_.own_norm_ref, f32[40,768]{1,0:T(8,128)S(1)} %collective-permute-done.14.rest_5_.far_norm_ref, f32[6,64,768]{2,1,0:T(8,128)S(1)} %get-tuple-element.138.bar_ref, f32[6,64,768]{2,1,0:T(8,128)S(1)} %collective-permute-done.16.far_ref, ...), custom_call_target="tpu_custom_call" | custom-call | flops 6000000000 | tf_op jit(solution)/shard_map/rival_step/pallas_call | solution.py:540
  85.0 5.8 %rival_step.7 = (f32[12,64,663]{2,1,0:T(8,128)}, f32[12,16,663]{2,1,0:T(8,128)}) custom-call(f32[40,768]{1,0:T(8,128)S(1)} %add.23.rest_4_.own_norm_ref, f32[40,768]{1,0:T(8,128)S(1)} %collective-permute-done.14.rest_5_.far_norm_ref, f32[6,64,768]{2,1,0:T(8,128)S(1)} %get-tuple-element.136.bar_ref, ...), custom_call_target="tpu_custom_call", output_to_operand_aliasing={{0}: (20, {}), {1}: (21, {})} | custom-call | flops 6000000000 | tf_op jit(solution)/shard_map/rival_step/pallas_call | solution.py:540
  (78 shorter events, 14.4 us)
Async XLA Ops:
  0.6 15.7 %collective-permute-start.4 = (f32[12,64,663]{2,1,0:T(8,128)}, f32[12,64,663]{2,1,0:T(8,128)S(1)}, u32[]{:S(2)}, u32[]{:S(2)}) collective-permute-start(f32[12,64,663]{2,1,0:T(8,128)} %y_ref.11), channel_id=1, source_target_pairs={{0,1},{1,0},{2,3},{3,2},{4,5},{5,4},{6,7},{7,6},{8,9},{9,8},{10,11... | collective-permute-start | bytes 6110216 | tf_op jit(solution)/shard_map/ppermute | solution.py:505
  1.2 8.5 %collective-permute-start.2 = (s32[12,663]{1,0:T(8,128)}, s32[12,663]{1,0:T(8,128)S(1)}, u32[]{:S(2)}, u32[]{:S(2)}) collective-permute-start(s32[12,663]{1,0:T(8,128)} %refs_5_.3), channel_id=1, source_target_pairs={{0,1},{1,0},{2,3},{3,2},{4,5},{5,4},{6,7},{7,6},{8,9},{9,8},{10,11... | collective-permute-start | bytes 95480 | tf_op jit(solution)/shard_map/ppermute | solution.py:505
  1.2 8.4 %copy-start.10 = (s32[16,64]{1,0:T(8,128)S(1)}, s32[16,64]{1,0:T(8,128)}, u32[]{:S(2)}) copy-start(s32[16,64]{1,0:T(8,128)} %children_ref.7) | copy-start | bytes 12292
  1.3 8.4 %copy-start.13 = (s32[8]{0:T(128)S(1)}, s32[8]{0:T(128)}, u32[]{:S(2)}) copy-start(s32[8]{0:T(128)} %refs_0_.3) | copy-start | bytes 100
  1.3 8.4 %copy-start.14 = (s32[4]{0:T(128)S(1)}, s32[4]{0:T(128)}, u32[]{:S(2)}) copy-start(s32[4]{0:T(128)} %cards_now_ref.3) | copy-start | bytes 52
  1.3 8.4 %copy-start.15 = (bf16[2,128,1536]{2,1,0:T(8,128)(2,1)S(1)}, bf16[2,128,1536]{2,1,0:T(8,128)(2,1)}, u32[]{:S(2)}) copy-start(bf16[2,128,1536]{2,1,0:T(8,128)(2,1)} %constant.14.clone.refs_4_.spread_ref) | copy-start | bytes 2359300
  6.6 9.8 %copy-start = (f32[12,64,663]{2,1,0:T(8,128)S(1)}, f32[12,64,663]{2,1,0:T(8,128)}, u32[]{:S(2)}) copy-start(f32[12,64,663]{2,1,0:T(8,128)} %y_ref.11) | copy-start | bytes 6110212
  6.6 9.8 %copy-start.1 = (f32[12,16,663]{2,1,0:T(8,128)S(1)}, f32[12,16,663]{2,1,0:T(8,128)}, u32[]{:S(2)}) copy-start(f32[12,16,663]{2,1,0:T(8,128)} %u_ref.11) | copy-start | bytes 1527556
  6.6 9.7 %copy-start.2 = (f32[48,768]{1,0:T(8,128)S(1)}, f32[48,768]{1,0:T(8,128)}, u32[]{:S(2)}) copy-start(f32[48,768]{1,0:T(8,128)} %get-tuple-element.76.pack_ref.rest_0_) | copy-start | bytes 442372
  6.6 7.8 %collective-permute-start.1 = (f32[56,768]{1,0:T(8,128)}, f32[56,768]{1,0:T(8,128)S(1)}, u32[]{:S(2)}, u32[]{:S(2)}) collective-permute-start(f32[56,768]{1,0:T(8,128)} %get-tuple-element.77), channel_id=1, source_target_pairs={{0,2},{2,0},{4,6},{6,4},{8,10},{10,8},{12,14},{14,12},{1,3},{3,1},... | collective-permute-start | bytes 516104 | tf_op jit(solution)/shard_map/ppermute | solution.py:508
  14.5 5.9 %collective-permute-start.3 = (f32[56,768]{1,0:T(8,128)S(1)}, f32[56,768]{1,0:T(8,128)S(1)}, u32[]{:S(2)}, u32[]{:S(2)}) collective-permute-start(f32[56,768]{1,0:T(8,128)S(1)} %add.18), channel_id=1, source_target_pairs={{0,4},{2,6},{4,0},{6,2},{8,12},{10,14},{12,8},{14,10},{1,5},{3,7},... | collective-permute-start | bytes 516104 | tf_op jit(solution)/shard_map/ppermute | solution.py:508
  20.4 9.6 %collective-permute-start.5 = (f32[56,768]{1,0:T(8,128)S(1)}, f32[56,768]{1,0:T(8,128)S(1)}, u32[]{:S(2)}, u32[]{:S(2)}) collective-permute-start(f32[56,768]{1,0:T(8,128)S(1)} %add.19), channel_id=1, source_target_pairs={{0,8},{2,10},{4,12},{6,14},{8,0},{10,2},{12,4},{14,6},{1,9},{3,11}... | collective-permute-start | bytes 516104 | tf_op jit(solution)/shard_map/ppermute | solution.py:508
  30.0 2.5 %collective-permute-start.6 = (f32[56,768]{1,0:T(8,128)S(1)}, f32[56,768]{1,0:T(8,128)S(1)}, u32[]{:S(2)}, u32[]{:S(2)}) collective-permute-start(f32[56,768]{1,0:T(8,128)S(1)} %add.20.rest_2_.own_norm_ref), channel_id=1, source_target_pairs={{0,1},{1,0},{2,3},{3,2},{4,5},{5,4},{6,7},{7,6},{8,9},{9,8},{10,11... | collective-permute-start | bytes 516104 | tf_op jit(solution)/shard_map/ppermute | solution.py:505
  33.3 8.8 %collective-permute-start.8 = (f32[6,64,768]{2,1,0:T(8,128)S(1)}, f32[6,64,768]{2,1,0:T(8,128)S(1)}, u32[]{:S(2)}, u32[]{:S(2)}) collective-permute-start(f32[6,64,768]{2,1,0:T(8,128)S(1)} %get-tuple-element.105.bar_ref), channel_id=1, source_target_pairs={{0,1},{1,0},{2,3},{3,2},{4,5},{5,4},{6,7},{7,6},{8,9},{9,8},{10,11... | collective-permute-start | bytes 3538952 | tf_op jit(solution)/shard_map/ppermute | solution.py:505
  37.0 10.4 %collective-permute-start.7 = (f32[6,64,768]{2,1,0:T(8,128)S(1)}, f32[6,64,768]{2,1,0:T(8,128)S(1)}, u32[]{:S(2)}, u32[]{:S(2)}) collective-permute-start(f32[6,64,768]{2,1,0:T(8,128)S(1)} %get-tuple-element.103.bar_ref), channel_id=1, source_target_pairs={{0,1},{1,0},{2,3},{3,2},{4,5},{5,4},{6,7},{7,6},{8,9},{9,8},{10,11... | collective-permute-start | bytes 3538952 | tf_op jit(solution)/shard_map/ppermute | solution.py:505
  37.1 3.0 %collective-permute-start = (f32[48,768]{1,0:T(8,128)S(1)}, f32[48,768]{1,0:T(8,128)S(1)}, u32[]{:S(2)}, u32[]{:S(2)}) collective-permute-start(f32[48,768]{1,0:T(8,128)S(1)} %copy-done.2), channel_id=1, source_target_pairs={{0,1},{1,0},{2,3},{3,2},{4,5},{5,4},{6,7},{7,6},{8,9},{9,8},{10,11... | collective-permute-start | bytes 442376 | tf_op jit(solution)/shard_map/ppermute | solution.py:505
  47.2 6.7 %collective-permute-start.10 = (f32[6,64,768]{2,1,0:T(8,128)S(1)}, f32[6,64,768]{2,1,0:T(8,128)S(1)}, u32[]{:S(2)}, u32[]{:S(2)}) collective-permute-start(f32[6,64,768]{2,1,0:T(8,128)S(1)} %get-tuple-element.111.y_ref), channel_id=1, source_target_pairs={{0,1},{1,0},{2,3},{3,2},{4,5},{5,4},{6,7},{7,6},{8,9},{9,8},{10,11... | collective-permute-start | bytes 3538952 | tf_op jit(solution)/shard_map/ppermute | solution.py:505
  52.5 12.4 %collective-permute-start.13 = (f32[6,64,768]{2,1,0:T(8,128)S(1)}, f32[6,64,768]{2,1,0:T(8,128)S(1)}, u32[]{:S(2)}, u32[]{:S(2)}) collective-permute-start(f32[6,64,768]{2,1,0:T(8,128)S(1)} %get-tuple-element.117.y_ref), channel_id=1, source_target_pairs={{0,1},{1,0},{2,3},{3,2},{4,5},{5,4},{6,7},{7,6},{8,9},{9,8},{10,11... | collective-permute-start | bytes 3538952 | tf_op jit(solution)/shard_map/ppermute | solution.py:505
  52.9 5.3 %collective-permute-start.9 = (f32[40,768]{1,0:T(8,128)S(1)}, f32[40,768]{1,0:T(8,128)S(1)}, u32[]{:S(2)}, u32[]{:S(2)}) collective-permute-start(f32[40,768]{1,0:T(8,128)S(1)} %get-tuple-element.110), channel_id=1, source_target_pairs={{0,2},{2,0},{4,6},{6,4},{8,10},{10,8},{12,14},{14,12},{1,3},{3,1},... | collective-permute-start | bytes 368648 | tf_op jit(solution)/shard_map/ppermute | solution.py:508
  58.2 4.9 %collective-permute-start.11 = (f32[40,768]{1,0:T(8,128)S(1)}, f32[40,768]{1,0:T(8,128)S(1)}, u32[]{:S(2)}, u32[]{:S(2)}) collective-permute-start(f32[40,768]{1,0:T(8,128)S(1)} %add.21), channel_id=1, source_target_pairs={{0,4},{2,6},{4,0},{6,2},{8,12},{10,14},{12,8},{14,10},{1,5},{3,7},... | collective-permute-start | bytes 368648 | tf_op jit(solution)/shard_map/ppermute | solution.py:508
  63.2 7.2 %collective-permute-start.12 = (f32[40,768]{1,0:T(8,128)S(1)}, f32[40,768]{1,0:T(8,128)S(1)}, u32[]{:S(2)}, u32[]{:S(2)}) collective-permute-start(f32[40,768]{1,0:T(8,128)S(1)} %add.22), channel_id=1, source_target_pairs={{0,8},{2,10},{4,12},{6,14},{8,0},{10,2},{12,4},{14,6},{1,9},{3,11}... | collective-permute-start | bytes 368648 | tf_op jit(solution)/shard_map/ppermute | solution.py:508
  70.4 2.5 %collective-permute-start.14 = (f32[40,768]{1,0:T(8,128)S(1)}, f32[40,768]{1,0:T(8,128)S(1)}, u32[]{:S(2)}, u32[]{:S(2)}) collective-permute-start(f32[40,768]{1,0:T(8,128)S(1)} %add.23.rest_4_.own_norm_ref), channel_id=1, source_target_pairs={{0,1},{1,0},{2,3},{3,2},{4,5},{5,4},{6,7},{7,6},{8,9},{9,8},{10,11... | collective-permute-start | bytes 368648 | tf_op jit(solution)/shard_map/ppermute | solution.py:505
  74.5 4.5 %collective-permute-start.16 = (f32[6,64,768]{2,1,0:T(8,128)S(1)}, f32[6,64,768]{2,1,0:T(8,128)S(1)}, u32[]{:S(2)}, u32[]{:S(2)}) collective-permute-start(f32[6,64,768]{2,1,0:T(8,128)S(1)} %get-tuple-element.138.bar_ref), channel_id=1, source_target_pairs={{0,1},{1,0},{2,3},{3,2},{4,5},{5,4},{6,7},{7,6},{8,9},{9,8},{10,11... | collective-permute-start | bytes 3538952 | tf_op jit(solution)/shard_map/ppermute | solution.py:505
  76.7 8.4 %collective-permute-start.15 = (f32[6,64,768]{2,1,0:T(8,128)S(1)}, f32[6,64,768]{2,1,0:T(8,128)S(1)}, u32[]{:S(2)}, u32[]{:S(2)}) collective-permute-start(f32[6,64,768]{2,1,0:T(8,128)S(1)} %get-tuple-element.136.bar_ref), channel_id=1, source_target_pairs={{0,1},{1,0},{2,3},{3,2},{4,5},{5,4},{6,7},{7,6},{8,9},{9,8},{10,11... | collective-permute-start | bytes 3538952 | tf_op jit(solution)/shard_map/ppermute | solution.py:505
  (14 other events, 85.7 us)
where the time goes:
time: 91 us; the launch traced here: 90.8 us
  Pallas kernels  56.9 us (63%)
  waiting for transfers between devices  19.2 us (21%)
  starting transfers between devices  13.4 us (15%)
  between operations  1.02 us (1%)
    pallas_call x20, Pallas kernels, call(): pl.pallas_call(kernel, grid_spec=pltpu.PrefetchScalarGridSpec(num_scalar_...  56.9 us
    ppermute x6, waiting for transfers between devices, hop_total(): lax.ppermute(value, 'river', [(at, at ^ hop) for at in range(river_count)])  16.7 us
    ppermute x6, starting transfers between devices, hop_total(): lax.ppermute(value, 'river', [(at, at ^ hop) for at in range(river_count)])  10.5 us
    ppermute x11, starting transfers between devices, swap(): return lax.ppermute(value, 'hand', [(0, 1), (1, 0)])  2.9 us
    ppermute x11, waiting for transfers between devices, swap(): return lax.ppermute(value, 'hand', [(0, 1), (1, 0)])  2.57 us
  transfers between devices with their start and end apart: 17, of which 7 were waited for; matrix products, arithmetic and copies ran while one was open for 0% of the time, Pallas kernels for 54%

commit v1 on v0

--- a/solution.py
+++ b/solution.py
@@ -17,6 +17,7 @@
 LANES = 128
 TILE = 256
 VMEM_BYTES = 20 * 2**20
+STATS_BOARDS = 6
 F32 = jnp.float32
 BF16 = jnp.bfloat16
 
@@ -311,17 +312,27 @@
         total_ref[...] = rest[2 * parts][...] if start else jnp.zeros_like(total_ref)
     padded = bar_ref.shape[2]
     primal, _ = steps_from(own_norm_ref[norm_row:norm_row + 8], far_norm_ref[norm_row:norm_row + 8], count)
-    for board in range(parts * group):
-        live = live_ref[start + board][:, :padded]
-        x = jnp.where(live > 0, pick(x_ref, bases[0], 0, board, group), 0.0)
-        v = jnp.where(live > 0, pick(v_ref, bases[1], 0, board, group), 0.0)
-        new_x = live * jnp.maximum(x - primal * grads[board // group][board % group], 0.0)
-        new_v = v + primal * flows[board // group][board % group]
-        new_x_ref[board] = new_x
-        new_v_ref[board] = new_v
-        bar_ref[board] = 2.0 * new_x - x
-        if not last:
-            total_ref[0:1] += row_sums(new_x * new_x) + row_sums(new_v * new_v)
+
+    def work(part):
+        for inner in range(group):
+            board = part * group + inner
+            place = inner if last else board
+            live = live_ref[start + board][:, :padded]
+            x = jnp.where(live > 0, pick(x_ref, bases[0], 0, board, group), 0.0)
+            v = jnp.where(live > 0, pick(v_ref, bases[1], 0, board, group), 0.0)
+            new_x = live * jnp.maximum(x - primal * grads[part][inner], 0.0)
+            new_v = v + primal * flows[part][inner]
+            new_x_ref[place] = new_x
+            new_v_ref[place] = new_v
+            bar_ref[board] = 2.0 * new_x - x
+            if not last:
+                total_ref[0:1] += row_sums(new_x * new_x) + row_sums(new_v * new_v)
+
+    for part in range(parts):
+        if last:
+            pl.when(pl.program_id(0) == part)(functools.partial(work, part))
+        else:
+            work(part)
 
 
 def rival_step_kernel(group, start, bases, count, norm_row, parts, last, own_norm_ref, far_norm_ref, bar_ref, far_ref, y_ref,
@@ -388,42 +399,71 @@
             total_ref[infosets:2 * infosets] += exact_left(step, plan_scratch[...])
 
 
+def turn_places(sequences, points):
+    return 0, 2 * sequences, sequences, 2 * sequences + round_up(points, 8)
+
+
+def turn_mix(turn, plan, gather_ref, spread_ref):
+    return turn * (exact_right(exact_right(plan, gather_ref[0]), spread_ref[0]) + plan)
+
+
+def turn_tree(turn_children_ref, turn_parents_ref):
+    parents = turn_parents_ref[...].astype(F32)
+    return turn_children_ref[...].astype(F32) - parents, 1.0 - jnp.sum(parents, axis=1, keepdims=True)
+
+
+def turn_start_kernel(first, hand_ref, cards_now_ref, card_ref, gather_ref, spread_ref, *rest):
+    if first:
+        own_ref, far_ref = rest[:2]
+        pack = jnp.concatenate([own_ref[...], far_ref[...]], axis=1)
+    else:
+        pack_ref, old_bar_ref = rest[:2]
+        pack = pack_ref[...]
+    turn_fold_ref, turn_children_ref, turn_parents_ref, children_ref, parents_ref = rest[2:7]
+    grad_ref, flow_ref, link_ref, extra_ref = rest[7:]
+    turn = alive_rows(card_ref[0], cards_now_ref)
+    link = river_link(parents_ref, children_ref.shape[1])
+    step, root = turn_tree(turn_children_ref, turn_parents_ref)
+    fold = turn_fold_ref[...]
+    sequences, points = fold.shape[0], step.shape[0]
+    _, _, y_at, u_at = turn_places(sequences, points)
+    y = pack[y_at:y_at + sequences]
+    u = pack[u_at:u_at + points]
+    grad_ref[...] = pair_dot(fold, turn_mix(turn, y, gather_ref, spread_ref)) / H + turn * exact_left(step.T, u)
+    flow_ref[...] = turn * (exact_left(step, y) - root)
+    link_ref[...] = exact_left(link, y)
+    extra_ref[...] = pack if first else exact_left(link, old_bar_ref[...])
+
+
 def turn_step_kernel(count, first, names, hand_ref, cards_now_ref, card_ref, gather_ref, spread_ref, *rest):
+    pack_ref, grad_ref, flow_ref, link_ref = rest[:4]
     if first:
-        own_ref, far_ref, sums_ref, sums_far_ref = rest[:4]
-        rest = rest[4:]
+        sums_ref, sums_far_ref = rest[4:6]
+        rest = rest[6:]
     else:
-        pack_ref, kept_ref, old_bar_ref, old_steps_ref, sums_ref, sums_far_ref = rest[:6]
-        rest = rest[6:]
+        bar_link_ref, kept_ref, old_steps_ref, sums_ref, sums_far_ref = rest[4:9]
+        rest = rest[9:]
     turn_fold_ref, turn_children_ref, turn_parents_ref, children_ref, parents_ref = rest[:5]
     rest = rest[5:]
     turn = alive_rows(card_ref[0], cards_now_ref)
-    _, link = river_steps(children_ref, parents_ref)
-    link_turned = link.T
-    parents = turn_parents_ref[...].astype(F32)
-    turn_step = turn_children_ref[...].astype(F32) - parents
-    turn_root = 1.0 - jnp.sum(parents, axis=1, keepdims=True)
-    step_turned = turn_step.T
+    link_turned = river_link(parents_ref, children_ref.shape[1]).T
+    turn_step, turn_root = turn_tree(turn_children_ref, turn_parents_ref)
     fold = turn_fold_ref[...]
     meetings = (CARDS - 6) * turn
     sequences = fold.shape[0]
     points = turn_step.shape[0]
-    slab = round_up(points, 8)
-    starts = (0, 2 * sequences, sequences, 2 * sequences + slab)
-    infosets = link.shape[0]
+    starts = turn_places(sequences, points)
+    infosets = link_turned.shape[1]
     norm_row = (3 if first else 2) * infosets
     primal, dual = steps_from(sums_ref[norm_row:norm_row + 8], sums_far_ref[norm_row:norm_row + 8], count)
     sums = jnp.concatenate([sums_ref[:norm_row], sums_far_ref[:norm_row]], axis=1)
+    pack = pack_ref[...]
     if first:
-        pack = jnp.concatenate([own_ref[...], far_ref[...]], axis=1)
         price_sum = sums[:infosets]
         kept = sums[infosets:2 * infosets]
         plan_sum = sums[2 * infosets:]
     else:
-        pack = pack_ref[...]
-        old_dual = old_steps_ref[1:2, 0:1]
-        price_sum = kept_ref[:infosets] + old_dual * (
-            sums[:infosets] - meetings * exact_left(link, old_bar_ref[...]))
+        price_sum = kept_ref[:infosets] + old_steps_ref[1:2, 0:1] * (sums[:infosets] - meetings * bar_link_ref[...])
         kept = kept_ref[infosets:]
         plan_sum = sums[infosets:]
     x = pack[starts[0]:starts[0] + sequences]
@@ -431,17 +471,14 @@
     y = pack[starts[2]:starts[2] + sequences]
     u = pack[starts[3]:starts[3] + points]
 
-    def mix(plan):
-        return turn * (exact_right(exact_right(plan, gather_ref[0]), spread_ref[0]) + plan)
-
-    grad = pair_dot(fold, mix(y)) / H + turn * (exact_left(step_turned, u) - exact_left(link_turned, price_sum))
+    grad = grad_ref[...] - turn * exact_left(link_turned, price_sum)
     new_x = turn * jnp.maximum(x - primal * grad, 0.0)
-    new_v = v + primal * (turn * (exact_left(turn_step, y) - turn_root))
+    new_v = v + primal * flow_ref[...]
     bar = 2.0 * new_x - x
     price_bar = 2.0 * new_v - v
-    drift = primal * (plan_sum - meetings * exact_left(link, y))
-    rise = pair_dot(fold.T, mix(bar)) / H - turn * (
-        exact_left(step_turned, price_bar) - exact_left(link_turned, kept + 2.0 * drift))
+    drift = primal * (plan_sum - meetings * link_ref[...])
+    rise = pair_dot(fold.T, turn_mix(turn, bar, gather_ref, spread_ref)) / H - turn * (
+        exact_left(turn_step.T, price_bar) - exact_left(link_turned, kept + 2.0 * drift))
     new_y = turn * jnp.maximum(y + dual * rise, 0.0)
     new_u = u + dual * (turn * (exact_left(turn_step, bar) - turn_root))
     if first:
@@ -491,6 +528,7 @@
     group = next(size for size in (3, 2, 1) if slots % size == 0)
     chunks = slots // group
     parts = 2 if chunks % 2 == 0 else 1
+    stats_group = STATS_BOARDS if slots % STATS_BOARDS == 0 else group
     span = parts * group
     cards, gather, spread, near = (jnp.asarray(table) for table in halves(width, padded))
     hand = lax.axis_index("hand").astype(jnp.int32).reshape(1)
@@ -509,20 +547,6 @@
         if gate is not None:
             came, _ = lax.optimization_barrier((came, gate))
         return value + came
-
-    def reduced(value, gates):
-        gates = list(gates)
-        if river_count & (river_count - 1):
-            value = lax.psum(value, "river")
-        else:
-            hop = 1
-            while hop < river_count:
-                value = hop_total(value, hop, gates.pop(0) if gates else None)
-                hop *= 2
-        far = swap(value)
-        if gates:
-            far, _ = lax.optimization_barrier((far, gates[0]))
-        return value, far
 
     def boards(rows, size=group, start=0):
         return pl.BlockSpec((size, rows, padded), lambda at, *_: (at + start, 0, 0))
@@ -559,15 +583,15 @@
     rival_far = swap(rival_river)
 
     def stats_kernel_here(hand_ref, *refs):
-        stats_kernel(slots, group, "river", *refs)
+        stats_kernel(slots, stats_group, "river", *refs)
 
     def prepare_kernel_here(hand_ref, *refs):
         prepare_kernel(slots, group, "river", *refs)
 
     sums, pack = call(
-        stats_kernel_here, "stats", 1, (slots // group,),
-        [smem(), smem(), card_block, half_block(slots), boards(sequences), boards(infosets),
-         boards(sequences), boards(infosets), half_block(turn_sequences), half_block(points),
+        stats_kernel_here, "stats", 1, (slots // stats_group,),
+        [smem(), smem(), card_block, half_block(slots), boards(sequences, stats_group), boards(infosets, stats_group),
+         boards(sequences, stats_group), boards(infosets, stats_group), half_block(turn_sequences), half_block(points),
          half_block(turn_sequences), half_block(points)] + tree_blocks,
         [whole((stat_rows, padded)), whole((pack_rows, padded))],
         [shape(stat_rows, padded), shape(pack_rows, padded)],
@@ -589,16 +613,35 @@
          river_children, river_parents), 2)
     live = tables[0]
 
-    def gradients(y, y_far, u, pack):
+    def gradients(value, early, y, y_far, u, pack, beside, stage):
         out = []
-        for first in range(0, slots, group):
-            arrays, specs, bases = zip(*(operand(item, first, group) for item in (y, y_far, u)))
-            args = (*arrays, *tables, pack, river_parents)
-            out.append(call(
-                functools.partial(mover_gradient_kernel, group, first, bases, turn_sequences), "mover_gradient", 0, (1,),
-                [*specs] + [vmem] * (len(args) - 3), [vmem] * 2,
-                [shape(group, sequences, padded), shape(group, infosets, padded)], [], args, group))
-        return [item[0] for item in out], [item[1] for item in out]
+        hops = [1 << at for at in range(max(river_count - 1, 1).bit_length())]
+        if river_count & (river_count - 1):
+            value = lax.psum(value, "river")
+            hops = []
+        extra = None
+        for place in range(max(len(hops), 1)):
+            near_now = tables[4]
+            if place:
+                near_now, _ = lax.optimization_barrier((near_now, value))
+            gate = []
+            if place == min(stage, len(hops) - 1) or not hops:
+                extra = beside(early, value)
+                gate.extend(extra)
+            while len(out) * group < slots and (len(out) <= place or place >= len(hops) - 1):
+                first = len(out) * group
+                arrays, specs, bases = zip(*(operand(item, first, group) for item in (y, y_far, u)))
+                args = (*arrays, *tables[:4], near_now, *tables[5:], pack, river_parents)
+                out.append(call(
+                    functools.partial(mover_gradient_kernel, group, first, bases, turn_sequences), "mover_gradient", 0, (1,),
+                    [*specs] + [vmem] * (len(args) - 3), [vmem] * 2,
+                    [shape(group, sequences, padded), shape(group, infosets, padded)], [], args, group))
+                gate.append(out[-1][1])
+            if hops:
+                value = hop_total(value, hops[place], gate)
+                if place == 0:
+                    value, early = lax.optimization_barrier((value, early))
+        return [item[0] for item in out], [item[1] for item in out], (value, swap(value)), extra
 
     def mover_steps(last, norms, norm_row, x, v, grad, flow):
         outs = []
@@ -609,7 +652,7 @@
             in_specs = [vmem] * 2 + [*specs] + [vmem] * (1 + 2 * parts)
             aliases = {}
             if last:
-                out_specs = [boards(sequences, span, first // span), boards(infosets, span, first // span), vmem]
+                out_specs = [boards(sequences, group, first // group), boards(infosets, group, first // group), vmem]
                 out_shape = [shape(slots, sequences, width), shape(slots, infosets, width), shape(span, sequences, padded)]
                 if first:
                     aliases = {len(args): 0, len(args) + 1: 1}
@@ -623,7 +666,7 @@
                     in_specs += [vmem]
                     args += (outs[-1][3],)
             outs.append(call(functools.partial(mover_step_kernel, group, first, bases, count, norm_row, parts, last),
-                             "mover_step", 0, (1,), in_specs, out_specs, out_shape, [], args, parts, aliases))
+                             "mover_step", 0, (parts if last else 1,), in_specs, out_specs, out_shape, [], args, parts, aliases))
         if last:
             return outs[-1][0], outs[-1][1], [item[2] for item in outs]
         return [item[0] for item in outs], [item[1] for item in outs], [item[2] for item in outs], outs[-1][3]
@@ -672,22 +715,36 @@
             functools.partial(turn_step_kernel, count, first, ("river", "hand")), "turn_step", 1, (1,),
             turn_blocks + [vmem] * len(data) + [whole(item.shape) for item in turn_matrices],
             [vmem] * 5 if first else [vmem] + [whole(item.shape) for item in out_shape[1:]],
-            out_shape, [], (hand, *turn_tables, *data, *turn_matrices), 3)
-
-    pack_far = swap(pack)
-    grad, flow = gradients(rival_river, rival_far, rival_river_price, pack)
-    norms = reduced(sums, [live] + flow[:3])
+            out_shape, [], (hand, *turn_tables, *data, *turn_matrices), 2)
+
+    def turn_start(first, data):
+        out_shape = [shape(turn_sequences, both), shape(points, both), shape(infosets, both),
+                     shape(pack_rows if first else infosets, both)]
+        return call(
+            functools.partial(turn_start_kernel, first), "turn_start", 1, (1,),
+            turn_blocks + [vmem] * 2 + [whole(item.shape) for item in turn_matrices], [vmem] * 4, out_shape, [],
+            (hand, *turn_tables, *data, *turn_matrices), 1)
+
+    def first_start(far, value):
+        near_now, _ = lax.optimization_barrier((pack, value))
+        return turn_start(True, (near_now, far))
+
+    grad, flow, norms, starts = gradients(sums, swap(pack), rival_river, rival_far, rival_river_price, pack, first_start, 2)
     x, v, bar, part = mover_steps(False, norms, 3 * infosets, mover_river, mover_river_price, grad, flow)
     bar_far = [swap(item) for item in bar]
-    pack, kept, bar_turn, turn_norms, turn_steps = turn_call(True, (pack, pack_far, *norms))
+    pack, kept, bar_turn, turn_norms, turn_steps = turn_call(True, (starts[3], *starts[:3], *norms))
     y, u, total = rival_steps(False, norms, 3 * infosets, bar, bar_far, rival_river, rival_river_price, v, flow, bar_turn,
                               (part, turn_norms))
     y_far = [swap(item) for item in y]
-    grad, flow = gradients(y, y_far, u, pack)
-    norms = reduced(total, flow)
+
+    def second_start(far, value):
+        now, _ = lax.optimization_barrier((pack, value))
+        return turn_start(False, (now, bar_turn))
+
+    grad, flow, norms, starts = gradients(total, y_far[0], y, y_far, u, pack, second_start, 1)
     next_x, next_v, bar = mover_steps(True, norms, 2 * infosets, x, v, grad, flow)
     bar_far = [swap(item) for item in bar]
-    bar_turn, next_xt, next_vt, next_yt, next_ut = turn_call(False, (pack, kept, bar_turn, turn_steps, *norms))
+    bar_turn, next_xt, next_vt, next_yt, next_ut = turn_call(False, (pack, *starts, kept, turn_steps, *norms))
     next_y, next_u = rival_steps(True, norms, 2 * infosets, bar, bar_far, y, u, next_v, flow, bar_turn, None)
     return (next_xt, next_x, next_vt, next_v, next_yt, next_y, next_ut, next_u)
 

time: 91 us -> 83.7 us (0.920)
  waiting for transfers between devices: 19.2 us -> 10.2 us
  Pallas kernels: 56.9 us -> 58 us
    ppermute x6, waiting for transfers between devices: 16.7 us -> 7.42 us  [hop_total(): lax.ppermute(value, 'river', [(at, at ^ hop) for at in range(river_count)])]
    pallas_call x20 -> x22, Pallas kernels: 56.9 us -> 58 us  [call(): pl.pallas_call(kernel, grid_spec=pltpu.PrefetchScalarGridSpec(num_scalar_...]
  transfers between devices with their start and end apart: 17 -> 17, of which waited for: 7 -> 8; matrix products, arithmetic and copies ran while one was open for 0% -> 0% of each run, Pallas kernels for 54% -> 60%
where the time goes in v1:
time: 83.7 us; the launch traced here: 83.6 us
  Pallas kernels  58 us (69%)
  starting transfers between devices  14.1 us (17%)
  waiting for transfers between devices  10.2 us (12%)
  between operations  1.02 us (1%)
    pallas_call x22, Pallas kernels, call(): pl.pallas_call(kernel, grid_spec=pltpu.PrefetchScalarGridSpec(num_scalar_...  58 us
    ppermute x6, starting transfers between devices, hop_total(): lax.ppermute(value, 'river', [(at, at ^ hop) for at in range(river_count)])  11.2 us
    ppermute x6, waiting for transfers between devices, hop_total(): lax.ppermute(value, 'river', [(at, at ^ hop) for at in range(river_count)])  7.42 us
    ppermute x11, starting transfers between devices, swap(): return lax.ppermute(value, 'hand', [(0, 1), (1, 0)])  2.9 us
    ppermute x11, waiting for transfers between devices, swap(): return lax.ppermute(value, 'hand', [(0, 1), (1, 0)])  2.74 us
  transfers between devices with their start and end apart: 17, of which 8 were waited for; matrix products, arithmetic and copies ran while one was open for 0% of the time, Pallas kernels for 60%

profile of v1, /device:TPU:0, one launch (start us, length us, event | category | flops | bytes accessed | tf_op | source)
XLA Modules:
  0.0 83.6 jit_solution(14170151611086625186)
XLA Ops:
  1.3 4.8 %stats.1 = (f32[56,768]{1,0:T(8,128)}, f32[48,768]{1,0:T(8,128)}) custom-call(s32[1]{0:T(128)} %bitcast.hand_ref, s32[8]{0:T(128)} %refs_0_.3, s32[4]{0:T(128)} %cards_now_ref.7, s32[2,8,1536]{2,1,0:T(8,128)} %constant.12.clone.refs_2_.card_ref, s32[12,663]{1,0:T(8,128)} %refs_5_.3, f32[12,64,663]{2,1,0:T(8,128)} %x_ref.3, f32[12,16,663]{2,1,0:T(8,128)} %v_ref.3, ...), custom_call_target="tpu_custom_call" | custom-call | flops 5000000000 | tf_op jit(solution)/shard_map/stats/pallas_call | solution.py:564
  6.7 2.7 %collective-permute-start = (f32[56,768]{1,0:T(8,128)}, f32[56,768]{1,0:T(8,128)S(1)}, u32[]{:S(2)}, u32[]{:S(2)}) collective-permute-start(f32[56,768]{1,0:T(8,128)} %get-tuple-element.92), channel_id=1, source_target_pairs={{0,2},{2,0},{4,6},{6,4},{8,10},{10,8},{12,14},{14,12},{1,3},{3,1},... | collective-permute-start | bytes 516104 | tf_op jit(solution)/shard_map/ppermute | solution.py:546
  9.4 1.6 %prepare.1 = (f32[12,1,1536]{2,1,0:T(1,128)S(1)}, bf16[12,1,768]{2,1,0:T(2,128)(2,1)S(1)}, f32[4,1536,3]{2,1,0:T(8,128)S(1)}, bf16[1536,768]{1,0:T(8,128)(2,1)S(...) custom-call(s32[1]{0:T(128)} %bitcast.hand_ref, ...), custom_call_target="tpu_custom_call" | custom-call | flops 2000000000 | tf_op jit(solution)/shard_map/prepare/pallas_call | solution.py:564
  11.1 2.4 %mover_gradient.8 = (f32[3,64,768]{2,1,0:T(8,128)S(1)}, f32[3,16,768]{2,1,0:T(8,128)S(1)}) custom-call(f32[12,64,663]{2,1,0:T(8,128)S(1)} %copy-done, f32[12,64,663]{2,1,0:T(8,128)S(1)} %collective-permute-done.1.far_ref, f32[12,16,663]{2,1,0:T(8,128)S(1)} %copy-done.1, f32[12,1,1536]{2,1,0:T(1,128)S(1)} %get-tuple-element.93.live_ref, ...), custom_call_target="tpu_custom_call" | custom-call | flops 3000000000 | tf_op jit(solution)/shard_map/mover_gradient/pallas_call | solution.py:564
  14.5 1.9 %collective-permute-start.4 = (f32[56,768]{1,0:T(8,128)S(1)}, f32[56,768]{1,0:T(8,128)S(1)}, u32[]{:S(2)}, u32[]{:S(2)}) collective-permute-start(f32[56,768]{1,0:T(8,128)S(1)} %add.18), channel_id=1, source_target_pairs={{0,4},{2,6},{4,0},{6,2},{8,12},{10,14},{12,8},{14,10},{1,5},{3,7},... | collective-permute-start | bytes 516104 | tf_op jit(solution)/shard_map/ppermute | solution.py:546
  16.3 2.4 %mover_gradient.9 = (f32[3,64,768]{2,1,0:T(8,128)S(1)}, f32[3,16,768]{2,1,0:T(8,128)S(1)}) custom-call(f32[12,64,663]{2,1,0:T(8,128)S(1)} %copy-done, f32[12,64,663]{2,1,0:T(8,128)S(1)} %collective-permute-done.1.far_ref, f32[12,16,663]{2,1,0:T(8,128)S(1)} %copy-done.1, f32[12,1,1536]{2,1,0:T(1,128)S(1)} %get-tuple-element.93.live_ref, ...), custom_call_target="tpu_custom_call" | custom-call | flops 3000000000 | tf_op jit(solution)/shard_map/mover_gradient/pallas_call | solution.py:564
  18.7 1.9 %collective-permute-done.4 = f32[56,768]{1,0:T(8,128)S(1)} collective-permute-done((f32[56,768]{1,0:T(8,128)S(1)}, f32[56,768]{1,0:T(8,128)S(1)}, u32[]{:S(2)}, u32[]{:S(2)}) %collective-permute-start.4) | collective-permute-done | bytes 172064 | tf_op jit(solution)/shard_map/ppermute | solution.py:546
  20.7 2.6 %collective-permute-start.5 = (f32[56,768]{1,0:T(8,128)S(1)}, f32[56,768]{1,0:T(8,128)S(1)}, u32[]{:S(2)}, u32[]{:S(2)}) collective-permute-start(f32[56,768]{1,0:T(8,128)S(1)} %add.19), channel_id=1, source_target_pairs={{0,8},{2,10},{4,12},{6,14},{8,0},{10,2},{12,4},{14,6},{1,9},{3,11}... | collective-permute-start | bytes 516104 | tf_op jit(solution)/shard_map/ppermute | solution.py:546
  23.3 2.4 %mover_gradient.11 = (f32[3,64,768]{2,1,0:T(8,128)S(1)}, f32[3,16,768]{2,1,0:T(8,128)S(1)}) custom-call(f32[12,64,663]{2,1,0:T(8,128)S(1)} %copy-done, f32[12,64,663]{2,1,0:T(8,128)S(1)} %collective-permute-done.1.far_ref, f32[12,16,663]{2,1,0:T(8,128)S(1)} %copy-done.1, f32[12,1,1536]{2,1,0:T(1,128)S(1)} %get-tuple-element.93.live_ref, ...), custom_call_target="tpu_custom_call" | custom-call | flops 3000000000 | tf_op jit(solution)/shard_map/mover_gradient/pallas_call | solution.py:564
  25.7 2.4 %mover_gradient.10 = (f32[3,64,768]{2,1,0:T(8,128)S(1)}, f32[3,16,768]{2,1,0:T(8,128)S(1)}) custom-call(f32[12,64,663]{2,1,0:T(8,128)S(1)} %copy-done, f32[12,64,663]{2,1,0:T(8,128)S(1)} %collective-permute-done.1.far_ref, f32[12,16,663]{2,1,0:T(8,128)S(1)} %copy-done.1, f32[12,1,1536]{2,1,0:T(1,128)S(1)} %get-tuple-element.93.live_ref, ...), custom_call_target="tpu_custom_call" | custom-call | flops 3000000000 | tf_op jit(solution)/shard_map/mover_gradient/pallas_call | solution.py:564
  34.2 1.7 %turn_step.2 = (f32[48,1536]{1,0:T(8,128)S(1)}, f32[32,1536]{1,0:T(8,128)S(1)}, f32[16,1536]{1,0:T(8,128)S(1)}, f32[8,768]{1,0:T(8,128)S(1)}, f32[8,128]{1,0:T(8,128)S(1)}) custom-call(s32[1]{0:T(128)} %bitcast.hand_ref, s32[4]{0:T(128)S(1)} %copy-done.14, s32[2,8,1536]{2,1,0:T(8,128)S(1)} %copy-done.19, bf16[2,1536,128]{2,1,0:T(8,128)(2,1)S(1)} %copy-done.16, ...), custom_call_target="tpu_custom_call" | custom-call | flops 2000000000 | tf_op jit(solution)/shard_map/turn_step/pallas_call | solution.py:564
  35.9 5.2 %rival_step.4 = (f32[6,64,768]{2,1,0:T(8,128)S(1)}, f32[6,16,768]{2,1,0:T(8,128)S(1)}, f32[40,768]{1,0:T(8,128)S(1)}) custom-call(f32[56,768]{1,0:T(8,128)S(1)} %add.20.rest_4_.own_norm_ref, f32[56,768]{1,0:T(8,128)S(1)} %collective-permute-done.6.rest_5_.far_norm_ref, f32[6,64,768]{2,1,0:T(8,128)S(1)} %get-tuple-element.126.bar_ref, ...), custom_call_target="tpu_custom_call" | custom-call | flops 6000000000 | tf_op jit(solution)/shard_map/rival_step/pallas_call | solution.py:564
  41.2 5.1 %rival_step.5 = (f32[6,64,768]{2,1,0:T(8,128)S(1)}, f32[6,16,768]{2,1,0:T(8,128)S(1)}, f32[40,768]{1,0:T(8,128)S(1)}) custom-call(f32[56,768]{1,0:T(8,128)S(1)} %add.20.rest_4_.own_norm_ref, f32[56,768]{1,0:T(8,128)S(1)} %collective-permute-done.6.rest_5_.far_norm_ref, f32[6,64,768]{2,1,0:T(8,128)S(1)} %get-tuple-element.123.bar_ref, ...), custom_call_target="tpu_custom_call" | custom-call | flops 6000000000 | tf_op jit(solution)/shard_map/rival_step/pallas_call | solution.py:564
  47.9 2.4 %mover_gradient.12 = (f32[3,64,768]{2,1,0:T(8,128)S(1)}, f32[3,16,768]{2,1,0:T(8,128)S(1)}) custom-call(f32[6,64,768]{2,1,0:T(8,128)S(1)} %get-tuple-element.132.y_ref, f32[6,64,768]{2,1,0:T(8,128)S(1)} %collective-permute-done.10.far_ref, f32[6,16,768]{2,1,0:T(8,128)S(1)} %get-tuple-element.133.u_ref, f32[12,1,1536]{2,1,0:T(1,128)S(1)} %get-tuple-element.93.live_ref, ...), custom_call_target="tpu_custom_call" | custom-call | flops 3000000000 | tf_op jit(solution)/shard_map/mover_gradient/pallas_call | solution.py:564
  50.3 1.8 %collective-permute-done.9 = f32[40,768]{1,0:T(8,128)S(1)} collective-permute-done((f32[40,768]{1,0:T(8,128)S(1)}, f32[40,768]{1,0:T(8,128)S(1)}, u32[]{:S(2)}, u32[]{:S(2)}) %collective-permute-start.9) | collective-permute-done | bytes 122912 | tf_op jit(solution)/shard_map/ppermute | solution.py:546
  52.5 2.3 %mover_gradient.13 = (f32[3,64,768]{2,1,0:T(8,128)S(1)}, f32[3,16,768]{2,1,0:T(8,128)S(1)}) custom-call(f32[6,64,768]{2,1,0:T(8,128)S(1)} %get-tuple-element.132.y_ref, f32[6,64,768]{2,1,0:T(8,128)S(1)} %collective-permute-done.10.far_ref, f32[6,16,768]{2,1,0:T(8,128)S(1)} %get-tuple-element.133.u_ref, f32[12,1,1536]{2,1,0:T(1,128)S(1)} %get-tuple-element.93.live_ref, ...), custom_call_target="tpu_custom_call" | custom-call | flops 3000000000 | tf_op jit(solution)/shard_map/mover_gradient/pallas_call | solution.py:564
  57.0 2.5 %collective-permute-start.12 = (f32[40,768]{1,0:T(8,128)S(1)}, f32[40,768]{1,0:T(8,128)S(1)}, u32[]{:S(2)}, u32[]{:S(2)}) collective-permute-start(f32[40,768]{1,0:T(8,128)S(1)} %add.22), channel_id=1, source_target_pairs={{0,8},{2,10},{4,12},{6,14},{8,0},{10,2},{12,4},{14,6},{1,9},{3,11}... | collective-permute-start | bytes 368648 | tf_op jit(solution)/shard_map/ppermute | solution.py:546
  59.5 2.4 %mover_gradient.15 = (f32[3,64,768]{2,1,0:T(8,128)S(1)}, f32[3,16,768]{2,1,0:T(8,128)S(1)}) custom-call(f32[6,64,768]{2,1,0:T(8,128)S(1)} %get-tuple-element.147.y_ref, f32[6,64,768]{2,1,0:T(8,128)S(1)} %collective-permute-done.13.far_ref, f32[6,16,768]{2,1,0:T(8,128)S(1)} %get-tuple-element.148.u_ref, f32[12,1,1536]{2,1,0:T(1,128)S(1)} %get-tuple-element.93.live_ref, ...), custom_call_target="tpu_custom_call" | custom-call | flops 3000000000 | tf_op jit(solution)/shard_map/mover_gradient/pallas_call | solution.py:564
  61.9 2.4 %mover_gradient.14 = (f32[3,64,768]{2,1,0:T(8,128)S(1)}, f32[3,16,768]{2,1,0:T(8,128)S(1)}) custom-call(f32[6,64,768]{2,1,0:T(8,128)S(1)} %get-tuple-element.147.y_ref, f32[6,64,768]{2,1,0:T(8,128)S(1)} %collective-permute-done.13.far_ref, f32[6,16,768]{2,1,0:T(8,128)S(1)} %get-tuple-element.148.u_ref, f32[12,1,1536]{2,1,0:T(1,128)S(1)} %get-tuple-element.93.live_ref, ...), custom_call_target="tpu_custom_call" | custom-call | flops 3000000000 | tf_op jit(solution)/shard_map/mover_gradient/pallas_call | solution.py:564
  66.1 1.6 %mover_step.6 = (f32[12,64,663]{2,1,0:T(8,128)}, f32[12,16,663]{2,1,0:T(8,128)}, f32[6,64,768]{2,1,0:T(8,128)S(1)}) custom-call(f32[40,768]{1,0:T(8,128)S(1)} %add.23.rest_7_.own_norm_ref, f32[40,768]{1,0:T(8,128)S(1)} %collective-permute-done.14.rest_8_.far_norm_ref, f32[6,64,768]{2,1,0:T(8,128)S(1)} %get-tuple-element.157.x_ref, ...), custom_call_target="tpu_custom_call" | custom-call | flops 2000000000 | tf_op jit(solution)/shard_map/mover_step/pallas_call | solution.py:564
  67.8 1.6 %mover_step.7 = (f32[12,64,663]{2,1,0:T(8,128)}, f32[12,16,663]{2,1,0:T(8,128)}, f32[6,64,768]{2,1,0:T(8,128)S(1)}) custom-call(f32[40,768]{1,0:T(8,128)S(1)} %add.23.rest_7_.own_norm_ref, f32[40,768]{1,0:T(8,128)S(1)} %collective-permute-done.14.rest_8_.far_norm_ref, ...), custom_call_target="tpu_custom_call", output_to_operand_aliasing={{0}: (9, {}), {1}: (10, {})} | custom-call | flops 2000000000 | tf_op jit(solution)/shard_map/mover_step/pallas_call | solution.py:564
  69.8 2.0 %turn_step.3 = (f32[16,1536]{1,0:T(8,128)S(1)}, f32[16,663]{1,0:T(8,128)}, f32[6,663]{1,0:T(8,128)}, f32[16,663]{1,0:T(8,128)}, f32[6,663]{1,0:T(8,128)}) custom-call(s32[1]{0:T(128)} %bitcast.hand_ref, s32[4]{0:T(128)S(1)} %copy-done.14, s32[2,8,1536]{2,1,0:T(8,128)S(1)} %copy-done.19, bf16[2,1536,128]{2,1,0:T(8,128)(2,1)S(1)} %copy-done.16, ...), custom_call_target="tpu_custom_call" | custom-call | flops 2000000000 | tf_op jit(solution)/shard_map/turn_step/pallas_call | solution.py:564
  71.8 6.0 %rival_step.6 = (f32[12,64,663]{2,1,0:T(8,128)}, f32[12,16,663]{2,1,0:T(8,128)}) custom-call(f32[40,768]{1,0:T(8,128)S(1)} %add.23.rest_7_.own_norm_ref, f32[40,768]{1,0:T(8,128)S(1)} %collective-permute-done.14.rest_8_.far_norm_ref, f32[6,64,768]{2,1,0:T(8,128)S(1)} %get-tuple-element.168.bar_ref, f32[6,64,768]{2,1,0:T(8,128)S(1)} %collective-permute-done.16.far_ref, ...), custom_call_target="tpu_custom_call" | custom-call | flops 6000000000 | tf_op jit(solution)/shard_map/rival_step/pallas_call | solution.py:564
  77.8 5.8 %rival_step.7 = (f32[12,64,663]{2,1,0:T(8,128)}, f32[12,16,663]{2,1,0:T(8,128)}) custom-call(f32[40,768]{1,0:T(8,128)S(1)} %add.23.rest_7_.own_norm_ref, f32[40,768]{1,0:T(8,128)S(1)} %collective-permute-done.14.rest_8_.far_norm_ref, f32[6,64,768]{2,1,0:T(8,128)S(1)} %get-tuple-element.166.bar_ref, ...), custom_call_target="tpu_custom_call", output_to_operand_aliasing={{0}: (20, {}), {1}: (21, {})} | custom-call | flops 6000000000 | tf_op jit(solution)/shard_map/rival_step/pallas_call | solution.py:564
  (80 shorter events, 15.0 us)
Async XLA Ops:
  0.6 10.4 %collective-permute-start.1 = (f32[12,64,663]{2,1,0:T(8,128)}, f32[12,64,663]{2,1,0:T(8,128)S(1)}, u32[]{:S(2)}, u32[]{:S(2)}) collective-permute-start(f32[12,64,663]{2,1,0:T(8,128)} %y_ref.11), channel_id=1, source_target_pairs={{0,1},{1,0},{2,3},{3,2},{4,5},{5,4},{6,7},{7,6},{8,9},{9,8},{10,11... | collective-permute-start | bytes 6110216 | tf_op jit(solution)/shard_map/ppermute | solution.py:543
  1.2 8.2 %collective-permute-start.2 = (s32[12,663]{1,0:T(8,128)}, s32[12,663]{1,0:T(8,128)S(1)}, u32[]{:S(2)}, u32[]{:S(2)}) collective-permute-start(s32[12,663]{1,0:T(8,128)} %refs_5_.3), channel_id=1, source_target_pairs={{0,1},{1,0},{2,3},{3,2},{4,5},{5,4},{6,7},{7,6},{8,9},{9,8},{10,11... | collective-permute-start | bytes 95480 | tf_op jit(solution)/shard_map/ppermute | solution.py:543
  1.2 8.1 %copy-start.8 = (f32[64,64]{1,0:T(8,128)S(1)}, f32[64,64]{1,0:T(8,128)}, u32[]{:S(2)}) copy-start(f32[64,64]{1,0:T(8,128)} %refs_9_.3) | copy-start | bytes 49156
  1.2 8.1 %copy-start.10 = (s32[16,64]{1,0:T(8,128)S(1)}, s32[16,64]{1,0:T(8,128)}, u32[]{:S(2)}) copy-start(s32[16,64]{1,0:T(8,128)} %children_ref.7) | copy-start | bytes 12292
  1.3 8.1 %copy-start.13 = (s32[8]{0:T(128)S(1)}, s32[8]{0:T(128)}, u32[]{:S(2)}) copy-start(s32[8]{0:T(128)} %refs_0_.3) | copy-start | bytes 100
  1.3 8.1 %copy-start.14 = (s32[4]{0:T(128)S(1)}, s32[4]{0:T(128)}, u32[]{:S(2)}) copy-start(s32[4]{0:T(128)} %cards_now_ref.7) | copy-start | bytes 52
  1.3 8.1 %copy-start.15 = (bf16[2,128,1536]{2,1,0:T(8,128)(2,1)S(1)}, bf16[2,128,1536]{2,1,0:T(8,128)(2,1)}, u32[]{:S(2)}) copy-start(bf16[2,128,1536]{2,1,0:T(8,128)(2,1)} %constant.14.clone.refs_4_.spread_ref) | copy-start | bytes 2359300
  1.3 8.1 %copy-start.16 = (bf16[2,1536,128]{2,1,0:T(8,128)(2,1)S(1)}, bf16[2,1536,128]{2,1,0:T(8,128)(2,1)}, u32[]{:S(2)}) copy-start(bf16[2,1536,128]{2,1,0:T(8,128)(2,1)} %constant.13.clone.refs_3_.gather_ref) | copy-start | bytes 2359300
  1.3 8.1 %copy-start.18 = (bf16[2,128,768]{2,1,0:T(8,128)(2,1)S(1)}, bf16[2,128,768]{2,1,0:T(8,128)(2,1)}, u32[]{:S(2)}) copy-start(bf16[2,128,768]{2,1,0:T(8,128)(2,1)} %constant.15.clone.refs_7_) | copy-start | bytes 1179652
  6.2 8.3 %collective-permute-start.3 = (f32[48,768]{1,0:T(8,128)}, f32[48,768]{1,0:T(8,128)S(1)}, u32[]{:S(2)}, u32[]{:S(2)}) collective-permute-start(f32[48,768]{1,0:T(8,128)} %get-tuple-element.107.pack_ref.rest_0_), channel_id=1, source_target_pairs={{0,1},{1,0},{2,3},{3,2},{4,5},{5,4},{6,7},{7,6},{8,9},{9,8},{10,11... | collective-permute-start | bytes 442376 | tf_op jit(solution)/shard_map/ppermute | solution.py:543
  6.7 7.8 %collective-permute-start = (f32[56,768]{1,0:T(8,128)}, f32[56,768]{1,0:T(8,128)S(1)}, u32[]{:S(2)}, u32[]{:S(2)}) collective-permute-start(f32[56,768]{1,0:T(8,128)} %get-tuple-element.92), channel_id=1, source_target_pairs={{0,2},{2,0},{4,6},{6,4},{8,10},{10,8},{12,14},{14,12},{1,3},{3,1},... | collective-permute-start | bytes 516104 | tf_op jit(solution)/shard_map/ppermute | solution.py:546
  14.5 6.2 %collective-permute-start.4 = (f32[56,768]{1,0:T(8,128)S(1)}, f32[56,768]{1,0:T(8,128)S(1)}, u32[]{:S(2)}, u32[]{:S(2)}) collective-permute-start(f32[56,768]{1,0:T(8,128)S(1)} %add.18), channel_id=1, source_target_pairs={{0,4},{2,6},{4,0},{6,2},{8,12},{10,14},{12,8},{14,10},{1,5},{3,7},... | collective-permute-start | bytes 516104 | tf_op jit(solution)/shard_map/ppermute | solution.py:546
  20.7 9.9 %collective-permute-start.5 = (f32[56,768]{1,0:T(8,128)S(1)}, f32[56,768]{1,0:T(8,128)S(1)}, u32[]{:S(2)}, u32[]{:S(2)}) collective-permute-start(f32[56,768]{1,0:T(8,128)S(1)} %add.19), channel_id=1, source_target_pairs={{0,8},{2,10},{4,12},{6,14},{8,0},{10,2},{12,4},{14,6},{1,9},{3,11}... | collective-permute-start | bytes 516104 | tf_op jit(solution)/shard_map/ppermute | solution.py:546
  30.5 1.5 %collective-permute-start.6 = (f32[56,768]{1,0:T(8,128)S(1)}, f32[56,768]{1,0:T(8,128)S(1)}, u32[]{:S(2)}, u32[]{:S(2)}) collective-permute-start(f32[56,768]{1,0:T(8,128)S(1)} %add.20.rest_4_.own_norm_ref), channel_id=1, source_target_pairs={{0,1},{1,0},{2,3},{3,2},{4,5},{5,4},{6,7},{7,6},{8,9},{9,8},{10,11... | collective-permute-start | bytes 516104 | tf_op jit(solution)/shard_map/ppermute | solution.py:543
  32.8 3.1 %collective-permute-start.8 = (f32[6,64,768]{2,1,0:T(8,128)S(1)}, f32[6,64,768]{2,1,0:T(8,128)S(1)}, u32[]{:S(2)}, u32[]{:S(2)}) collective-permute-start(f32[6,64,768]{2,1,0:T(8,128)S(1)} %get-tuple-element.126.bar_ref), channel_id=1, source_target_pairs={{0,1},{1,0},{2,3},{3,2},{4,5},{5,4},{6,7},{7,6},{8,9},{9,8},{10,11... | collective-permute-start | bytes 3538952 | tf_op jit(solution)/shard_map/ppermute | solution.py:543
  33.8 7.5 %collective-permute-start.7 = (f32[6,64,768]{2,1,0:T(8,128)S(1)}, f32[6,64,768]{2,1,0:T(8,128)S(1)}, u32[]{:S(2)}, u32[]{:S(2)}) collective-permute-start(f32[6,64,768]{2,1,0:T(8,128)S(1)} %get-tuple-element.123.bar_ref), channel_id=1, source_target_pairs={{0,1},{1,0},{2,3},{3,2},{4,5},{5,4},{6,7},{7,6},{8,9},{9,8},{10,11... | collective-permute-start | bytes 3538952 | tf_op jit(solution)/shard_map/ppermute | solution.py:543
  41.1 6.8 %collective-permute-start.10 = (f32[6,64,768]{2,1,0:T(8,128)S(1)}, f32[6,64,768]{2,1,0:T(8,128)S(1)}, u32[]{:S(2)}, u32[]{:S(2)}) collective-permute-start(f32[6,64,768]{2,1,0:T(8,128)S(1)} %get-tuple-element.132.y_ref), channel_id=1, source_target_pairs={{0,1},{1,0},{2,3},{3,2},{4,5},{5,4},{6,7},{7,6},{8,9},{9,8},{10,11... | collective-permute-start | bytes 3538952 | tf_op jit(solution)/shard_map/ppermute | solution.py:543
  46.3 13.2 %collective-permute-start.13 = (f32[6,64,768]{2,1,0:T(8,128)S(1)}, f32[6,64,768]{2,1,0:T(8,128)S(1)}, u32[]{:S(2)}, u32[]{:S(2)}) collective-permute-start(f32[6,64,768]{2,1,0:T(8,128)S(1)} %get-tuple-element.147.y_ref), channel_id=1, source_target_pairs={{0,1},{1,0},{2,3},{3,2},{4,5},{5,4},{6,7},{7,6},{8,9},{9,8},{10,11... | collective-permute-start | bytes 3538952 | tf_op jit(solution)/shard_map/ppermute | solution.py:543
  46.7 5.4 %collective-permute-start.9 = (f32[40,768]{1,0:T(8,128)S(1)}, f32[40,768]{1,0:T(8,128)S(1)}, u32[]{:S(2)}, u32[]{:S(2)}) collective-permute-start(f32[40,768]{1,0:T(8,128)S(1)} %get-tuple-element.131), channel_id=1, source_target_pairs={{0,2},{2,0},{4,6},{6,4},{8,10},{10,8},{12,14},{14,12},{1,3},{3,1},... | collective-permute-start | bytes 368648 | tf_op jit(solution)/shard_map/ppermute | solution.py:546
  52.1 4.9 %collective-permute-start.11 = (f32[40,768]{1,0:T(8,128)S(1)}, f32[40,768]{1,0:T(8,128)S(1)}, u32[]{:S(2)}, u32[]{:S(2)}) collective-permute-start(f32[40,768]{1,0:T(8,128)S(1)} %add.21), channel_id=1, source_target_pairs={{0,4},{2,6},{4,0},{6,2},{8,12},{10,14},{12,8},{14,10},{1,5},{3,7},... | collective-permute-start | bytes 368648 | tf_op jit(solution)/shard_map/ppermute | solution.py:546
  57.0 7.6 %collective-permute-start.12 = (f32[40,768]{1,0:T(8,128)S(1)}, f32[40,768]{1,0:T(8,128)S(1)}, u32[]{:S(2)}, u32[]{:S(2)}) collective-permute-start(f32[40,768]{1,0:T(8,128)S(1)} %add.22), channel_id=1, source_target_pairs={{0,8},{2,10},{4,12},{6,14},{8,0},{10,2},{12,4},{14,6},{1,9},{3,11}... | collective-permute-start | bytes 368648 | tf_op jit(solution)/shard_map/ppermute | solution.py:546
  64.7 1.4 %collective-permute-start.14 = (f32[40,768]{1,0:T(8,128)S(1)}, f32[40,768]{1,0:T(8,128)S(1)}, u32[]{:S(2)}, u32[]{:S(2)}) collective-permute-start(f32[40,768]{1,0:T(8,128)S(1)} %add.23.rest_7_.own_norm_ref), channel_id=1, source_target_pairs={{0,1},{1,0},{2,3},{3,2},{4,5},{5,4},{6,7},{7,6},{8,9},{9,8},{10,11... | collective-permute-start | bytes 368648 | tf_op jit(solution)/shard_map/ppermute | solution.py:543
  67.7 4.1 %collective-permute-start.16 = (f32[6,64,768]{2,1,0:T(8,128)S(1)}, f32[6,64,768]{2,1,0:T(8,128)S(1)}, u32[]{:S(2)}, u32[]{:S(2)}) collective-permute-start(f32[6,64,768]{2,1,0:T(8,128)S(1)} %get-tuple-element.168.bar_ref), channel_id=1, source_target_pairs={{0,1},{1,0},{2,3},{3,2},{4,5},{5,4},{6,7},{7,6},{8,9},{9,8},{10,11... | collective-permute-start | bytes 3538952 | tf_op jit(solution)/shard_map/ppermute | solution.py:543
  69.4 8.4 %collective-permute-start.15 = (f32[6,64,768]{2,1,0:T(8,128)S(1)}, f32[6,64,768]{2,1,0:T(8,128)S(1)}, u32[]{:S(2)}, u32[]{:S(2)}) collective-permute-start(f32[6,64,768]{2,1,0:T(8,128)S(1)} %get-tuple-element.166.bar_ref), channel_id=1, source_target_pairs={{0,1},{1,0},{2,3},{3,2},{4,5},{5,4},{6,7},{7,6},{8,9},{9,8},{10,11... | collective-permute-start | bytes 3538952 | tf_op jit(solution)/shard_map/ppermute | solution.py:543
  (14 other events, 66.0 us)

commit v2 on v1

--- a/solution.py
+++ b/solution.py
@@ -99,8 +99,14 @@
     return jnp.sum(value, axis=0, keepdims=True)
 
 
-def steps_from(own_norms, far_norms, count):
-    totals = jnp.sum(own_norms + far_norms, axis=1, keepdims=True)
+def add_squares(sums_ref, row, squares):
+    last = sums_ref.shape[1] - 1
+    sums_ref[row:row + 1, last:] += jnp.sum(squares, axis=1, keepdims=True)
+
+
+def steps_from(own_ref, far_ref, count):
+    last = own_ref.shape[1] - 1
+    totals = own_ref[0:2, last:] + far_ref[0:2, last:]
     weight = jnp.sqrt((totals[1:2] / count + EPSILON) / (totals[0:1] / count + EPSILON))
     return STEP_SCALE / weight, STEP_SCALE * weight
 
@@ -121,7 +127,6 @@
     at = pl.program_id(0)
     padded = live_scratch.shape[2]
     prices = v_ref.shape[1]
-    nx, ny = 3 * prices, 3 * prices + 1
     river_here = lax.axis_index(river_axis)
 
     @pl.when(at == 0)
@@ -137,11 +142,11 @@
         pack_ref[...] = jnp.zeros_like(pack_ref)
         first = jnp.where(river_here == 0, 1.0, 0.0)
         base = 0
-        for rows, row in ((xt_ref, nx), (yt_ref, ny), (vt_ref, nx), (ut_ref, ny)):
+        for rows, row in ((xt_ref, 0), (yt_ref, 1), (vt_ref, 0), (ut_ref, 1)):
             value = jnp.where(turn > 0, rows[...], 0.0)
             pack_ref[base:base + value.shape[0]] = value
             base += round_up(value.shape[0], 8)
-            sums_ref[row:row + 1] += first * row_sums(value * value)
+            add_squares(sums_ref, row, first * row_sums(value * value))
 
     mover = jnp.zeros((1, padded), F32)
     rival = jnp.zeros((1, padded), F32)
@@ -156,8 +161,8 @@
         sums_ref[0:prices] += u
         sums_ref[prices:2 * prices] += v
         plan_scratch[...] += y
-    sums_ref[nx:nx + 1] += mover
-    sums_ref[ny:ny + 1] += rival
+    add_squares(sums_ref, 0, mover)
+    add_squares(sums_ref, 1, rival)
 
     @pl.when(at == pl.num_programs(0) - 1)
     def _():
@@ -302,7 +307,7 @@
         flow_ref[inner] = lives[inner] * (flow - turn_flow)
 
 
-def mover_step_kernel(group, start, bases, count, norm_row, parts, last, own_norm_ref, far_norm_ref, x_ref, v_ref, live_ref,
+def mover_step_kernel(group, start, bases, count, parts, last, own_norm_ref, far_norm_ref, x_ref, v_ref, live_ref,
                       *rest):
     grads, flows = rest[:parts], rest[parts:2 * parts]
     if last:
@@ -311,7 +316,7 @@
         new_x_ref, new_v_ref, bar_ref, total_ref = rest[-4:]
         total_ref[...] = rest[2 * parts][...] if start else jnp.zeros_like(total_ref)
     padded = bar_ref.shape[2]
-    primal, _ = steps_from(own_norm_ref[norm_row:norm_row + 8], far_norm_ref[norm_row:norm_row + 8], count)
+    primal, _ = steps_from(own_norm_ref, far_norm_ref, count)
 
     def work(part):
         for inner in range(group):
@@ -335,7 +340,7 @@
             work(part)
 
 
-def rival_step_kernel(group, start, bases, count, norm_row, parts, last, own_norm_ref, far_norm_ref, bar_ref, far_ref, y_ref,
+def rival_step_kernel(group, start, bases, count, parts, last, own_norm_ref, far_norm_ref, bar_ref, far_ref, y_ref,
                       u_ref, new_v_ref, live_ref, row_ref, col_ref, compat_ref, near_ref, main_ref, folds_ref, back_ref,
                       bart_ref, children_ref, parents_ref, *rest):
     flows = rest[:parts]
@@ -347,11 +352,9 @@
         new_y_ref, new_u_ref, total_ref, link_scratch, flow_scratch, step_scratch, plan_scratch = rest[-7:]
     padded = live_ref.shape[2] // 2
     infosets = u_ref.shape[1]
-    nx, ny = 2 * infosets, 2 * infosets + 1
-
     @pl.when(at == 0)
     def _():
-        primal, dual = steps_from(own_norm_ref[norm_row:norm_row + 8], far_norm_ref[norm_row:norm_row + 8], count)
+        primal, dual = steps_from(own_norm_ref, far_norm_ref, count)
         step_scratch[0:1, :] = jnp.broadcast_to(primal, (1, LANES))
         step_scratch[1:2, :] = jnp.broadcast_to(dual, (1, LANES))
         link_scratch[...] = exact_left(river_link(parents_ref, bar_ref.shape[1]), bart_ref[:, :padded])
@@ -361,7 +364,8 @@
                 total_ref[...] = rest[0][...]
             else:
                 total_ref[...] = jnp.zeros_like(total_ref)
-                total_ref[nx:ny + 1] = rest[0][0:2] + rest[1][0:2]
+                for row in range(2):
+                    add_squares(total_ref, row, rest[0][row:row + 1] + rest[1][row:row + 1])
 
     for part in range(parts):
         @pl.when(at == part)
@@ -377,6 +381,7 @@
         prices.append(pick(new_v_ref, bases[4], at, inner, group) + primal * flow_scratch[inner])
     done = group_payoffs(group, start, 1, at, own_plans, far_plans, prices, live_ref, row_ref, col_ref, compat_ref, near_ref,
                          main_ref, folds_ref, back_ref)
+    squares = jnp.zeros((1, padded), F32)
     for inner, (gradient, flow) in enumerate(done):
         live = live_ref[start + at * group + inner][:, :padded]
         y = jnp.where(live > 0, pick(y_ref, bases[2], at, inner, group), 0.0)
@@ -390,9 +395,11 @@
         if not last:
             plan_scratch[...] += new_y
             total_ref[0:infosets] += flow
-            total_ref[ny:ny + 1] += row_sums(new_y * new_y) + row_sums(new_u * new_u)
+            squares = squares + row_sums(new_y * new_y) + row_sums(new_u * new_u)
 
     if not last:
+        add_squares(total_ref, 1, squares)
+
         @pl.when(at == pl.num_programs(0) - 1)
         def _():
             step, _ = river_steps(children_ref, parents_ref)
@@ -454,9 +461,8 @@
     points = turn_step.shape[0]
     starts = turn_places(sequences, points)
     infosets = link_turned.shape[1]
-    norm_row = (3 if first else 2) * infosets
-    primal, dual = steps_from(sums_ref[norm_row:norm_row + 8], sums_far_ref[norm_row:norm_row + 8], count)
-    sums = jnp.concatenate([sums_ref[:norm_row], sums_far_ref[:norm_row]], axis=1)
+    primal, dual = steps_from(sums_ref, sums_far_ref, count)
+    sums = jnp.concatenate([sums_ref[...], sums_far_ref[...]], axis=1)
     pack = pack_ref[...]
     if first:
         price_sum = sums[:infosets]
@@ -533,8 +539,8 @@
     cards, gather, spread, near = (jnp.asarray(table) for table in halves(width, padded))
     hand = lax.axis_index("hand").astype(jnp.int32).reshape(1)
     pack_rows = 2 * (turn_sequences + round_up(points, 8))
-    stat_rows = 3 * infosets + 8
-    total_rows = 2 * infosets + 8
+    stat_rows = 3 * infosets
+    total_rows = 2 * infosets
 
     def shape(*dims, dtype=F32):
         return jax.ShapeDtypeStruct(dims, dtype)
@@ -643,7 +649,7 @@
                     value, early = lax.optimization_barrier((value, early))
         return [item[0] for item in out], [item[1] for item in out], (value, swap(value)), extra
 
-    def mover_steps(last, norms, norm_row, x, v, grad, flow):
+    def mover_steps(last, norms, x, v, grad, flow):
         outs = []
         for first in range(0, slots, span):
             arrays, specs, bases = zip(*(operand(item, first, span) for item in (x, v)))
@@ -665,13 +671,13 @@
                 if first:
                     in_specs += [vmem]
                     args += (outs[-1][3],)
-            outs.append(call(functools.partial(mover_step_kernel, group, first, bases, count, norm_row, parts, last),
+            outs.append(call(functools.partial(mover_step_kernel, group, first, bases, count, parts, last),
                              "mover_step", 0, (parts if last else 1,), in_specs, out_specs, out_shape, [], args, parts, aliases))
         if last:
             return outs[-1][0], outs[-1][1], [item[2] for item in outs]
         return [item[0] for item in outs], [item[1] for item in outs], [item[2] for item in outs], outs[-1][3]
 
-    def rival_steps(last, norms, norm_row, bar, bar_far, y, u, new_v, flow, bar_turn, parts_before):
+    def rival_steps(last, norms, bar, bar_far, y, u, new_v, flow, bar_turn, parts_before):
         outs = []
         for first in range(0, slots, span):
             arrays, specs, bases = zip(*(operand(item, first, group) for item in (bar, bar_far, y, u, new_v)))
@@ -694,7 +700,7 @@
                 before = (outs[-1][2],) if first else tuple(parts_before)
                 in_specs += [vmem] * len(before)
                 args += before
-            outs.append(call(functools.partial(rival_step_kernel, group, first, bases, count, norm_row, parts, last),
+            outs.append(call(functools.partial(rival_step_kernel, group, first, bases, count, parts, last),
                              "rival_step", 0, (parts,), in_specs, out_specs, out_shape, scratch, args, span, aliases))
         if last:
             return outs[-1]
@@ -730,10 +736,10 @@
         return turn_start(True, (near_now, far))
 
     grad, flow, norms, starts = gradients(sums, swap(pack), rival_river, rival_far, rival_river_price, pack, first_start, 2)
-    x, v, bar, part = mover_steps(False, norms, 3 * infosets, mover_river, mover_river_price, grad, flow)
+    x, v, bar, part = mover_steps(False, norms, mover_river, mover_river_price, grad, flow)
     bar_far = [swap(item) for item in bar]
     pack, kept, bar_turn, turn_norms, turn_steps = turn_call(True, (starts[3], *starts[:3], *norms))
-    y, u, total = rival_steps(False, norms, 3 * infosets, bar, bar_far, rival_river, rival_river_price, v, flow, bar_turn,
+    y, u, total = rival_steps(False, norms, bar, bar_far, rival_river, rival_river_price, v, flow, bar_turn,
                               (part, turn_norms))
     y_far = [swap(item) for item in y]
 
@@ -742,10 +748,10 @@
         return turn_start(False, (now, bar_turn))
 
     grad, flow, norms, starts = gradients(total, y_far[0], y, y_far, u, pack, second_start, 1)
-    next_x, next_v, bar = mover_steps(True, norms, 2 * infosets, x, v, grad, flow)
+    next_x, next_v, bar = mover_steps(True, norms, x, v, grad, flow)
     bar_far = [swap(item) for item in bar]
     bar_turn, next_xt, next_vt, next_yt, next_ut = turn_call(False, (pack, *starts, kept, turn_steps, *norms))
-    next_y, next_u = rival_steps(True, norms, 2 * infosets, bar, bar_far, y, u, next_v, flow, bar_turn, None)
+    next_y, next_u = rival_steps(True, norms, bar, bar_far, y, u, next_v, flow, bar_turn, None)
     return (next_xt, next_x, next_vt, next_v, next_yt, next_y, next_ut, next_u)
 
 

time: 83.7 us -> 81.5 us (0.974)
  waiting for transfers between devices: 10.2 us -> 8.45 us
    ppermute x6, waiting for transfers between devices: 7.42 us -> 5.78 us  [hop_total(): lax.ppermute(value, 'river', [(at, at ^ hop) for at in range(river_count)])]
  transfers between devices with their start and end apart: 17 -> 17, of which waited for: 8 -> 7; matrix products, arithmetic and copies ran while one was open for 0% -> 0% of each run, Pallas kernels for 60% -> 61%
where the time goes in v2:
time: 81.5 us; the launch traced here: 81.3 us
  Pallas kernels  58 us (71%)
  starting transfers between devices  13.6 us (17%)
  waiting for transfers between devices  8.45 us (10%)
  between operations  1.06 us (1%)
    pallas_call x22, Pallas kernels, call(): pl.pallas_call(kernel, grid_spec=pltpu.PrefetchScalarGridSpec(num_scalar_...  58 us
    ppermute x6, starting transfers between devices, hop_total(): lax.ppermute(value, 'river', [(at, at ^ hop) for at in range(river_count)])  11.1 us
    ppermute x6, waiting for transfers between devices, hop_total(): lax.ppermute(value, 'river', [(at, at ^ hop) for at in range(river_count)])  5.78 us
    ppermute x11, waiting for transfers between devices, swap(): return lax.ppermute(value, 'hand', [(0, 1), (1, 0)])  2.67 us
    ppermute x11, starting transfers between devices, swap(): return lax.ppermute(value, 'hand', [(0, 1), (1, 0)])  2.47 us
  transfers between devices with their start and end apart: 17, of which 7 were waited for; matrix products, arithmetic and copies ran while one was open for 0% of the time, Pallas kernels for 61%

profile of v2, /device:TPU:0, one launch (start us, length us, event | category | flops | bytes accessed | tf_op | source)
XLA Modules:
  0.0 81.3 jit_solution(3780522899996623306)
XLA Ops:
  1.3 4.8 %stats.1 = (f32[48,768]{1,0:T(8,128)}, f32[48,768]{1,0:T(8,128)}) custom-call(s32[1]{0:T(128)} %bitcast.hand_ref, s32[8]{0:T(128)} %refs_0_.3, s32[4]{0:T(128)} %cards_now_ref.7, s32[2,8,1536]{2,1,0:T(8,128)} %constant.12.clone.refs_2_.card_ref, s32[12,663]{1,0:T(8,128)} %refs_5_.3, f32[12,64,663]{2,1,0:T(8,128)} %x_ref.3, f32[12,16,663]{2,1,0:T(8,128)} %v_ref.3, ...), custom_call_target="tpu_custom_call" | custom-call | flops 5000000000 | tf_op jit(solution)/shard_map/stats/pallas_call | solution.py:570
  6.2 3.0 %collective-permute-start = (f32[48,768]{1,0:T(8,128)}, f32[48,768]{1,0:T(8,128)S(1)}, u32[]{:S(2)}, u32[]{:S(2)}) collective-permute-start(f32[48,768]{1,0:T(8,128)} %get-tuple-element.92), channel_id=1, source_target_pairs={{0,2},{2,0},{4,6},{6,4},{8,10},{10,8},{12,14},{14,12},{1,3},{3,1},... | collective-permute-start | bytes 442376 | tf_op jit(solution)/shard_map/ppermute | solution.py:552
  9.3 1.6 %prepare.1 = (f32[12,1,1536]{2,1,0:T(1,128)S(1)}, bf16[12,1,768]{2,1,0:T(2,128)(2,1)S(1)}, f32[4,1536,3]{2,1,0:T(8,128)S(1)}, bf16[1536,768]{1,0:T(8,128)(2,1)S(...) custom-call(s32[1]{0:T(128)} %bitcast.hand_ref, ...), custom_call_target="tpu_custom_call" | custom-call | flops 2000000000 | tf_op jit(solution)/shard_map/prepare/pallas_call | solution.py:570
  11.0 2.4 %mover_gradient.8 = (f32[3,64,768]{2,1,0:T(8,128)S(1)}, f32[3,16,768]{2,1,0:T(8,128)S(1)}) custom-call(f32[12,64,663]{2,1,0:T(8,128)S(1)} %copy-done, f32[12,64,663]{2,1,0:T(8,128)S(1)} %collective-permute-done.1.far_ref, f32[12,16,663]{2,1,0:T(8,128)S(1)} %copy-done.1, f32[12,1,1536]{2,1,0:T(1,128)S(1)} %get-tuple-element.93.live_ref, ...), custom_call_target="tpu_custom_call" | custom-call | flops 3000000000 | tf_op jit(solution)/shard_map/mover_gradient/pallas_call | solution.py:570
  13.5 1.9 %collective-permute-start.4 = (f32[48,768]{1,0:T(8,128)S(1)}, f32[48,768]{1,0:T(8,128)S(1)}, u32[]{:S(2)}, u32[]{:S(2)}) collective-permute-start(f32[48,768]{1,0:T(8,128)S(1)} %add.18), channel_id=1, source_target_pairs={{0,4},{2,6},{4,0},{6,2},{8,12},{10,14},{12,8},{14,10},{1,5},{3,7},... | collective-permute-start | bytes 442376 | tf_op jit(solution)/shard_map/ppermute | solution.py:552
  15.3 2.3 %mover_gradient.9 = (f32[3,64,768]{2,1,0:T(8,128)S(1)}, f32[3,16,768]{2,1,0:T(8,128)S(1)}) custom-call(f32[12,64,663]{2,1,0:T(8,128)S(1)} %copy-done, f32[12,64,663]{2,1,0:T(8,128)S(1)} %collective-permute-done.1.far_ref, f32[12,16,663]{2,1,0:T(8,128)S(1)} %copy-done.1, f32[12,1,1536]{2,1,0:T(1,128)S(1)} %get-tuple-element.93.live_ref, ...), custom_call_target="tpu_custom_call" | custom-call | flops 3000000000 | tf_op jit(solution)/shard_map/mover_gradient/pallas_call | solution.py:570
  17.7 2.0 %collective-permute-done.4 = f32[48,768]{1,0:T(8,128)S(1)} collective-permute-done((f32[48,768]{1,0:T(8,128)S(1)}, f32[48,768]{1,0:T(8,128)S(1)}, u32[]{:S(2)}, u32[]{:S(2)}) %collective-permute-start.4) | collective-permute-done | bytes 147488 | tf_op jit(solution)/shard_map/ppermute | solution.py:552
  19.7 2.6 %collective-permute-start.5 = (f32[48,768]{1,0:T(8,128)S(1)}, f32[48,768]{1,0:T(8,128)S(1)}, u32[]{:S(2)}, u32[]{:S(2)}) collective-permute-start(f32[48,768]{1,0:T(8,128)S(1)} %add.19), channel_id=1, source_target_pairs={{0,8},{2,10},{4,12},{6,14},{8,0},{10,2},{12,4},{14,6},{1,9},{3,11}... | collective-permute-start | bytes 442376 | tf_op jit(solution)/shard_map/ppermute | solution.py:552
  22.3 2.4 %mover_gradient.11 = (f32[3,64,768]{2,1,0:T(8,128)S(1)}, f32[3,16,768]{2,1,0:T(8,128)S(1)}) custom-call(f32[12,64,663]{2,1,0:T(8,128)S(1)} %copy-done, f32[12,64,663]{2,1,0:T(8,128)S(1)} %collective-permute-done.1.far_ref, f32[12,16,663]{2,1,0:T(8,128)S(1)} %copy-done.1, f32[12,1,1536]{2,1,0:T(1,128)S(1)} %get-tuple-element.93.live_ref, ...), custom_call_target="tpu_custom_call" | custom-call | flops 3000000000 | tf_op jit(solution)/shard_map/mover_gradient/pallas_call | solution.py:570
  24.7 2.4 %mover_gradient.10 = (f32[3,64,768]{2,1,0:T(8,128)S(1)}, f32[3,16,768]{2,1,0:T(8,128)S(1)}) custom-call(f32[12,64,663]{2,1,0:T(8,128)S(1)} %copy-done, f32[12,64,663]{2,1,0:T(8,128)S(1)} %collective-permute-done.1.far_ref, f32[12,16,663]{2,1,0:T(8,128)S(1)} %copy-done.1, f32[12,1,1536]{2,1,0:T(1,128)S(1)} %get-tuple-element.93.live_ref, ...), custom_call_target="tpu_custom_call" | custom-call | flops 3000000000 | tf_op jit(solution)/shard_map/mover_gradient/pallas_call | solution.py:570
  32.8 1.7 %turn_step.2 = (f32[48,1536]{1,0:T(8,128)S(1)}, f32[32,1536]{1,0:T(8,128)S(1)}, f32[16,1536]{1,0:T(8,128)S(1)}, f32[8,768]{1,0:T(8,128)S(1)}, f32[8,128]{1,0:T(8,128)S(1)}) custom-call(s32[1]{0:T(128)} %bitcast.hand_ref, s32[4]{0:T(128)S(1)} %copy-done.14, s32[2,8,1536]{2,1,0:T(8,128)S(1)} %copy-done.19, bf16[2,1536,128]{2,1,0:T(8,128)(2,1)S(1)} %copy-done.16, ...), custom_call_target="tpu_custom_call" | custom-call | flops 2000000000 | tf_op jit(solution)/shard_map/turn_step/pallas_call | solution.py:570
  34.4 5.2 %rival_step.4 = (f32[6,64,768]{2,1,0:T(8,128)S(1)}, f32[6,16,768]{2,1,0:T(8,128)S(1)}, f32[32,768]{1,0:T(8,128)S(1)}) custom-call(f32[48,768]{1,0:T(8,128)S(1)} %add.20.rest_4_.own_norm_ref, f32[48,768]{1,0:T(8,128)S(1)} %collective-permute-done.6.rest_5_.far_norm_ref, f32[6,64,768]{2,1,0:T(8,128)S(1)} %get-tuple-element.126.bar_ref, ...), custom_call_target="tpu_custom_call" | custom-call | flops 6000000000 | tf_op jit(solution)/shard_map/rival_step/pallas_call | solution.py:570
  39.9 5.2 %rival_step.5 = (f32[6,64,768]{2,1,0:T(8,128)S(1)}, f32[6,16,768]{2,1,0:T(8,128)S(1)}, f32[32,768]{1,0:T(8,128)S(1)}) custom-call(f32[48,768]{1,0:T(8,128)S(1)} %add.20.rest_4_.own_norm_ref, f32[48,768]{1,0:T(8,128)S(1)} %collective-permute-done.6.rest_5_.far_norm_ref, f32[6,64,768]{2,1,0:T(8,128)S(1)} %get-tuple-element.123.bar_ref, ...), custom_call_target="tpu_custom_call" | custom-call | flops 6000000000 | tf_op jit(solution)/shard_map/rival_step/pallas_call | solution.py:570
  45.4 2.4 %mover_gradient.12 = (f32[3,64,768]{2,1,0:T(8,128)S(1)}, f32[3,16,768]{2,1,0:T(8,128)S(1)}) custom-call(f32[6,64,768]{2,1,0:T(8,128)S(1)} %get-tuple-element.132.y_ref, f32[6,64,768]{2,1,0:T(8,128)S(1)} %collective-permute-done.10.far_ref, f32[6,16,768]{2,1,0:T(8,128)S(1)} %get-tuple-element.133.u_ref, f32[12,1,1536]{2,1,0:T(1,128)S(1)} %get-tuple-element.93.live_ref, ...), custom_call_target="tpu_custom_call" | custom-call | flops 3000000000 | tf_op jit(solution)/shard_map/mover_gradient/pallas_call | solution.py:570
  47.8 2.5 %collective-permute-done.9 = f32[32,768]{1,0:T(8,128)S(1)} collective-permute-done((f32[32,768]{1,0:T(8,128)S(1)}, f32[32,768]{1,0:T(8,128)S(1)}, u32[]{:S(2)}, u32[]{:S(2)}) %collective-permute-start.9) | collective-permute-done | bytes 98336 | tf_op jit(solution)/shard_map/ppermute | solution.py:552
  51.1 2.3 %mover_gradient.13 = (f32[3,64,768]{2,1,0:T(8,128)S(1)}, f32[3,16,768]{2,1,0:T(8,128)S(1)}) custom-call(f32[6,64,768]{2,1,0:T(8,128)S(1)} %get-tuple-element.132.y_ref, f32[6,64,768]{2,1,0:T(8,128)S(1)} %collective-permute-done.10.far_ref, f32[6,16,768]{2,1,0:T(8,128)S(1)} %get-tuple-element.133.u_ref, f32[12,1,1536]{2,1,0:T(1,128)S(1)} %get-tuple-element.93.live_ref, ...), custom_call_target="tpu_custom_call" | custom-call | flops 3000000000 | tf_op jit(solution)/shard_map/mover_gradient/pallas_call | solution.py:570
  55.0 2.8 %collective-permute-start.12 = (f32[32,768]{1,0:T(8,128)S(1)}, f32[32,768]{1,0:T(8,128)S(1)}, u32[]{:S(2)}, u32[]{:S(2)}) collective-permute-start(f32[32,768]{1,0:T(8,128)S(1)} %add.22), channel_id=1, source_target_pairs={{0,8},{2,10},{4,12},{6,14},{8,0},{10,2},{12,4},{14,6},{1,9},{3,11}... | collective-permute-start | bytes 294920 | tf_op jit(solution)/shard_map/ppermute | solution.py:552
  57.8 2.4 %mover_gradient.15 = (f32[3,64,768]{2,1,0:T(8,128)S(1)}, f32[3,16,768]{2,1,0:T(8,128)S(1)}) custom-call(f32[6,64,768]{2,1,0:T(8,128)S(1)} %get-tuple-element.147.y_ref, f32[6,64,768]{2,1,0:T(8,128)S(1)} %collective-permute-done.13.far_ref, f32[6,16,768]{2,1,0:T(8,128)S(1)} %get-tuple-element.148.u_ref, f32[12,1,1536]{2,1,0:T(1,128)S(1)} %get-tuple-element.93.live_ref, ...), custom_call_target="tpu_custom_call" | custom-call | flops 3000000000 | tf_op jit(solution)/shard_map/mover_gradient/pallas_call | solution.py:570
  60.2 2.4 %mover_gradient.14 = (f32[3,64,768]{2,1,0:T(8,128)S(1)}, f32[3,16,768]{2,1,0:T(8,128)S(1)}) custom-call(f32[6,64,768]{2,1,0:T(8,128)S(1)} %get-tuple-element.147.y_ref, f32[6,64,768]{2,1,0:T(8,128)S(1)} %collective-permute-done.13.far_ref, f32[6,16,768]{2,1,0:T(8,128)S(1)} %get-tuple-element.148.u_ref, f32[12,1,1536]{2,1,0:T(1,128)S(1)} %get-tuple-element.93.live_ref, ...), custom_call_target="tpu_custom_call" | custom-call | flops 3000000000 | tf_op jit(solution)/shard_map/mover_gradient/pallas_call | solution.py:570
  63.9 1.5 %mover_step.6 = (f32[12,64,663]{2,1,0:T(8,128)}, f32[12,16,663]{2,1,0:T(8,128)}, f32[6,64,768]{2,1,0:T(8,128)S(1)}) custom-call(f32[32,768]{1,0:T(8,128)S(1)} %add.23.rest_7_.own_norm_ref, f32[32,768]{1,0:T(8,128)S(1)} %collective-permute-done.14.rest_8_.far_norm_ref, f32[6,64,768]{2,1,0:T(8,128)S(1)} %get-tuple-element.157.x_ref, ...), custom_call_target="tpu_custom_call" | custom-call | flops 2000000000 | tf_op jit(solution)/shard_map/mover_step/pallas_call | solution.py:570
  65.6 1.5 %mover_step.7 = (f32[12,64,663]{2,1,0:T(8,128)}, f32[12,16,663]{2,1,0:T(8,128)}, f32[6,64,768]{2,1,0:T(8,128)S(1)}) custom-call(f32[32,768]{1,0:T(8,128)S(1)} %add.23.rest_7_.own_norm_ref, f32[32,768]{1,0:T(8,128)S(1)} %collective-permute-done.14.rest_8_.far_norm_ref, ...), custom_call_target="tpu_custom_call", output_to_operand_aliasing={{0}: (9, {}), {1}: (10, {})} | custom-call | flops 2000000000 | tf_op jit(solution)/shard_map/mover_step/pallas_call | solution.py:570
  67.5 2.0 %turn_step.3 = (f32[16,1536]{1,0:T(8,128)S(1)}, f32[16,663]{1,0:T(8,128)}, f32[6,663]{1,0:T(8,128)}, f32[16,663]{1,0:T(8,128)}, f32[6,663]{1,0:T(8,128)}) custom-call(s32[1]{0:T(128)} %bitcast.hand_ref, s32[4]{0:T(128)S(1)} %copy-done.14, s32[2,8,1536]{2,1,0:T(8,128)S(1)} %copy-done.19, bf16[2,1536,128]{2,1,0:T(8,128)(2,1)S(1)} %copy-done.16, ...), custom_call_target="tpu_custom_call" | custom-call | flops 2000000000 | tf_op jit(solution)/shard_map/turn_step/pallas_call | solution.py:570
  69.5 6.0 %rival_step.6 = (f32[12,64,663]{2,1,0:T(8,128)}, f32[12,16,663]{2,1,0:T(8,128)}) custom-call(f32[32,768]{1,0:T(8,128)S(1)} %add.23.rest_7_.own_norm_ref, f32[32,768]{1,0:T(8,128)S(1)} %collective-permute-done.14.rest_8_.far_norm_ref, f32[6,64,768]{2,1,0:T(8,128)S(1)} %get-tuple-element.168.bar_ref, f32[6,64,768]{2,1,0:T(8,128)S(1)} %collective-permute-done.16.far_ref, ...), custom_call_target="tpu_custom_call" | custom-call | flops 6000000000 | tf_op jit(solution)/shard_map/rival_step/pallas_call | solution.py:570
  75.5 5.8 %rival_step.7 = (f32[12,64,663]{2,1,0:T(8,128)}, f32[12,16,663]{2,1,0:T(8,128)}) custom-call(f32[32,768]{1,0:T(8,128)S(1)} %add.23.rest_7_.own_norm_ref, f32[32,768]{1,0:T(8,128)S(1)} %collective-permute-done.14.rest_8_.far_norm_ref, f32[6,64,768]{2,1,0:T(8,128)S(1)} %get-tuple-element.166.bar_ref, ...), custom_call_target="tpu_custom_call", output_to_operand_aliasing={{0}: (20, {}), {1}: (21, {})} | custom-call | flops 6000000000 | tf_op jit(solution)/shard_map/rival_step/pallas_call | solution.py:570
  (80 shorter events, 11.3 us)
Async XLA Ops:
  0.6 10.3 %collective-permute-start.1 = (f32[12,64,663]{2,1,0:T(8,128)}, f32[12,64,663]{2,1,0:T(8,128)S(1)}, u32[]{:S(2)}, u32[]{:S(2)}) collective-permute-start(f32[12,64,663]{2,1,0:T(8,128)} %y_ref.11), channel_id=1, source_target_pairs={{0,1},{1,0},{2,3},{3,2},{4,5},{5,4},{6,7},{7,6},{8,9},{9,8},{10,11... | collective-permute-start | bytes 6110216 | tf_op jit(solution)/shard_map/ppermute | solution.py:549
  1.2 8.0 %collective-permute-start.2 = (s32[12,663]{1,0:T(8,128)}, s32[12,663]{1,0:T(8,128)S(1)}, u32[]{:S(2)}, u32[]{:S(2)}) collective-permute-start(s32[12,663]{1,0:T(8,128)} %refs_5_.3), channel_id=1, source_target_pairs={{0,1},{1,0},{2,3},{3,2},{4,5},{5,4},{6,7},{7,6},{8,9},{9,8},{10,11... | collective-permute-start | bytes 95480 | tf_op jit(solution)/shard_map/ppermute | solution.py:549
  1.2 8.0 %copy-start.8 = (f32[64,64]{1,0:T(8,128)S(1)}, f32[64,64]{1,0:T(8,128)}, u32[]{:S(2)}) copy-start(f32[64,64]{1,0:T(8,128)} %refs_9_.3) | copy-start | bytes 49156
  1.2 8.0 %copy-start.10 = (s32[16,64]{1,0:T(8,128)S(1)}, s32[16,64]{1,0:T(8,128)}, u32[]{:S(2)}) copy-start(s32[16,64]{1,0:T(8,128)} %children_ref.7) | copy-start | bytes 12292
  1.3 8.0 %copy-start.13 = (s32[8]{0:T(128)S(1)}, s32[8]{0:T(128)}, u32[]{:S(2)}) copy-start(s32[8]{0:T(128)} %refs_0_.3) | copy-start | bytes 100
  1.3 8.0 %copy-start.14 = (s32[4]{0:T(128)S(1)}, s32[4]{0:T(128)}, u32[]{:S(2)}) copy-start(s32[4]{0:T(128)} %cards_now_ref.7) | copy-start | bytes 52
  1.3 8.0 %copy-start.15 = (bf16[2,128,1536]{2,1,0:T(8,128)(2,1)S(1)}, bf16[2,128,1536]{2,1,0:T(8,128)(2,1)}, u32[]{:S(2)}) copy-start(bf16[2,128,1536]{2,1,0:T(8,128)(2,1)} %constant.14.clone.refs_4_.spread_ref) | copy-start | bytes 2359300
  1.3 8.0 %copy-start.16 = (bf16[2,1536,128]{2,1,0:T(8,128)(2,1)S(1)}, bf16[2,1536,128]{2,1,0:T(8,128)(2,1)}, u32[]{:S(2)}) copy-start(bf16[2,1536,128]{2,1,0:T(8,128)(2,1)} %constant.13.clone.refs_3_.gather_ref) | copy-start | bytes 2359300
  1.3 8.0 %copy-start.18 = (bf16[2,128,768]{2,1,0:T(8,128)(2,1)S(1)}, bf16[2,128,768]{2,1,0:T(8,128)(2,1)}, u32[]{:S(2)}) copy-start(bf16[2,128,768]{2,1,0:T(8,128)(2,1)} %constant.15.clone.refs_7_) | copy-start | bytes 1179652
  6.2 7.3 %collective-permute-start = (f32[48,768]{1,0:T(8,128)}, f32[48,768]{1,0:T(8,128)S(1)}, u32[]{:S(2)}, u32[]{:S(2)}) collective-permute-start(f32[48,768]{1,0:T(8,128)} %get-tuple-element.92), channel_id=1, source_target_pairs={{0,2},{2,0},{4,6},{6,4},{8,10},{10,8},{12,14},{14,12},{1,3},{3,1},... | collective-permute-start | bytes 442376 | tf_op jit(solution)/shard_map/ppermute | solution.py:552
  9.1 4.3 %collective-permute-start.3 = (f32[48,768]{1,0:T(8,128)}, f32[48,768]{1,0:T(8,128)S(1)}, u32[]{:S(2)}, u32[]{:S(2)}) collective-permute-start(f32[48,768]{1,0:T(8,128)} %get-tuple-element.107.pack_ref.rest_0_), channel_id=1, source_target_pairs={{0,1},{1,0},{2,3},{3,2},{4,5},{5,4},{6,7},{7,6},{8,9},{9,8},{10,11... | collective-permute-start | bytes 442376 | tf_op jit(solution)/shard_map/ppermute | solution.py:549
  13.5 6.2 %collective-permute-start.4 = (f32[48,768]{1,0:T(8,128)S(1)}, f32[48,768]{1,0:T(8,128)S(1)}, u32[]{:S(2)}, u32[]{:S(2)}) collective-permute-start(f32[48,768]{1,0:T(8,128)S(1)} %add.18), channel_id=1, source_target_pairs={{0,4},{2,6},{4,0},{6,2},{8,12},{10,14},{12,8},{14,10},{1,5},{3,7},... | collective-permute-start | bytes 442376 | tf_op jit(solution)/shard_map/ppermute | solution.py:552
  19.7 9.4 %collective-permute-start.5 = (f32[48,768]{1,0:T(8,128)S(1)}, f32[48,768]{1,0:T(8,128)S(1)}, u32[]{:S(2)}, u32[]{:S(2)}) collective-permute-start(f32[48,768]{1,0:T(8,128)S(1)} %add.19), channel_id=1, source_target_pairs={{0,8},{2,10},{4,12},{6,14},{8,0},{10,2},{12,4},{14,6},{1,9},{3,11}... | collective-permute-start | bytes 442376 | tf_op jit(solution)/shard_map/ppermute | solution.py:552
  29.2 1.4 %collective-permute-start.6 = (f32[48,768]{1,0:T(8,128)S(1)}, f32[48,768]{1,0:T(8,128)S(1)}, u32[]{:S(2)}, u32[]{:S(2)}) collective-permute-start(f32[48,768]{1,0:T(8,128)S(1)} %add.20.rest_4_.own_norm_ref), channel_id=1, source_target_pairs={{0,1},{1,0},{2,3},{3,2},{4,5},{5,4},{6,7},{7,6},{8,9},{9,8},{10,11... | collective-permute-start | bytes 442376 | tf_op jit(solution)/shard_map/ppermute | solution.py:549
  31.4 3.1 %collective-permute-start.8 = (f32[6,64,768]{2,1,0:T(8,128)S(1)}, f32[6,64,768]{2,1,0:T(8,128)S(1)}, u32[]{:S(2)}, u32[]{:S(2)}) collective-permute-start(f32[6,64,768]{2,1,0:T(8,128)S(1)} %get-tuple-element.126.bar_ref), channel_id=1, source_target_pairs={{0,1},{1,0},{2,3},{3,2},{4,5},{5,4},{6,7},{7,6},{8,9},{9,8},{10,11... | collective-permute-start | bytes 3538952 | tf_op jit(solution)/shard_map/ppermute | solution.py:549
  32.3 7.5 %collective-permute-start.7 = (f32[6,64,768]{2,1,0:T(8,128)S(1)}, f32[6,64,768]{2,1,0:T(8,128)S(1)}, u32[]{:S(2)}, u32[]{:S(2)}) collective-permute-start(f32[6,64,768]{2,1,0:T(8,128)S(1)} %get-tuple-element.123.bar_ref), channel_id=1, source_target_pairs={{0,1},{1,0},{2,3},{3,2},{4,5},{5,4},{6,7},{7,6},{8,9},{9,8},{10,11... | collective-permute-start | bytes 3538952 | tf_op jit(solution)/shard_map/ppermute | solution.py:549
  39.7 5.8 %collective-permute-start.10 = (f32[6,64,768]{2,1,0:T(8,128)S(1)}, f32[6,64,768]{2,1,0:T(8,128)S(1)}, u32[]{:S(2)}, u32[]{:S(2)}) collective-permute-start(f32[6,64,768]{2,1,0:T(8,128)S(1)} %get-tuple-element.132.y_ref), channel_id=1, source_target_pairs={{0,1},{1,0},{2,3},{3,2},{4,5},{5,4},{6,7},{7,6},{8,9},{9,8},{10,11... | collective-permute-start | bytes 3538952 | tf_op jit(solution)/shard_map/ppermute | solution.py:549
  45.0 12.7 %collective-permute-start.13 = (f32[6,64,768]{2,1,0:T(8,128)S(1)}, f32[6,64,768]{2,1,0:T(8,128)S(1)}, u32[]{:S(2)}, u32[]{:S(2)}) collective-permute-start(f32[6,64,768]{2,1,0:T(8,128)S(1)} %get-tuple-element.147.y_ref), channel_id=1, source_target_pairs={{0,1},{1,0},{2,3},{3,2},{4,5},{5,4},{6,7},{7,6},{8,9},{9,8},{10,11... | collective-permute-start | bytes 3538952 | tf_op jit(solution)/shard_map/ppermute | solution.py:549
  45.4 4.9 %collective-permute-start.9 = (f32[32,768]{1,0:T(8,128)S(1)}, f32[32,768]{1,0:T(8,128)S(1)}, u32[]{:S(2)}, u32[]{:S(2)}) collective-permute-start(f32[32,768]{1,0:T(8,128)S(1)} %get-tuple-element.131), channel_id=1, source_target_pairs={{0,2},{2,0},{4,6},{6,4},{8,10},{10,8},{12,14},{14,12},{1,3},{3,1},... | collective-permute-start | bytes 294920 | tf_op jit(solution)/shard_map/ppermute | solution.py:552
  50.3 4.7 %collective-permute-start.11 = (f32[32,768]{1,0:T(8,128)S(1)}, f32[32,768]{1,0:T(8,128)S(1)}, u32[]{:S(2)}, u32[]{:S(2)}) collective-permute-start(f32[32,768]{1,0:T(8,128)S(1)} %add.21), channel_id=1, source_target_pairs={{0,4},{2,6},{4,0},{6,2},{8,12},{10,14},{12,8},{14,10},{1,5},{3,7},... | collective-permute-start | bytes 294920 | tf_op jit(solution)/shard_map/ppermute | solution.py:552
  55.0 7.5 %collective-permute-start.12 = (f32[32,768]{1,0:T(8,128)S(1)}, f32[32,768]{1,0:T(8,128)S(1)}, u32[]{:S(2)}, u32[]{:S(2)}) collective-permute-start(f32[32,768]{1,0:T(8,128)S(1)} %add.22), channel_id=1, source_target_pairs={{0,8},{2,10},{4,12},{6,14},{8,0},{10,2},{12,4},{14,6},{1,9},{3,11}... | collective-permute-start | bytes 294920 | tf_op jit(solution)/shard_map/ppermute | solution.py:552
  62.6 1.4 %collective-permute-start.14 = (f32[32,768]{1,0:T(8,128)S(1)}, f32[32,768]{1,0:T(8,128)S(1)}, u32[]{:S(2)}, u32[]{:S(2)}) collective-permute-start(f32[32,768]{1,0:T(8,128)S(1)} %add.23.rest_7_.own_norm_ref), channel_id=1, source_target_pairs={{0,1},{1,0},{2,3},{3,2},{4,5},{5,4},{6,7},{7,6},{8,9},{9,8},{10,11... | collective-permute-start | bytes 294920 | tf_op jit(solution)/shard_map/ppermute | solution.py:549
  65.5 4.0 %collective-permute-start.16 = (f32[6,64,768]{2,1,0:T(8,128)S(1)}, f32[6,64,768]{2,1,0:T(8,128)S(1)}, u32[]{:S(2)}, u32[]{:S(2)}) collective-permute-start(f32[6,64,768]{2,1,0:T(8,128)S(1)} %get-tuple-element.168.bar_ref), channel_id=1, source_target_pairs={{0,1},{1,0},{2,3},{3,2},{4,5},{5,4},{6,7},{7,6},{8,9},{9,8},{10,11... | collective-permute-start | bytes 3538952 | tf_op jit(solution)/shard_map/ppermute | solution.py:549
  67.2 8.4 %collective-permute-start.15 = (f32[6,64,768]{2,1,0:T(8,128)S(1)}, f32[6,64,768]{2,1,0:T(8,128)S(1)}, u32[]{:S(2)}, u32[]{:S(2)}) collective-permute-start(f32[6,64,768]{2,1,0:T(8,128)S(1)} %get-tuple-element.166.bar_ref), channel_id=1, source_target_pairs={{0,1},{1,0},{2,3},{3,2},{4,5},{5,4},{6,7},{7,6},{8,9},{9,8},{10,11... | collective-permute-start | bytes 3538952 | tf_op jit(solution)/shard_map/ppermute | solution.py:549
  (14 other events, 55.7 us)

commit v3 on v2

--- a/solution.py
+++ b/solution.py
@@ -747,7 +747,7 @@
         now, _ = lax.optimization_barrier((pack, value))
         return turn_start(False, (now, bar_turn))
 
-    grad, flow, norms, starts = gradients(total, y_far[0], y, y_far, u, pack, second_start, 1)
+    grad, flow, norms, starts = gradients(total, y_far[0], y, y_far, u, pack, second_start, 0)
     next_x, next_v, bar = mover_steps(True, norms, x, v, grad, flow)
     bar_far = [swap(item) for item in bar]
     bar_turn, next_xt, next_vt, next_yt, next_ut = turn_call(False, (pack, *starts, kept, turn_steps, *norms))

time: 81.5 us -> 80.5 us (0.988)
  starting transfers between devices: 13.6 us -> 12.7 us
    ppermute x6, starting transfers between devices: 11.1 us -> 10.2 us  [hop_total(): lax.ppermute(value, 'river', [(at, at ^ hop) for at in range(river_count)])]
  transfers between devices with their start and end apart: 17 -> 17, of which waited for: 7 -> 7; matrix products, arithmetic and copies ran while one was open for 0% -> 0% of each run, Pallas kernels for 61% -> 62%
where the time goes in v3:
time: 80.5 us; the launch traced here: 80.4 us
  Pallas kernels  58 us (72%)
  starting transfers between devices  12.7 us (16%)
  waiting for transfers between devices  8.39 us (10%)
  between operations  1.05 us (1%)
    pallas_call x22, Pallas kernels, call(): pl.pallas_call(kernel, grid_spec=pltpu.PrefetchScalarGridSpec(num_scalar_...  58 us
    ppermute x6, starting transfers between devices, hop_total(): lax.ppermute(value, 'river', [(at, at ^ hop) for at in range(river_count)])  10.2 us
    ppermute x6, waiting for transfers between devices, hop_total(): lax.ppermute(value, 'river', [(at, at ^ hop) for at in range(river_count)])  5.72 us
    ppermute x11, waiting for transfers between devices, swap(): return lax.ppermute(value, 'hand', [(0, 1), (1, 0)])  2.67 us
    ppermute x11, starting transfers between devices, swap(): return lax.ppermute(value, 'hand', [(0, 1), (1, 0)])  2.48 us
  transfers between devices with their start and end apart: 17, of which 7 were waited for; matrix products, arithmetic and copies ran while one was open for 0% of the time, Pallas kernels for 62%

profile of v3, /device:TPU:0, one launch (start us, length us, event | category | flops | bytes accessed | tf_op | source)
XLA Modules:
  0.0 80.4 jit_solution(17301994990932712122)
XLA Ops:
  1.3 4.8 %stats.1 = (f32[48,768]{1,0:T(8,128)}, f32[48,768]{1,0:T(8,128)}) custom-call(s32[1]{0:T(128)} %bitcast.hand_ref, s32[8]{0:T(128)} %refs_0_.3, s32[4]{0:T(128)} %cards_now_ref.7, s32[2,8,1536]{2,1,0:T(8,128)} %constant.12.clone.refs_2_.card_ref, s32[12,663]{1,0:T(8,128)} %refs_5_.3, f32[12,64,663]{2,1,0:T(8,128)} %x_ref.3, f32[12,16,663]{2,1,0:T(8,128)} %v_ref.3, ...), custom_call_target="tpu_custom_call" | custom-call | flops 5000000000 | tf_op jit(solution)/shard_map/stats/pallas_call | solution.py:570
  6.2 3.0 %collective-permute-start = (f32[48,768]{1,0:T(8,128)}, f32[48,768]{1,0:T(8,128)S(1)}, u32[]{:S(2)}, u32[]{:S(2)}) collective-permute-start(f32[48,768]{1,0:T(8,128)} %get-tuple-element.92), channel_id=1, source_target_pairs={{0,2},{2,0},{4,6},{6,4},{8,10},{10,8},{12,14},{14,12},{1,3},{3,1},... | collective-permute-start | bytes 442376 | tf_op jit(solution)/shard_map/ppermute | solution.py:552
  9.3 1.6 %prepare.1 = (f32[12,1,1536]{2,1,0:T(1,128)S(1)}, bf16[12,1,768]{2,1,0:T(2,128)(2,1)S(1)}, f32[4,1536,3]{2,1,0:T(8,128)S(1)}, bf16[1536,768]{1,0:T(8,128)(2,1)S(...) custom-call(s32[1]{0:T(128)} %bitcast.hand_ref, ...), custom_call_target="tpu_custom_call" | custom-call | flops 2000000000 | tf_op jit(solution)/shard_map/prepare/pallas_call | solution.py:570
  10.9 2.4 %mover_gradient.8 = (f32[3,64,768]{2,1,0:T(8,128)S(1)}, f32[3,16,768]{2,1,0:T(8,128)S(1)}) custom-call(f32[12,64,663]{2,1,0:T(8,128)S(1)} %copy-done, f32[12,64,663]{2,1,0:T(8,128)S(1)} %collective-permute-done.1.far_ref, f32[12,16,663]{2,1,0:T(8,128)S(1)} %copy-done.1, f32[12,1,1536]{2,1,0:T(1,128)S(1)} %get-tuple-element.93.live_ref, ...), custom_call_target="tpu_custom_call" | custom-call | flops 3000000000 | tf_op jit(solution)/shard_map/mover_gradient/pallas_call | solution.py:570
  13.5 1.9 %collective-permute-start.4 = (f32[48,768]{1,0:T(8,128)S(1)}, f32[48,768]{1,0:T(8,128)S(1)}, u32[]{:S(2)}, u32[]{:S(2)}) collective-permute-start(f32[48,768]{1,0:T(8,128)S(1)} %add.18), channel_id=1, source_target_pairs={{0,4},{2,6},{4,0},{6,2},{8,12},{10,14},{12,8},{14,10},{1,5},{3,7},... | collective-permute-start | bytes 442376 | tf_op jit(solution)/shard_map/ppermute | solution.py:552
  15.3 2.3 %mover_gradient.9 = (f32[3,64,768]{2,1,0:T(8,128)S(1)}, f32[3,16,768]{2,1,0:T(8,128)S(1)}) custom-call(f32[12,64,663]{2,1,0:T(8,128)S(1)} %copy-done, f32[12,64,663]{2,1,0:T(8,128)S(1)} %collective-permute-done.1.far_ref, f32[12,16,663]{2,1,0:T(8,128)S(1)} %copy-done.1, f32[12,1,1536]{2,1,0:T(1,128)S(1)} %get-tuple-element.93.live_ref, ...), custom_call_target="tpu_custom_call" | custom-call | flops 3000000000 | tf_op jit(solution)/shard_map/mover_gradient/pallas_call | solution.py:570
  17.7 2.0 %collective-permute-done.4 = f32[48,768]{1,0:T(8,128)S(1)} collective-permute-done((f32[48,768]{1,0:T(8,128)S(1)}, f32[48,768]{1,0:T(8,128)S(1)}, u32[]{:S(2)}, u32[]{:S(2)}) %collective-permute-start.4) | collective-permute-done | bytes 147488 | tf_op jit(solution)/shard_map/ppermute | solution.py:552
  19.7 2.6 %collective-permute-start.5 = (f32[48,768]{1,0:T(8,128)S(1)}, f32[48,768]{1,0:T(8,128)S(1)}, u32[]{:S(2)}, u32[]{:S(2)}) collective-permute-start(f32[48,768]{1,0:T(8,128)S(1)} %add.19), channel_id=1, source_target_pairs={{0,8},{2,10},{4,12},{6,14},{8,0},{10,2},{12,4},{14,6},{1,9},{3,11}... | collective-permute-start | bytes 442376 | tf_op jit(solution)/shard_map/ppermute | solution.py:552
  22.3 2.4 %mover_gradient.11 = (f32[3,64,768]{2,1,0:T(8,128)S(1)}, f32[3,16,768]{2,1,0:T(8,128)S(1)}) custom-call(f32[12,64,663]{2,1,0:T(8,128)S(1)} %copy-done, f32[12,64,663]{2,1,0:T(8,128)S(1)} %collective-permute-done.1.far_ref, f32[12,16,663]{2,1,0:T(8,128)S(1)} %copy-done.1, f32[12,1,1536]{2,1,0:T(1,128)S(1)} %get-tuple-element.93.live_ref, ...), custom_call_target="tpu_custom_call" | custom-call | flops 3000000000 | tf_op jit(solution)/shard_map/mover_gradient/pallas_call | solution.py:570
  24.7 2.4 %mover_gradient.10 = (f32[3,64,768]{2,1,0:T(8,128)S(1)}, f32[3,16,768]{2,1,0:T(8,128)S(1)}) custom-call(f32[12,64,663]{2,1,0:T(8,128)S(1)} %copy-done, f32[12,64,663]{2,1,0:T(8,128)S(1)} %collective-permute-done.1.far_ref, f32[12,16,663]{2,1,0:T(8,128)S(1)} %copy-done.1, f32[12,1,1536]{2,1,0:T(1,128)S(1)} %get-tuple-element.93.live_ref, ...), custom_call_target="tpu_custom_call" | custom-call | flops 3000000000 | tf_op jit(solution)/shard_map/mover_gradient/pallas_call | solution.py:570
  32.7 1.7 %turn_step.2 = (f32[48,1536]{1,0:T(8,128)S(1)}, f32[32,1536]{1,0:T(8,128)S(1)}, f32[16,1536]{1,0:T(8,128)S(1)}, f32[8,768]{1,0:T(8,128)S(1)}, f32[8,128]{1,0:T(8,128)S(1)}) custom-call(s32[1]{0:T(128)} %bitcast.hand_ref, s32[4]{0:T(128)S(1)} %copy-done.14, s32[2,8,1536]{2,1,0:T(8,128)S(1)} %copy-done.19, bf16[2,1536,128]{2,1,0:T(8,128)(2,1)S(1)} %copy-done.16, ...), custom_call_target="tpu_custom_call" | custom-call | flops 2000000000 | tf_op jit(solution)/shard_map/turn_step/pallas_call | solution.py:570
  34.4 5.2 %rival_step.4 = (f32[6,64,768]{2,1,0:T(8,128)S(1)}, f32[6,16,768]{2,1,0:T(8,128)S(1)}, f32[32,768]{1,0:T(8,128)S(1)}) custom-call(f32[48,768]{1,0:T(8,128)S(1)} %add.20.rest_4_.own_norm_ref, f32[48,768]{1,0:T(8,128)S(1)} %collective-permute-done.6.rest_5_.far_norm_ref, f32[6,64,768]{2,1,0:T(8,128)S(1)} %get-tuple-element.126.bar_ref, ...), custom_call_target="tpu_custom_call" | custom-call | flops 6000000000 | tf_op jit(solution)/shard_map/rival_step/pallas_call | solution.py:570
  39.8 5.2 %rival_step.5 = (f32[6,64,768]{2,1,0:T(8,128)S(1)}, f32[6,16,768]{2,1,0:T(8,128)S(1)}, f32[32,768]{1,0:T(8,128)S(1)}) custom-call(f32[48,768]{1,0:T(8,128)S(1)} %add.20.rest_4_.own_norm_ref, f32[48,768]{1,0:T(8,128)S(1)} %collective-permute-done.6.rest_5_.far_norm_ref, f32[6,64,768]{2,1,0:T(8,128)S(1)} %get-tuple-element.123.bar_ref, ...), custom_call_target="tpu_custom_call" | custom-call | flops 6000000000 | tf_op jit(solution)/shard_map/rival_step/pallas_call | solution.py:570
  46.6 2.4 %mover_gradient.12 = (f32[3,64,768]{2,1,0:T(8,128)S(1)}, f32[3,16,768]{2,1,0:T(8,128)S(1)}) custom-call(f32[6,64,768]{2,1,0:T(8,128)S(1)} %get-tuple-element.139.y_ref, f32[6,64,768]{2,1,0:T(8,128)S(1)} %collective-permute-done.10.far_ref, f32[6,16,768]{2,1,0:T(8,128)S(1)} %get-tuple-element.140.u_ref, f32[12,1,1536]{2,1,0:T(1,128)S(1)} %get-tuple-element.93.live_ref, ...), custom_call_target="tpu_custom_call" | custom-call | flops 3000000000 | tf_op jit(solution)/shard_map/mover_gradient/pallas_call | solution.py:570
  51.1 2.3 %mover_gradient.13 = (f32[3,64,768]{2,1,0:T(8,128)S(1)}, f32[3,16,768]{2,1,0:T(8,128)S(1)}) custom-call(f32[6,64,768]{2,1,0:T(8,128)S(1)} %get-tuple-element.139.y_ref, f32[6,64,768]{2,1,0:T(8,128)S(1)} %collective-permute-done.10.far_ref, f32[6,16,768]{2,1,0:T(8,128)S(1)} %get-tuple-element.140.u_ref, f32[12,1,1536]{2,1,0:T(1,128)S(1)} %get-tuple-element.93.live_ref, ...), custom_call_target="tpu_custom_call" | custom-call | flops 3000000000 | tf_op jit(solution)/shard_map/mover_gradient/pallas_call | solution.py:570
  53.5 1.5 %collective-permute-done.11 = f32[32,768]{1,0:T(8,128)S(1)} collective-permute-done((f32[32,768]{1,0:T(8,128)S(1)}, f32[32,768]{1,0:T(8,128)S(1)}, u32[]{:S(2)}, u32[]{:S(2)}) %collective-permute-start.11) | collective-permute-done | bytes 98336 | tf_op jit(solution)/shard_map/ppermute | solution.py:552
  55.0 1.9 %collective-permute-start.12 = (f32[32,768]{1,0:T(8,128)S(1)}, f32[32,768]{1,0:T(8,128)S(1)}, u32[]{:S(2)}, u32[]{:S(2)}) collective-permute-start(f32[32,768]{1,0:T(8,128)S(1)} %add.22), channel_id=1, source_target_pairs={{0,8},{2,10},{4,12},{6,14},{8,0},{10,2},{12,4},{14,6},{1,9},{3,11}... | collective-permute-start | bytes 294920 | tf_op jit(solution)/shard_map/ppermute | solution.py:552
  56.8 2.4 %mover_gradient.15 = (f32[3,64,768]{2,1,0:T(8,128)S(1)}, f32[3,16,768]{2,1,0:T(8,128)S(1)}) custom-call(f32[6,64,768]{2,1,0:T(8,128)S(1)} %get-tuple-element.147.y_ref, f32[6,64,768]{2,1,0:T(8,128)S(1)} %collective-permute-done.13.far_ref, f32[6,16,768]{2,1,0:T(8,128)S(1)} %get-tuple-element.148.u_ref, f32[12,1,1536]{2,1,0:T(1,128)S(1)} %get-tuple-element.93.live_ref, ...), custom_call_target="tpu_custom_call" | custom-call | flops 3000000000 | tf_op jit(solution)/shard_map/mover_gradient/pallas_call | solution.py:570
  59.2 2.4 %mover_gradient.14 = (f32[3,64,768]{2,1,0:T(8,128)S(1)}, f32[3,16,768]{2,1,0:T(8,128)S(1)}) custom-call(f32[6,64,768]{2,1,0:T(8,128)S(1)} %get-tuple-element.147.y_ref, f32[6,64,768]{2,1,0:T(8,128)S(1)} %collective-permute-done.13.far_ref, f32[6,16,768]{2,1,0:T(8,128)S(1)} %get-tuple-element.148.u_ref, f32[12,1,1536]{2,1,0:T(1,128)S(1)} %get-tuple-element.93.live_ref, ...), custom_call_target="tpu_custom_call" | custom-call | flops 3000000000 | tf_op jit(solution)/shard_map/mover_gradient/pallas_call | solution.py:570
  63.0 1.5 %mover_step.6 = (f32[12,64,663]{2,1,0:T(8,128)}, f32[12,16,663]{2,1,0:T(8,128)}, f32[6,64,768]{2,1,0:T(8,128)S(1)}) custom-call(f32[32,768]{1,0:T(8,128)S(1)} %add.23.rest_7_.own_norm_ref, f32[32,768]{1,0:T(8,128)S(1)} %collective-permute-done.14.rest_8_.far_norm_ref, f32[6,64,768]{2,1,0:T(8,128)S(1)} %get-tuple-element.157.x_ref, ...), custom_call_target="tpu_custom_call" | custom-call | flops 2000000000 | tf_op jit(solution)/shard_map/mover_step/pallas_call | solution.py:570
  64.7 1.5 %mover_step.7 = (f32[12,64,663]{2,1,0:T(8,128)}, f32[12,16,663]{2,1,0:T(8,128)}, f32[6,64,768]{2,1,0:T(8,128)S(1)}) custom-call(f32[32,768]{1,0:T(8,128)S(1)} %add.23.rest_7_.own_norm_ref, f32[32,768]{1,0:T(8,128)S(1)} %collective-permute-done.14.rest_8_.far_norm_ref, ...), custom_call_target="tpu_custom_call", output_to_operand_aliasing={{0}: (9, {}), {1}: (10, {})} | custom-call | flops 2000000000 | tf_op jit(solution)/shard_map/mover_step/pallas_call | solution.py:570
  66.6 2.0 %turn_step.3 = (f32[16,1536]{1,0:T(8,128)S(1)}, f32[16,663]{1,0:T(8,128)}, f32[6,663]{1,0:T(8,128)}, f32[16,663]{1,0:T(8,128)}, f32[6,663]{1,0:T(8,128)}) custom-call(s32[1]{0:T(128)} %bitcast.hand_ref, s32[4]{0:T(128)S(1)} %copy-done.14, s32[2,8,1536]{2,1,0:T(8,128)S(1)} %copy-done.19, bf16[2,1536,128]{2,1,0:T(8,128)(2,1)S(1)} %copy-done.16, ...), custom_call_target="tpu_custom_call" | custom-call | flops 2000000000 | tf_op jit(solution)/shard_map/turn_step/pallas_call | solution.py:570
  68.6 6.0 %rival_step.6 = (f32[12,64,663]{2,1,0:T(8,128)}, f32[12,16,663]{2,1,0:T(8,128)}) custom-call(f32[32,768]{1,0:T(8,128)S(1)} %add.23.rest_7_.own_norm_ref, f32[32,768]{1,0:T(8,128)S(1)} %collective-permute-done.14.rest_8_.far_norm_ref, f32[6,64,768]{2,1,0:T(8,128)S(1)} %get-tuple-element.168.bar_ref, f32[6,64,768]{2,1,0:T(8,128)S(1)} %collective-permute-done.16.far_ref, ...), custom_call_target="tpu_custom_call" | custom-call | flops 6000000000 | tf_op jit(solution)/shard_map/rival_step/pallas_call | solution.py:570
  74.6 5.8 %rival_step.7 = (f32[12,64,663]{2,1,0:T(8,128)}, f32[12,16,663]{2,1,0:T(8,128)}) custom-call(f32[32,768]{1,0:T(8,128)S(1)} %add.23.rest_7_.own_norm_ref, f32[32,768]{1,0:T(8,128)S(1)} %collective-permute-done.14.rest_8_.far_norm_ref, f32[6,64,768]{2,1,0:T(8,128)S(1)} %get-tuple-element.166.bar_ref, ...), custom_call_target="tpu_custom_call", output_to_operand_aliasing={{0}: (20, {}), {1}: (21, {})} | custom-call | flops 6000000000 | tf_op jit(solution)/shard_map/rival_step/pallas_call | solution.py:570
  (80 shorter events, 12.3 us)
Async XLA Ops:
  0.6 10.3 %collective-permute-start.1 = (f32[12,64,663]{2,1,0:T(8,128)}, f32[12,64,663]{2,1,0:T(8,128)S(1)}, u32[]{:S(2)}, u32[]{:S(2)}) collective-permute-start(f32[12,64,663]{2,1,0:T(8,128)} %y_ref.11), channel_id=1, source_target_pairs={{0,1},{1,0},{2,3},{3,2},{4,5},{5,4},{6,7},{7,6},{8,9},{9,8},{10,11... | collective-permute-start | bytes 6110216 | tf_op jit(solution)/shard_map/ppermute | solution.py:549
  1.2 8.0 %collective-permute-start.2 = (s32[12,663]{1,0:T(8,128)}, s32[12,663]{1,0:T(8,128)S(1)}, u32[]{:S(2)}, u32[]{:S(2)}) collective-permute-start(s32[12,663]{1,0:T(8,128)} %refs_5_.3), channel_id=1, source_target_pairs={{0,1},{1,0},{2,3},{3,2},{4,5},{5,4},{6,7},{7,6},{8,9},{9,8},{10,11... | collective-permute-start | bytes 95480 | tf_op jit(solution)/shard_map/ppermute | solution.py:549
  1.2 8.0 %copy-start.8 = (f32[64,64]{1,0:T(8,128)S(1)}, f32[64,64]{1,0:T(8,128)}, u32[]{:S(2)}) copy-start(f32[64,64]{1,0:T(8,128)} %refs_9_.3) | copy-start | bytes 49156
  1.2 8.0 %copy-start.10 = (s32[16,64]{1,0:T(8,128)S(1)}, s32[16,64]{1,0:T(8,128)}, u32[]{:S(2)}) copy-start(s32[16,64]{1,0:T(8,128)} %children_ref.7) | copy-start | bytes 12292
  1.3 8.0 %copy-start.13 = (s32[8]{0:T(128)S(1)}, s32[8]{0:T(128)}, u32[]{:S(2)}) copy-start(s32[8]{0:T(128)} %refs_0_.3) | copy-start | bytes 100
  1.3 8.0 %copy-start.14 = (s32[4]{0:T(128)S(1)}, s32[4]{0:T(128)}, u32[]{:S(2)}) copy-start(s32[4]{0:T(128)} %cards_now_ref.7) | copy-start | bytes 52
  1.3 8.0 %copy-start.15 = (bf16[2,128,1536]{2,1,0:T(8,128)(2,1)S(1)}, bf16[2,128,1536]{2,1,0:T(8,128)(2,1)}, u32[]{:S(2)}) copy-start(bf16[2,128,1536]{2,1,0:T(8,128)(2,1)} %constant.14.clone.refs_4_.spread_ref) | copy-start | bytes 2359300
  1.3 8.0 %copy-start.16 = (bf16[2,1536,128]{2,1,0:T(8,128)(2,1)S(1)}, bf16[2,1536,128]{2,1,0:T(8,128)(2,1)}, u32[]{:S(2)}) copy-start(bf16[2,1536,128]{2,1,0:T(8,128)(2,1)} %constant.13.clone.refs_3_.gather_ref) | copy-start | bytes 2359300
  1.3 8.0 %copy-start.18 = (bf16[2,128,768]{2,1,0:T(8,128)(2,1)S(1)}, bf16[2,128,768]{2,1,0:T(8,128)(2,1)}, u32[]{:S(2)}) copy-start(bf16[2,128,768]{2,1,0:T(8,128)(2,1)} %constant.15.clone.refs_7_) | copy-start | bytes 1179652
  6.2 7.3 %collective-permute-start = (f32[48,768]{1,0:T(8,128)}, f32[48,768]{1,0:T(8,128)S(1)}, u32[]{:S(2)}, u32[]{:S(2)}) collective-permute-start(f32[48,768]{1,0:T(8,128)} %get-tuple-element.92), channel_id=1, source_target_pairs={{0,2},{2,0},{4,6},{6,4},{8,10},{10,8},{12,14},{14,12},{1,3},{3,1},... | collective-permute-start | bytes 442376 | tf_op jit(solution)/shard_map/ppermute | solution.py:552
  9.1 4.3 %collective-permute-start.3 = (f32[48,768]{1,0:T(8,128)}, f32[48,768]{1,0:T(8,128)S(1)}, u32[]{:S(2)}, u32[]{:S(2)}) collective-permute-start(f32[48,768]{1,0:T(8,128)} %get-tuple-element.107.pack_ref.rest_0_), channel_id=1, source_target_pairs={{0,1},{1,0},{2,3},{3,2},{4,5},{5,4},{6,7},{7,6},{8,9},{9,8},{10,11... | collective-permute-start | bytes 442376 | tf_op jit(solution)/shard_map/ppermute | solution.py:549
  13.5 6.2 %collective-permute-start.4 = (f32[48,768]{1,0:T(8,128)S(1)}, f32[48,768]{1,0:T(8,128)S(1)}, u32[]{:S(2)}, u32[]{:S(2)}) collective-permute-start(f32[48,768]{1,0:T(8,128)S(1)} %add.18), channel_id=1, source_target_pairs={{0,4},{2,6},{4,0},{6,2},{8,12},{10,14},{12,8},{14,10},{1,5},{3,7},... | collective-permute-start | bytes 442376 | tf_op jit(solution)/shard_map/ppermute | solution.py:552
  19.7 9.4 %collective-permute-start.5 = (f32[48,768]{1,0:T(8,128)S(1)}, f32[48,768]{1,0:T(8,128)S(1)}, u32[]{:S(2)}, u32[]{:S(2)}) collective-permute-start(f32[48,768]{1,0:T(8,128)S(1)} %add.19), channel_id=1, source_target_pairs={{0,8},{2,10},{4,12},{6,14},{8,0},{10,2},{12,4},{14,6},{1,9},{3,11}... | collective-permute-start | bytes 442376 | tf_op jit(solution)/shard_map/ppermute | solution.py:552
  29.1 1.4 %collective-permute-start.6 = (f32[48,768]{1,0:T(8,128)S(1)}, f32[48,768]{1,0:T(8,128)S(1)}, u32[]{:S(2)}, u32[]{:S(2)}) collective-permute-start(f32[48,768]{1,0:T(8,128)S(1)} %add.20.rest_4_.own_norm_ref), channel_id=1, source_target_pairs={{0,1},{1,0},{2,3},{3,2},{4,5},{5,4},{6,7},{7,6},{8,9},{9,8},{10,11... | collective-permute-start | bytes 442376 | tf_op jit(solution)/shard_map/ppermute | solution.py:549
  31.3 3.1 %collective-permute-start.8 = (f32[6,64,768]{2,1,0:T(8,128)S(1)}, f32[6,64,768]{2,1,0:T(8,128)S(1)}, u32[]{:S(2)}, u32[]{:S(2)}) collective-permute-start(f32[6,64,768]{2,1,0:T(8,128)S(1)} %get-tuple-element.126.bar_ref), channel_id=1, source_target_pairs={{0,1},{1,0},{2,3},{3,2},{4,5},{5,4},{6,7},{7,6},{8,9},{9,8},{10,11... | collective-permute-start | bytes 3538952 | tf_op jit(solution)/shard_map/ppermute | solution.py:549
  32.3 7.5 %collective-permute-start.7 = (f32[6,64,768]{2,1,0:T(8,128)S(1)}, f32[6,64,768]{2,1,0:T(8,128)S(1)}, u32[]{:S(2)}, u32[]{:S(2)}) collective-permute-start(f32[6,64,768]{2,1,0:T(8,128)S(1)} %get-tuple-element.123.bar_ref), channel_id=1, source_target_pairs={{0,1},{1,0},{2,3},{3,2},{4,5},{5,4},{6,7},{7,6},{8,9},{9,8},{10,11... | collective-permute-start | bytes 3538952 | tf_op jit(solution)/shard_map/ppermute | solution.py:549
  39.6 7.0 %collective-permute-start.10 = (f32[6,64,768]{2,1,0:T(8,128)S(1)}, f32[6,64,768]{2,1,0:T(8,128)S(1)}, u32[]{:S(2)}, u32[]{:S(2)}) collective-permute-start(f32[6,64,768]{2,1,0:T(8,128)S(1)} %get-tuple-element.139.y_ref), channel_id=1, source_target_pairs={{0,1},{1,0},{2,3},{3,2},{4,5},{5,4},{6,7},{7,6},{8,9},{9,8},{10,11... | collective-permute-start | bytes 3538952 | tf_op jit(solution)/shard_map/ppermute | solution.py:549
  45.0 11.8 %collective-permute-start.13 = (f32[6,64,768]{2,1,0:T(8,128)S(1)}, f32[6,64,768]{2,1,0:T(8,128)S(1)}, u32[]{:S(2)}, u32[]{:S(2)}) collective-permute-start(f32[6,64,768]{2,1,0:T(8,128)S(1)} %get-tuple-element.147.y_ref), channel_id=1, source_target_pairs={{0,1},{1,0},{2,3},{3,2},{4,5},{5,4},{6,7},{7,6},{8,9},{9,8},{10,11... | collective-permute-start | bytes 3538952 | tf_op jit(solution)/shard_map/ppermute | solution.py:549
  45.4 4.8 %collective-permute-start.9 = (f32[32,768]{1,0:T(8,128)S(1)}, f32[32,768]{1,0:T(8,128)S(1)}, u32[]{:S(2)}, u32[]{:S(2)}) collective-permute-start(f32[32,768]{1,0:T(8,128)S(1)} %get-tuple-element.131), channel_id=1, source_target_pairs={{0,2},{2,0},{4,6},{6,4},{8,10},{10,8},{12,14},{14,12},{1,3},{3,1},... | collective-permute-start | bytes 294920 | tf_op jit(solution)/shard_map/ppermute | solution.py:552
  50.3 4.7 %collective-permute-start.11 = (f32[32,768]{1,0:T(8,128)S(1)}, f32[32,768]{1,0:T(8,128)S(1)}, u32[]{:S(2)}, u32[]{:S(2)}) collective-permute-start(f32[32,768]{1,0:T(8,128)S(1)} %add.21), channel_id=1, source_target_pairs={{0,4},{2,6},{4,0},{6,2},{8,12},{10,14},{12,8},{14,10},{1,5},{3,7},... | collective-permute-start | bytes 294920 | tf_op jit(solution)/shard_map/ppermute | solution.py:552
  55.0 6.6 %collective-permute-start.12 = (f32[32,768]{1,0:T(8,128)S(1)}, f32[32,768]{1,0:T(8,128)S(1)}, u32[]{:S(2)}, u32[]{:S(2)}) collective-permute-start(f32[32,768]{1,0:T(8,128)S(1)} %add.22), channel_id=1, source_target_pairs={{0,8},{2,10},{4,12},{6,14},{8,0},{10,2},{12,4},{14,6},{1,9},{3,11}... | collective-permute-start | bytes 294920 | tf_op jit(solution)/shard_map/ppermute | solution.py:552
  61.6 1.4 %collective-permute-start.14 = (f32[32,768]{1,0:T(8,128)S(1)}, f32[32,768]{1,0:T(8,128)S(1)}, u32[]{:S(2)}, u32[]{:S(2)}) collective-permute-start(f32[32,768]{1,0:T(8,128)S(1)} %add.23.rest_7_.own_norm_ref), channel_id=1, source_target_pairs={{0,1},{1,0},{2,3},{3,2},{4,5},{5,4},{6,7},{7,6},{8,9},{9,8},{10,11... | collective-permute-start | bytes 294920 | tf_op jit(solution)/shard_map/ppermute | solution.py:549
  64.5 4.1 %collective-permute-start.16 = (f32[6,64,768]{2,1,0:T(8,128)S(1)}, f32[6,64,768]{2,1,0:T(8,128)S(1)}, u32[]{:S(2)}, u32[]{:S(2)}) collective-permute-start(f32[6,64,768]{2,1,0:T(8,128)S(1)} %get-tuple-element.168.bar_ref), channel_id=1, source_target_pairs={{0,1},{1,0},{2,3},{3,2},{4,5},{5,4},{6,7},{7,6},{8,9},{9,8},{10,11... | collective-permute-start | bytes 3538952 | tf_op jit(solution)/shard_map/ppermute | solution.py:549
  66.2 8.4 %collective-permute-start.15 = (f32[6,64,768]{2,1,0:T(8,128)S(1)}, f32[6,64,768]{2,1,0:T(8,128)S(1)}, u32[]{:S(2)}, u32[]{:S(2)}) collective-permute-start(f32[6,64,768]{2,1,0:T(8,128)S(1)} %get-tuple-element.166.bar_ref), channel_id=1, source_target_pairs={{0,1},{1,0},{2,3},{3,2},{4,5},{5,4},{6,7},{7,6},{8,9},{9,8},{10,11... | collective-permute-start | bytes 3538952 | tf_op jit(solution)/shard_map/ppermute | solution.py:549
  (14 other events, 55.7 us)

commit v4 on v3

--- a/solution.py
+++ b/solution.py
@@ -196,7 +196,8 @@
     for place in range(slots // group):
         col_ref[place] = turned[:, place * group:(place + 1) * group]
     free = jnp.dot(gather_ref[0], spread_ref[0][:, :padded], preferred_element_type=F32)
-    compat_ref[...] = jnp.maximum(free, 0.0).astype(BF16)
+    compat_ref[0] = jnp.maximum(free, 0.0).astype(BF16)
+    compat_ref[1] = jnp.minimum(-free, 0.0).astype(BF16)
     near_ref[...] = near_table_ref[0]
     for place in range(2):
         set_operators(place == 1, pot_ref, fold_ref, children_ref, parents_ref, main_ref.at[place], folds_ref.at[place],
@@ -249,8 +250,8 @@
             piece = left[place // tiles][:, (place % tiles) * TILE:(place % tiles) * TILE + depth]
             for across in range(tiles):
                 lanes = slice(across * TILE, (across + 1) * TILE)
-                bound = compat_ref[rows, lanes]
-                signs = jnp.minimum(jnp.maximum(column - row[:, lanes], -bound), bound)
+                bound = compat_ref[0, rows, lanes]
+                signs = jnp.minimum(jnp.maximum(column - row[:, lanes], compat_ref[1, rows, lanes]), bound)
                 part = jnp.dot(piece, signs, preferred_element_type=F32)
                 sums[across] = part if sums[across] is None else sums[across] + part
         mixes.append(split_two(jnp.concatenate([item[:sequences] + item[sequences:] for item in sums], axis=1)))
@@ -608,7 +609,7 @@
     gather_block = pl.BlockSpec((1, both, LANES), lambda at, ref: (ref[0], 0, 0))
     spread_block = pl.BlockSpec((1, LANES, both), lambda at, ref: (ref[0], 0, 0))
     prepared = [shape(slots, 1, both), shape(slots, 1, padded, dtype=BF16), shape(slots // group, both, group),
-                shape(both, padded, dtype=BF16), shape(LANES, padded, dtype=BF16)] + [shape(2, *size, dtype=BF16) for size in operator_sizes]
+                shape(2, both, padded, dtype=BF16), shape(LANES, padded, dtype=BF16)] + [shape(2, *size, dtype=BF16) for size in operator_sizes]
     near_block = pl.BlockSpec((1, LANES, padded), lambda at, ref: (ref[0], 0, 0))
     tables = call(
         prepare_kernel_here, "prepare", 1, (1,),

time: 80.5 us -> 80.3 us (level)
  no operation moved by 1% of the time
where the time goes in v4:
time: 80.3 us; the launch traced here: 80.1 us
  Pallas kernels  57.5 us (72%)
  starting transfers between devices  12.6 us (16%)
  waiting for transfers between devices  8.61 us (11%)
  between operations  1.04 us (1%)
    pallas_call x22, Pallas kernels, call(): pl.pallas_call(kernel, grid_spec=pltpu.PrefetchScalarGridSpec(num_scalar_...  57.5 us
    ppermute x6, starting transfers between devices, hop_total(): lax.ppermute(value, 'river', [(at, at ^ hop) for at in range(river_count)])  10.1 us
    ppermute x6, waiting for transfers between devices, hop_total(): lax.ppermute(value, 'river', [(at, at ^ hop) for at in range(river_count)])  5.94 us
    ppermute x11, waiting for transfers between devices, swap(): return lax.ppermute(value, 'hand', [(0, 1), (1, 0)])  2.67 us
    ppermute x11, starting transfers between devices, swap(): return lax.ppermute(value, 'hand', [(0, 1), (1, 0)])  2.48 us
  transfers between devices with their start and end apart: 17, of which 7 were waited for; matrix products, arithmetic and copies ran while one was open for 0% of the time, Pallas kernels for 62%

profile of v4, /device:TPU:0, one launch (start us, length us, event | category | flops | bytes accessed | tf_op | source)
XLA Modules:
  0.0 80.1 jit_solution(14883065496042781293)
XLA Ops:
  1.3 4.8 %stats.1 = (f32[48,768]{1,0:T(8,128)}, f32[48,768]{1,0:T(8,128)}) custom-call(s32[1]{0:T(128)} %bitcast.hand_ref, s32[8]{0:T(128)} %refs_0_.3, s32[4]{0:T(128)} %cards_now_ref.7, s32[2,8,1536]{2,1,0:T(8,128)} %constant.12.clone.refs_2_.card_ref, s32[12,663]{1,0:T(8,128)} %refs_5_.3, f32[12,64,663]{2,1,0:T(8,128)} %x_ref.3, f32[12,16,663]{2,1,0:T(8,128)} %v_ref.3, ...), custom_call_target="tpu_custom_call" | custom-call | flops 5000000000 | tf_op jit(solution)/shard_map/stats/pallas_call | solution.py:571
  6.2 3.0 %collective-permute-start = (f32[48,768]{1,0:T(8,128)}, f32[48,768]{1,0:T(8,128)S(1)}, u32[]{:S(2)}, u32[]{:S(2)}) collective-permute-start(f32[48,768]{1,0:T(8,128)} %get-tuple-element.92), channel_id=1, source_target_pairs={{0,2},{2,0},{4,6},{6,4},{8,10},{10,8},{12,14},{14,12},{1,3},{3,1},... | collective-permute-start | bytes 442376 | tf_op jit(solution)/shard_map/ppermute | solution.py:553
  9.3 1.6 %prepare.1 = (f32[12,1,1536]{2,1,0:T(1,128)S(1)}, bf16[12,1,768]{2,1,0:T(2,128)(2,1)S(1)}, f32[4,1536,3]{2,1,0:T(8,128)S(1)}, bf16[2,1536,768]{2,1,0:T(8,128)(2,...) custom-call(s32[1]{0:T(128)} %bitcast.hand_ref, ...), custom_call_target="tpu_custom_call" | custom-call | flops 2000000000 | tf_op jit(solution)/shard_map/prepare/pallas_call | solution.py:571
  11.1 2.3 %mover_gradient.8 = (f32[3,64,768]{2,1,0:T(8,128)S(1)}, f32[3,16,768]{2,1,0:T(8,128)S(1)}) custom-call(f32[12,64,663]{2,1,0:T(8,128)S(1)} %copy-done, f32[12,64,663]{2,1,0:T(8,128)S(1)} %collective-permute-done.1.far_ref, f32[12,16,663]{2,1,0:T(8,128)S(1)} %copy-done.1, f32[12,1,1536]{2,1,0:T(1,128)S(1)} %get-tuple-element.93.live_ref, ...), custom_call_target="tpu_custom_call" | custom-call | flops 3000000000 | tf_op jit(solution)/shard_map/mover_gradient/pallas_call | solution.py:571
  13.5 1.9 %collective-permute-start.4 = (f32[48,768]{1,0:T(8,128)S(1)}, f32[48,768]{1,0:T(8,128)S(1)}, u32[]{:S(2)}, u32[]{:S(2)}) collective-permute-start(f32[48,768]{1,0:T(8,128)S(1)} %add.18), channel_id=1, source_target_pairs={{0,4},{2,6},{4,0},{6,2},{8,12},{10,14},{12,8},{14,10},{1,5},{3,7},... | collective-permute-start | bytes 442376 | tf_op jit(solution)/shard_map/ppermute | solution.py:553
  15.3 2.3 %mover_gradient.9 = (f32[3,64,768]{2,1,0:T(8,128)S(1)}, f32[3,16,768]{2,1,0:T(8,128)S(1)}) custom-call(f32[12,64,663]{2,1,0:T(8,128)S(1)} %copy-done, f32[12,64,663]{2,1,0:T(8,128)S(1)} %collective-permute-done.1.far_ref, f32[12,16,663]{2,1,0:T(8,128)S(1)} %copy-done.1, f32[12,1,1536]{2,1,0:T(1,128)S(1)} %get-tuple-element.93.live_ref, ...), custom_call_target="tpu_custom_call" | custom-call | flops 3000000000 | tf_op jit(solution)/shard_map/mover_gradient/pallas_call | solution.py:571
  17.7 2.0 %collective-permute-done.4 = f32[48,768]{1,0:T(8,128)S(1)} collective-permute-done((f32[48,768]{1,0:T(8,128)S(1)}, f32[48,768]{1,0:T(8,128)S(1)}, u32[]{:S(2)}, u32[]{:S(2)}) %collective-permute-start.4) | collective-permute-done | bytes 147488 | tf_op jit(solution)/shard_map/ppermute | solution.py:553
  19.7 2.7 %collective-permute-start.5 = (f32[48,768]{1,0:T(8,128)S(1)}, f32[48,768]{1,0:T(8,128)S(1)}, u32[]{:S(2)}, u32[]{:S(2)}) collective-permute-start(f32[48,768]{1,0:T(8,128)S(1)} %add.19), channel_id=1, source_target_pairs={{0,8},{2,10},{4,12},{6,14},{8,0},{10,2},{12,4},{14,6},{1,9},{3,11}... | collective-permute-start | bytes 442376 | tf_op jit(solution)/shard_map/ppermute | solution.py:553
  22.4 2.3 %mover_gradient.11 = (f32[3,64,768]{2,1,0:T(8,128)S(1)}, f32[3,16,768]{2,1,0:T(8,128)S(1)}) custom-call(f32[12,64,663]{2,1,0:T(8,128)S(1)} %copy-done, f32[12,64,663]{2,1,0:T(8,128)S(1)} %collective-permute-done.1.far_ref, f32[12,16,663]{2,1,0:T(8,128)S(1)} %copy-done.1, f32[12,1,1536]{2,1,0:T(1,128)S(1)} %get-tuple-element.93.live_ref, ...), custom_call_target="tpu_custom_call" | custom-call | flops 3000000000 | tf_op jit(solution)/shard_map/mover_gradient/pallas_call | solution.py:571
  24.7 2.3 %mover_gradient.10 = (f32[3,64,768]{2,1,0:T(8,128)S(1)}, f32[3,16,768]{2,1,0:T(8,128)S(1)}) custom-call(f32[12,64,663]{2,1,0:T(8,128)S(1)} %copy-done, f32[12,64,663]{2,1,0:T(8,128)S(1)} %collective-permute-done.1.far_ref, f32[12,16,663]{2,1,0:T(8,128)S(1)} %copy-done.1, f32[12,1,1536]{2,1,0:T(1,128)S(1)} %get-tuple-element.93.live_ref, ...), custom_call_target="tpu_custom_call" | custom-call | flops 3000000000 | tf_op jit(solution)/shard_map/mover_gradient/pallas_call | solution.py:571
  32.8 1.5 %turn_step.2 = (f32[48,1536]{1,0:T(8,128)S(1)}, f32[32,1536]{1,0:T(8,128)S(1)}, f32[16,1536]{1,0:T(8,128)S(1)}, f32[8,768]{1,0:T(8,128)S(1)}, f32[8,128]{1,0:T(8,128)S(1)}) custom-call(s32[1]{0:T(128)} %bitcast.hand_ref, s32[4]{0:T(128)S(1)} %copy-done.14, s32[2,8,1536]{2,1,0:T(8,128)S(1)} %copy-done.19, bf16[2,1536,128]{2,1,0:T(8,128)(2,1)S(1)} %copy-done.16, ...), custom_call_target="tpu_custom_call" | custom-call | flops 2000000000 | tf_op jit(solution)/shard_map/turn_step/pallas_call | solution.py:571
  34.3 5.4 %rival_step.4 = (f32[6,64,768]{2,1,0:T(8,128)S(1)}, f32[6,16,768]{2,1,0:T(8,128)S(1)}, f32[32,768]{1,0:T(8,128)S(1)}) custom-call(f32[48,768]{1,0:T(8,128)S(1)} %add.20.rest_4_.own_norm_ref, f32[48,768]{1,0:T(8,128)S(1)} %collective-permute-done.6.rest_5_.far_norm_ref, f32[6,64,768]{2,1,0:T(8,128)S(1)} %get-tuple-element.126.bar_ref, ...), custom_call_target="tpu_custom_call" | custom-call | flops 6000000000 | tf_op jit(solution)/shard_map/rival_step/pallas_call | solution.py:571
  39.9 5.2 %rival_step.5 = (f32[6,64,768]{2,1,0:T(8,128)S(1)}, f32[6,16,768]{2,1,0:T(8,128)S(1)}, f32[32,768]{1,0:T(8,128)S(1)}) custom-call(f32[48,768]{1,0:T(8,128)S(1)} %add.20.rest_4_.own_norm_ref, f32[48,768]{1,0:T(8,128)S(1)} %collective-permute-done.6.rest_5_.far_norm_ref, f32[6,64,768]{2,1,0:T(8,128)S(1)} %get-tuple-element.123.bar_ref, ...), custom_call_target="tpu_custom_call" | custom-call | flops 6000000000 | tf_op jit(solution)/shard_map/rival_step/pallas_call | solution.py:571
  46.7 2.4 %mover_gradient.12 = (f32[3,64,768]{2,1,0:T(8,128)S(1)}, f32[3,16,768]{2,1,0:T(8,128)S(1)}) custom-call(f32[6,64,768]{2,1,0:T(8,128)S(1)} %get-tuple-element.139.y_ref, f32[6,64,768]{2,1,0:T(8,128)S(1)} %collective-permute-done.10.far_ref, f32[6,16,768]{2,1,0:T(8,128)S(1)} %get-tuple-element.140.u_ref, f32[12,1,1536]{2,1,0:T(1,128)S(1)} %get-tuple-element.93.live_ref, ...), custom_call_target="tpu_custom_call" | custom-call | flops 3000000000 | tf_op jit(solution)/shard_map/mover_gradient/pallas_call | solution.py:571
  51.1 2.3 %mover_gradient.13 = (f32[3,64,768]{2,1,0:T(8,128)S(1)}, f32[3,16,768]{2,1,0:T(8,128)S(1)}) custom-call(f32[6,64,768]{2,1,0:T(8,128)S(1)} %get-tuple-element.139.y_ref, f32[6,64,768]{2,1,0:T(8,128)S(1)} %collective-permute-done.10.far_ref, f32[6,16,768]{2,1,0:T(8,128)S(1)} %get-tuple-element.140.u_ref, f32[12,1,1536]{2,1,0:T(1,128)S(1)} %get-tuple-element.93.live_ref, ...), custom_call_target="tpu_custom_call" | custom-call | flops 3000000000 | tf_op jit(solution)/shard_map/mover_gradient/pallas_call | solution.py:571
  53.4 1.6 %collective-permute-done.11 = f32[32,768]{1,0:T(8,128)S(1)} collective-permute-done((f32[32,768]{1,0:T(8,128)S(1)}, f32[32,768]{1,0:T(8,128)S(1)}, u32[]{:S(2)}, u32[]{:S(2)}) %collective-permute-start.11) | collective-permute-done | bytes 98336 | tf_op jit(solution)/shard_map/ppermute | solution.py:553
  55.1 1.9 %collective-permute-start.12 = (f32[32,768]{1,0:T(8,128)S(1)}, f32[32,768]{1,0:T(8,128)S(1)}, u32[]{:S(2)}, u32[]{:S(2)}) collective-permute-start(f32[32,768]{1,0:T(8,128)S(1)} %add.22), channel_id=1, source_target_pairs={{0,8},{2,10},{4,12},{6,14},{8,0},{10,2},{12,4},{14,6},{1,9},{3,11}... | collective-permute-start | bytes 294920 | tf_op jit(solution)/shard_map/ppermute | solution.py:553
  56.9 2.3 %mover_gradient.15 = (f32[3,64,768]{2,1,0:T(8,128)S(1)}, f32[3,16,768]{2,1,0:T(8,128)S(1)}) custom-call(f32[6,64,768]{2,1,0:T(8,128)S(1)} %get-tuple-element.147.y_ref, f32[6,64,768]{2,1,0:T(8,128)S(1)} %collective-permute-done.13.far_ref, f32[6,16,768]{2,1,0:T(8,128)S(1)} %get-tuple-element.148.u_ref, f32[12,1,1536]{2,1,0:T(1,128)S(1)} %get-tuple-element.93.live_ref, ...), custom_call_target="tpu_custom_call" | custom-call | flops 3000000000 | tf_op jit(solution)/shard_map/mover_gradient/pallas_call | solution.py:571
  59.3 2.3 %mover_gradient.14 = (f32[3,64,768]{2,1,0:T(8,128)S(1)}, f32[3,16,768]{2,1,0:T(8,128)S(1)}) custom-call(f32[6,64,768]{2,1,0:T(8,128)S(1)} %get-tuple-element.147.y_ref, f32[6,64,768]{2,1,0:T(8,128)S(1)} %collective-permute-done.13.far_ref, f32[6,16,768]{2,1,0:T(8,128)S(1)} %get-tuple-element.148.u_ref, f32[12,1,1536]{2,1,0:T(1,128)S(1)} %get-tuple-element.93.live_ref, ...), custom_call_target="tpu_custom_call" | custom-call | flops 3000000000 | tf_op jit(solution)/shard_map/mover_gradient/pallas_call | solution.py:571
  63.1 1.5 %mover_step.6 = (f32[12,64,663]{2,1,0:T(8,128)}, f32[12,16,663]{2,1,0:T(8,128)}, f32[6,64,768]{2,1,0:T(8,128)S(1)}) custom-call(f32[32,768]{1,0:T(8,128)S(1)} %add.23.rest_7_.own_norm_ref, f32[32,768]{1,0:T(8,128)S(1)} %collective-permute-done.14.rest_8_.far_norm_ref, f32[6,64,768]{2,1,0:T(8,128)S(1)} %get-tuple-element.157.x_ref, ...), custom_call_target="tpu_custom_call" | custom-call | flops 2000000000 | tf_op jit(solution)/shard_map/mover_step/pallas_call | solution.py:571
  64.8 1.5 %mover_step.7 = (f32[12,64,663]{2,1,0:T(8,128)}, f32[12,16,663]{2,1,0:T(8,128)}, f32[6,64,768]{2,1,0:T(8,128)S(1)}) custom-call(f32[32,768]{1,0:T(8,128)S(1)} %add.23.rest_7_.own_norm_ref, f32[32,768]{1,0:T(8,128)S(1)} %collective-permute-done.14.rest_8_.far_norm_ref, ...), custom_call_target="tpu_custom_call", output_to_operand_aliasing={{0}: (9, {}), {1}: (10, {})} | custom-call | flops 2000000000 | tf_op jit(solution)/shard_map/mover_step/pallas_call | solution.py:571
  66.7 2.0 %turn_step.3 = (f32[16,1536]{1,0:T(8,128)S(1)}, f32[16,663]{1,0:T(8,128)}, f32[6,663]{1,0:T(8,128)}, f32[16,663]{1,0:T(8,128)}, f32[6,663]{1,0:T(8,128)}) custom-call(s32[1]{0:T(128)} %bitcast.hand_ref, s32[4]{0:T(128)S(1)} %copy-done.14, s32[2,8,1536]{2,1,0:T(8,128)S(1)} %copy-done.19, bf16[2,1536,128]{2,1,0:T(8,128)(2,1)S(1)} %copy-done.16, ...), custom_call_target="tpu_custom_call" | custom-call | flops 2000000000 | tf_op jit(solution)/shard_map/turn_step/pallas_call | solution.py:571
  68.7 5.7 %rival_step.6 = (f32[12,64,663]{2,1,0:T(8,128)}, f32[12,16,663]{2,1,0:T(8,128)}) custom-call(f32[32,768]{1,0:T(8,128)S(1)} %add.23.rest_7_.own_norm_ref, f32[32,768]{1,0:T(8,128)S(1)} %collective-permute-done.14.rest_8_.far_norm_ref, f32[6,64,768]{2,1,0:T(8,128)S(1)} %get-tuple-element.168.bar_ref, f32[6,64,768]{2,1,0:T(8,128)S(1)} %collective-permute-done.16.far_ref, ...), custom_call_target="tpu_custom_call" | custom-call | flops 6000000000 | tf_op jit(solution)/shard_map/rival_step/pallas_call | solution.py:571
  74.4 5.7 %rival_step.7 = (f32[12,64,663]{2,1,0:T(8,128)}, f32[12,16,663]{2,1,0:T(8,128)}) custom-call(f32[32,768]{1,0:T(8,128)S(1)} %add.23.rest_7_.own_norm_ref, f32[32,768]{1,0:T(8,128)S(1)} %collective-permute-done.14.rest_8_.far_norm_ref, f32[6,64,768]{2,1,0:T(8,128)S(1)} %get-tuple-element.166.bar_ref, ...), custom_call_target="tpu_custom_call", output_to_operand_aliasing={{0}: (20, {}), {1}: (21, {})} | custom-call | flops 6000000000 | tf_op jit(solution)/shard_map/rival_step/pallas_call | solution.py:571
  (80 shorter events, 12.3 us)
Async XLA Ops:
  0.6 10.3 %collective-permute-start.1 = (f32[12,64,663]{2,1,0:T(8,128)}, f32[12,64,663]{2,1,0:T(8,128)S(1)}, u32[]{:S(2)}, u32[]{:S(2)}) collective-permute-start(f32[12,64,663]{2,1,0:T(8,128)} %y_ref.11), channel_id=1, source_target_pairs={{0,1},{1,0},{2,3},{3,2},{4,5},{5,4},{6,7},{7,6},{8,9},{9,8},{10,11... | collective-permute-start | bytes 6110216 | tf_op jit(solution)/shard_map/ppermute | solution.py:550
  1.2 8.0 %collective-permute-start.2 = (s32[12,663]{1,0:T(8,128)}, s32[12,663]{1,0:T(8,128)S(1)}, u32[]{:S(2)}, u32[]{:S(2)}) collective-permute-start(s32[12,663]{1,0:T(8,128)} %refs_5_.3), channel_id=1, source_target_pairs={{0,1},{1,0},{2,3},{3,2},{4,5},{5,4},{6,7},{7,6},{8,9},{9,8},{10,11... | collective-permute-start | bytes 95480 | tf_op jit(solution)/shard_map/ppermute | solution.py:550
  1.2 7.9 %copy-start.8 = (f32[64,64]{1,0:T(8,128)S(1)}, f32[64,64]{1,0:T(8,128)}, u32[]{:S(2)}) copy-start(f32[64,64]{1,0:T(8,128)} %refs_9_.3) | copy-start | bytes 49156
  1.2 8.0 %copy-start.10 = (s32[16,64]{1,0:T(8,128)S(1)}, s32[16,64]{1,0:T(8,128)}, u32[]{:S(2)}) copy-start(s32[16,64]{1,0:T(8,128)} %children_ref.7) | copy-start | bytes 12292
  1.3 8.0 %copy-start.13 = (s32[8]{0:T(128)S(1)}, s32[8]{0:T(128)}, u32[]{:S(2)}) copy-start(s32[8]{0:T(128)} %refs_0_.3) | copy-start | bytes 100
  1.3 8.0 %copy-start.14 = (s32[4]{0:T(128)S(1)}, s32[4]{0:T(128)}, u32[]{:S(2)}) copy-start(s32[4]{0:T(128)} %cards_now_ref.7) | copy-start | bytes 52
  1.3 8.0 %copy-start.15 = (bf16[2,128,1536]{2,1,0:T(8,128)(2,1)S(1)}, bf16[2,128,1536]{2,1,0:T(8,128)(2,1)}, u32[]{:S(2)}) copy-start(bf16[2,128,1536]{2,1,0:T(8,128)(2,1)} %constant.14.clone.refs_4_.spread_ref) | copy-start | bytes 2359300
  1.3 7.9 %copy-start.16 = (bf16[2,1536,128]{2,1,0:T(8,128)(2,1)S(1)}, bf16[2,1536,128]{2,1,0:T(8,128)(2,1)}, u32[]{:S(2)}) copy-start(bf16[2,1536,128]{2,1,0:T(8,128)(2,1)} %constant.13.clone.refs_3_.gather_ref) | copy-start | bytes 2359300
  1.3 7.9 %copy-start.18 = (bf16[2,128,768]{2,1,0:T(8,128)(2,1)S(1)}, bf16[2,128,768]{2,1,0:T(8,128)(2,1)}, u32[]{:S(2)}) copy-start(bf16[2,128,768]{2,1,0:T(8,128)(2,1)} %constant.15.clone.refs_7_) | copy-start | bytes 1179652
  6.2 7.3 %collective-permute-start = (f32[48,768]{1,0:T(8,128)}, f32[48,768]{1,0:T(8,128)S(1)}, u32[]{:S(2)}, u32[]{:S(2)}) collective-permute-start(f32[48,768]{1,0:T(8,128)} %get-tuple-element.92), channel_id=1, source_target_pairs={{0,2},{2,0},{4,6},{6,4},{8,10},{10,8},{12,14},{14,12},{1,3},{3,1},... | collective-permute-start | bytes 442376 | tf_op jit(solution)/shard_map/ppermute | solution.py:553
  9.1 4.3 %collective-permute-start.3 = (f32[48,768]{1,0:T(8,128)}, f32[48,768]{1,0:T(8,128)S(1)}, u32[]{:S(2)}, u32[]{:S(2)}) collective-permute-start(f32[48,768]{1,0:T(8,128)} %get-tuple-element.107.pack_ref.rest_0_), channel_id=1, source_target_pairs={{0,1},{1,0},{2,3},{3,2},{4,5},{5,4},{6,7},{7,6},{8,9},{9,8},{10,11... | collective-permute-start | bytes 442376 | tf_op jit(solution)/shard_map/ppermute | solution.py:550
  13.5 6.2 %collective-permute-start.4 = (f32[48,768]{1,0:T(8,128)S(1)}, f32[48,768]{1,0:T(8,128)S(1)}, u32[]{:S(2)}, u32[]{:S(2)}) collective-permute-start(f32[48,768]{1,0:T(8,128)S(1)} %add.18), channel_id=1, source_target_pairs={{0,4},{2,6},{4,0},{6,2},{8,12},{10,14},{12,8},{14,10},{1,5},{3,7},... | collective-permute-start | bytes 442376 | tf_op jit(solution)/shard_map/ppermute | solution.py:553
  19.7 9.4 %collective-permute-start.5 = (f32[48,768]{1,0:T(8,128)S(1)}, f32[48,768]{1,0:T(8,128)S(1)}, u32[]{:S(2)}, u32[]{:S(2)}) collective-permute-start(f32[48,768]{1,0:T(8,128)S(1)} %add.19), channel_id=1, source_target_pairs={{0,8},{2,10},{4,12},{6,14},{8,0},{10,2},{12,4},{14,6},{1,9},{3,11}... | collective-permute-start | bytes 442376 | tf_op jit(solution)/shard_map/ppermute | solution.py:553
  29.2 1.4 %collective-permute-start.6 = (f32[48,768]{1,0:T(8,128)S(1)}, f32[48,768]{1,0:T(8,128)S(1)}, u32[]{:S(2)}, u32[]{:S(2)}) collective-permute-start(f32[48,768]{1,0:T(8,128)S(1)} %add.20.rest_4_.own_norm_ref), channel_id=1, source_target_pairs={{0,1},{1,0},{2,3},{3,2},{4,5},{5,4},{6,7},{7,6},{8,9},{9,8},{10,11... | collective-permute-start | bytes 442376 | tf_op jit(solution)/shard_map/ppermute | solution.py:550
  31.4 2.9 %collective-permute-start.8 = (f32[6,64,768]{2,1,0:T(8,128)S(1)}, f32[6,64,768]{2,1,0:T(8,128)S(1)}, u32[]{:S(2)}, u32[]{:S(2)}) collective-permute-start(f32[6,64,768]{2,1,0:T(8,128)S(1)} %get-tuple-element.126.bar_ref), channel_id=1, source_target_pairs={{0,1},{1,0},{2,3},{3,2},{4,5},{5,4},{6,7},{7,6},{8,9},{9,8},{10,11... | collective-permute-start | bytes 3538952 | tf_op jit(solution)/shard_map/ppermute | solution.py:550
  32.3 7.5 %collective-permute-start.7 = (f32[6,64,768]{2,1,0:T(8,128)S(1)}, f32[6,64,768]{2,1,0:T(8,128)S(1)}, u32[]{:S(2)}, u32[]{:S(2)}) collective-permute-start(f32[6,64,768]{2,1,0:T(8,128)S(1)} %get-tuple-element.123.bar_ref), channel_id=1, source_target_pairs={{0,1},{1,0},{2,3},{3,2},{4,5},{5,4},{6,7},{7,6},{8,9},{9,8},{10,11... | collective-permute-start | bytes 3538952 | tf_op jit(solution)/shard_map/ppermute | solution.py:550
  39.7 7.0 %collective-permute-start.10 = (f32[6,64,768]{2,1,0:T(8,128)S(1)}, f32[6,64,768]{2,1,0:T(8,128)S(1)}, u32[]{:S(2)}, u32[]{:S(2)}) collective-permute-start(f32[6,64,768]{2,1,0:T(8,128)S(1)} %get-tuple-element.139.y_ref), channel_id=1, source_target_pairs={{0,1},{1,0},{2,3},{3,2},{4,5},{5,4},{6,7},{7,6},{8,9},{9,8},{10,11... | collective-permute-start | bytes 3538952 | tf_op jit(solution)/shard_map/ppermute | solution.py:550
  45.1 11.8 %collective-permute-start.13 = (f32[6,64,768]{2,1,0:T(8,128)S(1)}, f32[6,64,768]{2,1,0:T(8,128)S(1)}, u32[]{:S(2)}, u32[]{:S(2)}) collective-permute-start(f32[6,64,768]{2,1,0:T(8,128)S(1)} %get-tuple-element.147.y_ref), channel_id=1, source_target_pairs={{0,1},{1,0},{2,3},{3,2},{4,5},{5,4},{6,7},{7,6},{8,9},{9,8},{10,11... | collective-permute-start | bytes 3538952 | tf_op jit(solution)/shard_map/ppermute | solution.py:550
  45.5 4.9 %collective-permute-start.9 = (f32[32,768]{1,0:T(8,128)S(1)}, f32[32,768]{1,0:T(8,128)S(1)}, u32[]{:S(2)}, u32[]{:S(2)}) collective-permute-start(f32[32,768]{1,0:T(8,128)S(1)} %get-tuple-element.131), channel_id=1, source_target_pairs={{0,2},{2,0},{4,6},{6,4},{8,10},{10,8},{12,14},{14,12},{1,3},{3,1},... | collective-permute-start | bytes 294920 | tf_op jit(solution)/shard_map/ppermute | solution.py:553
  50.4 4.7 %collective-permute-start.11 = (f32[32,768]{1,0:T(8,128)S(1)}, f32[32,768]{1,0:T(8,128)S(1)}, u32[]{:S(2)}, u32[]{:S(2)}) collective-permute-start(f32[32,768]{1,0:T(8,128)S(1)} %add.21), channel_id=1, source_target_pairs={{0,4},{2,6},{4,0},{6,2},{8,12},{10,14},{12,8},{14,10},{1,5},{3,7},... | collective-permute-start | bytes 294920 | tf_op jit(solution)/shard_map/ppermute | solution.py:553
  55.1 6.6 %collective-permute-start.12 = (f32[32,768]{1,0:T(8,128)S(1)}, f32[32,768]{1,0:T(8,128)S(1)}, u32[]{:S(2)}, u32[]{:S(2)}) collective-permute-start(f32[32,768]{1,0:T(8,128)S(1)} %add.22), channel_id=1, source_target_pairs={{0,8},{2,10},{4,12},{6,14},{8,0},{10,2},{12,4},{14,6},{1,9},{3,11}... | collective-permute-start | bytes 294920 | tf_op jit(solution)/shard_map/ppermute | solution.py:553
  61.7 1.4 %collective-permute-start.14 = (f32[32,768]{1,0:T(8,128)S(1)}, f32[32,768]{1,0:T(8,128)S(1)}, u32[]{:S(2)}, u32[]{:S(2)}) collective-permute-start(f32[32,768]{1,0:T(8,128)S(1)} %add.23.rest_7_.own_norm_ref), channel_id=1, source_target_pairs={{0,1},{1,0},{2,3},{3,2},{4,5},{5,4},{6,7},{7,6},{8,9},{9,8},{10,11... | collective-permute-start | bytes 294920 | tf_op jit(solution)/shard_map/ppermute | solution.py:550
  64.6 4.0 %collective-permute-start.16 = (f32[6,64,768]{2,1,0:T(8,128)S(1)}, f32[6,64,768]{2,1,0:T(8,128)S(1)}, u32[]{:S(2)}, u32[]{:S(2)}) collective-permute-start(f32[6,64,768]{2,1,0:T(8,128)S(1)} %get-tuple-element.168.bar_ref), channel_id=1, source_target_pairs={{0,1},{1,0},{2,3},{3,2},{4,5},{5,4},{6,7},{7,6},{8,9},{9,8},{10,11... | collective-permute-start | bytes 3538952 | tf_op jit(solution)/shard_map/ppermute | solution.py:550
  66.3 8.1 %collective-permute-start.15 = (f32[6,64,768]{2,1,0:T(8,128)S(1)}, f32[6,64,768]{2,1,0:T(8,128)S(1)}, u32[]{:S(2)}, u32[]{:S(2)}) collective-permute-start(f32[6,64,768]{2,1,0:T(8,128)S(1)} %get-tuple-element.166.bar_ref), channel_id=1, source_target_pairs={{0,1},{1,0},{2,3},{3,2},{4,5},{5,4},{6,7},{7,6},{8,9},{9,8},{10,11... | collective-permute-start | bytes 3538952 | tf_op jit(solution)/shard_map/ppermute | solution.py:550
  (14 other events, 55.6 us)
